TPU v7x, 256 devices: a whole 4x4x8 slice. The times are simulated.
256 devices in a mesh: leaf: 4 (over y), row: 16 (over x_lo, z), col: 4 (over x_hi, core).
Axes of the slice: x: 4 (x_hi: 2, x_lo: 2; x = x_hi * 2 + x_lo), y: 4, z: 8, core: 2. Of those that a mesh axis runs over, the one named last changes fastest.
Arguments:
- ancestor_cols: bfloat16 [16, 4, 512, 32768], P(None, 'col', 'leaf', 'row'), may hold values from -6 to 6
- factor: bfloat16 [4, 32768, 256], P('leaf', ('row', 'col')), may hold values from -0.046875 to 0.046875
- block_mask: int32 [4, 128], P('leaf'), may hold values 0 or 1
- diag_inverse: float32 [4, 256, 256], P('leaf'), may hold values from -6 to 6
Outputs:
- inverse_cols: bfloat16 [4, 32768, 256], P('leaf', ('row', 'col'))
- diag_block: float32 [4, 256, 256], P('leaf')
All inputs are finite; a program needn't handle non-finite values. No bound on the sum of `block_mask` on one device may be relied on, other than what follows from the above.
Results may differ from a plain program's by a relative error of at most 0.0021.
Values may be sent and summed in bfloat16 or wider, within the bound.
No kernel may reach another device: no remote copies, remote signals or barrier semaphores. Data moves between devices by JAX's collectives and lax.ppermute only.
A program may use at most 128 MiB of HBM per device.

v0:
```python
import jax
import jax.numpy as jnp
from jax import lax
from jax.sharding import PartitionSpec as P


def shards(ancestor_cols, factor, block_mask, diag_inverse):
    num_rows = lax.axis_size("row")
    num_cols = lax.axis_size("col")
    kount, sub_rows, width = factor.shape
    per_group = sub_rows // width
    group_index = lax.axis_index("row") * num_cols + lax.axis_index("col")
    live = lax.dynamic_slice_in_dim(block_mask, group_index * per_group, per_group, 1)
    masked = factor.reshape(kount, per_group, width, width) * live[:, :, None, None].astype(
        factor.dtype
    )
    masked = masked.reshape(kount, sub_rows, width)
    column_rows = lax.all_gather(masked, "row", axis=1, tiled=True)
    grouped = column_rows.reshape(kount, num_rows, sub_rows, width)
    partial_value = jnp.einsum(
        "qti,kqtw->kiw",
        lax.all_gather(ancestor_cols, "leaf", axis=2, tiled=True)[:, 0],
        grouped,
        preferred_element_type=jnp.float32,
    )
    summed = lax.psum_scatter(partial_value, "col", scatter_dimension=1, tiled=True)
    inverse_cols = (-summed).astype(jnp.bfloat16)
    products = jnp.einsum("kjw,kjv->kwv", masked, inverse_cols, preferred_element_type=jnp.float32)
    total = lax.psum(products, ("row", "col"))
    return (inverse_cols, diag_inverse - total)


def solution(mesh):
    in_specs = (
        P(None, "col", "leaf", "row"),
        P("leaf", ("row", "col"), None),
        P("leaf", None),
        P("leaf", None, None),
    )
    out_specs = (P("leaf", ("row", "col"), None), P("leaf", None, None))
    return jax.shard_map(shards, mesh=mesh, in_specs=in_specs, out_specs=out_specs, check_vma=False)
```

profile of v0, /device:TPU:1, one launch (start us, length us, event | category | flops | bytes accessed | tf_op | source)
XLA Modules:
  0.0 636.1 jit_solution(12212282874622116274)
XLA Ops:
  7.2 0.0 all-gather.3.cloned.1.call-start
  7.2 0.7 convert_bitcast_fusion
  7.9 0.1 broadcast_bitcast_fusion
  8.0 1.8 broadcast_multiply_fusion
  9.8 0.0 all-gather.3.cloned.1.call-update
  9.8 0.0 all-gather.5.cloned.1.call-start
  9.9 0.7 all-gather.5.cloned.1.call-update
  10.6 0.0 reduce-scatter.2.cloned.1.call-start
  10.6 71.6 %all-gather.3.cloned.1.call-done = bf16[1,8192,256]{2,1,0:T(8,128)(2,1)} async-done(((bf16[1,512,256]{2,1,0:T(8,128)(2,1)}), bf16[1,8192,256]{2,1,0:T(8,128)(2,1)}) %all-gather.3.cloned.1.call-update) | async-done | bytes 4194320 | tf_op jit(solution)/shard_map/all_gather | solution.py:18
  82.2 304.5 %all-gather.5.cloned.1.call-done = bf16[16,1,512,2048]{3,2,0,1:T(8,128)(2,1)} async-done(((bf16[16,1,128,2048]{3,2,0,1:T(8,128)(2,1)}), bf16[16,1,512,2048]{3,2,0,1:T(8,128)(2,1)}) %all-gather.5.cloned.1.call-update) | async-done | bytes 33554448 | tf_op jit(solution)/shard_map/all_gather | solution.py:22
  386.7 0.0 copy-start
  386.7 17.3 %fusion.2 = f32[1,2048,256]{1,2,0:T(8,128)} fusion(bf16[16,512,256]{2,1,0:T(8,128)(2,1)} %bitcast.27, bf16[16,1,512,2048]{3,2,0,1:T(8,128)(2,1)} %all-gather.5.cloned.1.call-done), kind=kOutput, calls=%fused_computation.2 | convolution fusion | flops 8589934592 | bytes 39845888 | tf_op jit(solution)/shard_map/qti,kqtw->kiw/dot_general | solution.py:20
  404.1 0.0 copy-start.1
  404.1 0.0 reduce-scatter.2.cloned.1.call-update
  404.1 0.0 all-reduce.2.cloned.1.call-start
  404.2 44.6 %reduce-scatter.2.cloned.1.call-done = f32[1,512,256]{1,2,0:T(8,128)} async-done(((f32[1,2048,256]{1,2,0:T(8,128)}), f32[1,512,256]{1,2,0:T(8,128)}) %reduce-scatter.2.cloned.1.call-update) | async-done | bytes 524304 | tf_op jit(solution)/shard_map/reduce_scatter | solution.py:26
  448.8 1.1 negate_convert_fusion
  449.8 0.0 copy-done
  449.8 1.0 convolution_bitcast_fusion
  450.8 0.0 all-reduce.2.cloned.1.call-update
  450.8 0.8 copy.10
  451.7 176.2 %all-reduce.2.cloned.1.call-done = f32[1,256,256]{2,1,0:T(8,128)} async-done(((f32[1,256,256]{2,1,0:T(8,128)}), f32[1,256,256]{2,1,0:T(8,128)}) %all-reduce.2.cloned.1.call-update) | async-done | bytes 262160 | tf_op jit(solution)/shard_map/psum | solution.py:29
  627.8 0.0 copy-done.1
  627.8 1.7 sub.3
  (1 shorter events, 0.0 us)
Async XLA Ops:
  7.2 75.1 %all-gather.3.cloned.1.call-start = ((), (), s32[]{:S(2)}) async-start(), calls=%async_computation.1 | async-start | bytes 4456448 | tf_op jit(solution)/shard_map/all_gather | solution.py:18
  9.8 376.9 %all-gather.5.cloned.1.call-start = ((), (), s32[]{:S(2)}) async-start(), calls=%async_computation.2 | async-start | bytes 41943040 | tf_op jit(solution)/shard_map/all_gather | solution.py:22
  10.6 438.2 %reduce-scatter.2.cloned.1.call-start = ((), (), s32[]{:S(2)}) async-start(), calls=%async_computation.3 | async-start | bytes 2621440 | tf_op jit(solution)/shard_map/reduce_scatter | solution.py:26
  386.7 63.1 %copy-start = (bf16[1,512,256]{2,1,0:T(8,128)(2,1)S(1)}, bf16[1,512,256]{2,1,0:T(8,128)(2,1)}, u32[]{:S(2)}) copy-start(bf16[1,512,256]{2,1,0:T(8,128)(2,1)} %broadcast_multiply_fusion) | copy-start | bytes 786436
  404.1 223.8 %copy-start.1 = (f32[1,256,256]{2,1,0:T(8,128)S(1)}, f32[1,256,256]{2,1,0:T(8,128)}, u32[]{:S(2)}) copy-start(f32[1,256,256]{2,1,0:T(8,128)} %param.7) | copy-start | bytes 786436
  404.1 223.7 %all-reduce.2.cloned.1.call-start = ((), (), s32[]{:S(2)}) async-start(), calls=%async_computation.4 | async-start | bytes 524288 | tf_op jit(solution)/shard_map/psum | solution.py:29
Sparse Core Ops, SparseCore 0:
  10.4 71.8 all-gather.2
  84.0 302.6 all-gather.4
  404.2 44.4 reduce-scatter.1
  453.1 174.7 all-reduce.1
where the time goes:
time: 636 us
  waiting for transfers between devices  598 us (94%)
  matrix products  18.3 us (3%)
  between operations  13.8 us (2%)
    all_gather x1, waiting for transfers between devices, shards(): lax.all_gather(ancestor_cols, 'leaf', axis=2, tiled=True)[:, 0]  305 us
    psum x1, waiting for transfers between devices, shards(): total = lax.psum(products, ('row', 'col'))  176 us
    all_gather x1, waiting for transfers between devices, shards(): column_rows = lax.all_gather(masked, 'row', axis=1, tiled=True)  71.6 us
    reduce_scatter x1, waiting for transfers between devices, shards(): lax.psum_scatter(partial_value, 'col', scatter_dimension=1, tiled=True)  44.6 us
    dot_general x1, matrix products, shards(): jnp.einsum('qti,kqtw->kiw', lax.all_gather(ancestor_cols, 'leaf', axis=2,...  17.3 us
  transfers between devices with their start and end apart: 4, of which 4 were waited for; matrix products, arithmetic and copies ran while one was open for 0% of the time, Pallas kernels for 0%

commit v1 on v0

v1 whole, which is shorter than its diff:
```python
import jax
import jax.numpy as jnp
from jax import lax
from jax.sharding import Mesh, PartitionSpec as P

AXES = ("y", "xlo", "z", "xhi", "core")
ROW = ("xlo", "z")
COL = ("xhi", "core")
ALONG_X = ("xlo", "xhi", "core")
F32 = jnp.float32
BF16 = jnp.bfloat16


def ring_pairs(num):
    return [(2 * z + c, 2 * ((z + (1 if c == 0 else -1)) % num) + c) for z in range(num) for c in range(2)]


SWAP = [(0, 1), (1, 0)]


def shards(ancestor_cols, factor, block_mask, diag_inverse):
    num_z = lax.axis_size("z")
    num_y = lax.axis_size("y")
    quarter = ancestor_cols.shape[2]
    height = ancestor_cols.shape[3]
    width = factor.shape[2]
    sub = factor.shape[1]
    z = lax.axis_index("z")
    core = lax.axis_index("core")
    group = (lax.axis_index("xlo") * num_z + z) * 4 + lax.axis_index("xhi") * 2 + core
    per = sub // width
    live = lax.dynamic_slice_in_dim(block_mask[0], group * per, per, 0)
    masked = (factor.reshape(per, width, width) * live[:, None, None].astype(BF16)).reshape(sub, width)

    pieces = jnp.broadcast_to(masked.reshape(num_y, 1, quarter, width), (num_y, 2, quarter, width))
    own = lax.all_to_all(pieces.reshape(num_y * 2, quarter, width), ("y", "xlo"), 0, 0)
    other = lax.ppermute(own, "core", SWAP)
    blocks = ancestor_cols.reshape(2, num_z, quarter, height)
    step = jnp.where(core == 0, 1, -1)

    def term(rows, where):
        cols = lax.dynamic_index_in_dim(blocks, jnp.remainder(where, num_z), 1, keepdims=False)
        return jnp.einsum(
            "xti,kxtw->kiw", cols, rows.reshape(num_y, 2, quarter, width), preferred_element_type=F32
        )

    partial = term(own, z)
    both = jnp.concatenate([own[None], other[None]], 0)
    pairs = ring_pairs(num_z)
    for hop in range(1, num_z // 2):
        both = lax.ppermute(both, ("z", "core"), pairs)
        swapped = lax.ppermute(both[1], "core", SWAP)
        partial = partial + term(both[0], z - step * hop) + term(swapped, z + step * hop)
    last = lax.ppermute(both[0], ("z", "core"), pairs)
    partial = partial + term(last, z + num_z // 2)

    halves = partial.reshape(num_y, 2, 2, sub, width)
    keep = lax.dynamic_index_in_dim(halves, core, 2, keepdims=False)
    give = lax.dynamic_index_in_dim(halves, 1 - core, 2, keepdims=False)
    summed = keep + lax.ppermute(give, "core", SWAP)
    parts = lax.all_to_all(summed.reshape(num_y * 2, sub, width), ("y", "xhi"), 0, 0)
    inverse_cols = (-jnp.sum(parts, 0)).astype(BF16)

    product = jnp.einsum("jw,jv->wv", masked, inverse_cols, preferred_element_type=F32)
    split = product.reshape(8, width // 8, width)
    mine = jnp.sum(lax.all_to_all(split, ALONG_X, 0, 0), 0)
    over_z = jnp.sum(lax.all_to_all(jnp.broadcast_to(mine, (num_z,) + mine.shape), "z", 0, 0), 0)
    total = lax.all_to_all(jnp.broadcast_to(over_z, (8,) + over_z.shape), ALONG_X, 0, 0)
    return inverse_cols[None], diag_inverse - total.reshape(1, width, width)


def solution(mesh):
    fine = Mesh(mesh.devices.reshape(4, 2, 8, 2, 2), AXES)
    rows = ROW + COL
    in_specs = (P(None, COL, "y", ROW), P("y", rows, None), P("y", None), P("y", None, None))
    out_specs = (P("y", rows, None), P("y", None, None))
    return jax.shard_map(shards, mesh=fine, in_specs=in_specs, out_specs=out_specs, check_vma=False)
```

time: 636 us -> 266 us (0.42)
  waiting for transfers between devices: 598 us -> 76.6 us
  local copies, waits for them, and re-layouts: 0.93 us -> 47.5 us
  blocking collectives: 0 us -> 40.2 us
  matrix products: 18.3 us -> 57.3 us
  starting transfers between devices: 0.16 us -> 30.1 us
  between operations: 13.8 us -> 0.79 us
  other arithmetic: 5.28 us -> 11.9 us
    all_gather x2 -> x0, waiting for transfers between devices: 376 us -> none  [the longest x1 305 us: shards(): lax.all_gather(ancestor_cols, 'leaf', axis=2, tiled=True)[:, 0]]
    psum x1 -> x0, waiting for transfers between devices: 176 us -> none  [shards(): total = lax.psum(products, ('row', 'col'))]
    all_to_all x0 -> x2, waiting for transfers between devices: none -> 56.4 us  [the longest x1 50.8 us: shards(): lax.all_to_all(summed.reshape(num_y * 2, sub, width), ('y', 'xhi'), 0, 0)]
    reduce_scatter x1 -> x0, waiting for transfers between devices: 44.6 us -> none  [shards(): lax.psum_scatter(partial_value, 'col', scatter_dimension=1, tiled=True)]
    all_to_all x0 -> x3, blocking collectives: none -> 40.2 us  [the longest x1 15.6 us: shards(): lax.all_to_all(jnp.broadcast_to(mine, (num_z,) + mine.shape), 'z', 0, 0)]
    dot_general x2 -> x9, matrix products: 18.3 us -> 57.3 us  [the longest x8 57.1 us: term(): jnp.einsum('xti,kxtw->kiw', cols, rows.reshape(num_y, 2, quarter, width),...]
    dynamic_slice x0 -> x3, local copies, waits for them, and re-layouts: none -> 34 us  [the longest x2 23 us: shards(): keep = lax.dynamic_index_in_dim(halves, core, 2, keepdims=False)]
    ppermute x0 -> x9, waiting for transfers between devices: none -> 20.2 us  [the longest x3 18.7 us: shards(): both = lax.ppermute(both, ('z', 'core'), pairs)]
  transfers between devices with their start and end apart: 4 -> 11, of which waited for: 4 -> 6; matrix products, arithmetic and copies ran while one was open for 0% -> 16% of each run, Pallas kernels for 0% -> 0%
where the time goes in v1:
time: 266 us; the launch traced here: 264 us
  waiting for transfers between devices  76.6 us (29%)
  matrix products  57.3 us (22%)
  local copies, waits for them, and re-layouts  47.5 us (18%)
  blocking collectives  40.2 us (15%)
  starting transfers between devices  30.1 us (11%)
  other arithmetic  11.9 us (4%)
    dot_general x8, matrix products, term(): jnp.einsum('xti,kxtw->kiw', cols, rows.reshape(num_y, 2, quarter, width),...  57.1 us
    all_to_all x1, waiting for transfers between devices, shards(): lax.all_to_all(summed.reshape(num_y * 2, sub, width), ('y', 'xhi'), 0, 0)  50.8 us
    dynamic_slice x2, local copies, waits for them, and re-layouts, shards(): keep = lax.dynamic_index_in_dim(halves, core, 2, keepdims=False)  23 us
    ppermute x3, waiting for transfers between devices, shards(): both = lax.ppermute(both, ('z', 'core'), pairs)  18.7 us
    all_to_all x1, blocking collectives, shards(): lax.all_to_all(jnp.broadcast_to(mine, (num_z,) + mine.shape), 'z', 0, 0)  15.6 us
    all_to_all x1, blocking collectives, shards(): lax.all_to_all(pieces.reshape(num_y * 2, quarter, width), ('y', 'xlo'), 0...  15 us
    ppermute x3, starting transfers between devices, shards(): both = lax.ppermute(both, ('z', 'core'), pairs)  11.9 us
    reshape x1, local copies, waits for them, and re-layouts, shards(): halves = partial.reshape(num_y, 2, 2, sub, width)  11.8 us
  transfers between devices with their start and end apart: 11, of which 6 were waited for; matrix products, arithmetic and copies ran while one was open for 16% of the time, Pallas kernels for 0%

profile of v1, /device:TPU:1, one launch (start us, length us, event | category | flops | bytes accessed | tf_op | source)
XLA Modules:
  0.0 264.4 jit_solution(7096297693265450898)
XLA Ops:
  1.5 1.0 broadcast_multiply_fusion
  2.8 15.0 %all_to_all.25 = bf16[8,128,256]{1,2,0:T(8,128)(2,1)S(1)} all-to-all(bf16[8,128,256]{1,2,0:T(8,128)(2,1)S(1)} %bitcast.159), channel_id=1, replica_groups=mesh['y'=4,'xlo'=2,'z'=8,'xhi'=2,'core'=2] {'y','xlo'}, dimensions={0} | all-to-all | bytes 1048576 | tf_op jit(solution)/shard_map/all_to_all | solution.py:36
  17.8 1.9 collective-permute-start
  19.7 1.5 collective-permute-done
  21.3 5.7 %collective-permute-start.1 = (bf16[2,8,128,256]{2,3,1,0:T(8,128)(2,1)S(1)}, bf16[2,8,128,256]{2,3,1,0:T(8,128)(2,1)S(1)}, u32[]{:S(2)}, u32[]{:S(2)}) collective-permute-start(bf16[2,8,128,256]{2,3,1,0:T(8,128)(2,1)S(1)} %pad_maximum_fusion), channel_id=1, source_target_pairs={{0,4},{1,29},{4,8},{5,1},{8,12},{9,5},{12,16},{13,9},{16,20},{17,1... | collective-permute-start | bytes 3145736 | tf_op jit(solution)/shard_map/ppermute | solution.py:51
  26.9 11.7 %collective-permute-done.1 = bf16[2,8,128,256]{2,3,1,0:T(8,128)(2,1)S(1)} collective-permute-done((bf16[2,8,128,256]{2,3,1,0:T(8,128)(2,1)S(1)}, bf16[2,8,128,256]{2,3,1,0:T(8,128)(2,1)S(1)}, u32[]{:S(2)}, u32[]{:S(2)}) %collective-permute-start.1) | collective-permute-done | bytes 1048608 | tf_op jit(solution)/shard_map/ppermute | solution.py:51
  38.7 3.1 %collective-permute-start.3 = (bf16[2,8,128,256]{2,3,1,0:T(8,128)(2,1)S(1)}, bf16[2,8,128,256]{2,3,1,0:T(8,128)(2,1)S(1)}, u32[]{:S(2)}, u32[]{:S(2)}) collective-permute-start(bf16[2,8,128,256]{2,3,1,0:T(8,128)(2,1)S(1)} %collective-permute-done.1), channel_id=1, source_target_pairs={{0,4},{1,29},{4,8},{5,1},{8,12},{9,5},{12,16},{13,9},{16,20},{17,1... | collective-permute-start | bytes 3145736 | tf_op jit(solution)/shard_map/ppermute | solution.py:51
  42.0 5.9 %fusion.14 = f32[4,256,2048,1]{2,1,3,0:T(8,128)} fusion(bf16[4,2,128,256]{2,3,1,0:T(8,128)(2,1)S(1)} %bitcast.154, bf16[2,8,128,2048]{3,2,1,0:T(8,128)(2,1)} %bitcast.143, s32[]{:T(128)S(6)} %select_n.76), kind=kOutput, calls=%fused_computation.23 | convolution fusion | flops 1073741824 | bytes 9961476 | tf_op jit(solution)/shard_map/xti,kxtw->kiw/dot_general | solution.py:43
  47.9 5.7 %collective-permute-done.3 = bf16[2,8,128,256]{2,3,1,0:T(8,128)(2,1)S(1)} collective-permute-done((bf16[2,8,128,256]{2,3,1,0:T(8,128)(2,1)S(1)}, bf16[2,8,128,256]{2,3,1,0:T(8,128)(2,1)S(1)}, u32[]{:S(2)}, u32[]{:S(2)}) %collective-permute-start.3) | collective-permute-done | bytes 1048608 | tf_op jit(solution)/shard_map/ppermute | solution.py:51
  53.6 3.1 %collective-permute-start.5 = (bf16[2,8,128,256]{2,3,1,0:T(8,128)(2,1)S(1)}, bf16[2,8,128,256]{2,3,1,0:T(8,128)(2,1)S(1)}, u32[]{:S(2)}, u32[]{:S(2)}) collective-permute-start(bf16[2,8,128,256]{2,3,1,0:T(8,128)(2,1)S(1)} %collective-permute-done.3), channel_id=1, source_target_pairs={{0,4},{1,29},{4,8},{5,1},{8,12},{9,5},{12,16},{13,9},{16,20},{17,1... | collective-permute-start | bytes 3145736 | tf_op jit(solution)/shard_map/ppermute | solution.py:51
  56.7 5.8 %fusion.12 = f32[4,256,2048,1]{2,1,3,0:T(8,128)} fusion(bf16[4,2,128,256]{2,3,1,0:T(8,128)(2,1)S(1)} %bitcast.158, bf16[2,8,128,2048]{3,2,1,0:T(8,128)(2,1)} %bitcast.144, s32[]{:T(128)S(6)} %select_n.79), kind=kOutput, calls=%fused_computation.21 | convolution fusion | flops 1073741824 | bytes 9961476 | tf_op jit(solution)/shard_map/xti,kxtw->kiw/dot_general | solution.py:43
  62.5 4.5 %fusion.10 = f32[4,256,2048,1]{2,1,3,0:T(8,128)} fusion(bf16[4,2,128,256]{2,3,1,0:T(8,128)(2,1)S(1)} %bitcast.164, bf16[2,8,128,2048]{3,2,1,0:T(8,128)(2,1)S(1)} %bitcast.148, s32[]{:T(128)S(6)} %select_n.81), kind=kOutput, calls=%fused_computation.19 | convolution fusion | flops 1073741824 | bytes 9961476 | tf_op jit(solution)/shard_map/xti,kxtw->kiw/dot_general | solution.py:43
  67.2 1.2 collective-permute-done.5
  68.7 4.1 %collective-permute-start.6 = (bf16[8,128,256]{1,2,0:T(8,128)(2,1)S(1)}, bf16[8,128,256]{1,2,0:T(8,128)(2,1)S(1)}, u32[]{:S(2)}, u32[]{:S(2)}) collective-permute-start(bf16[8,128,256]{1,2,0:T(8,128)(2,1)S(1)} %get-tuple-element.6), channel_id=1, source_target_pairs={{0,1},{1,0},{2,3},{3,2},{4,5},{5,4},{6,7},{7,6},{8,9},{9,8},{10,11... | collective-permute-start | bytes 1572872 | tf_op jit(solution)/shard_map/ppermute | solution.py:52
  72.8 4.5 %fusion.8 = f32[4,256,2048,1]{2,1,3,0:T(8,128)} fusion(bf16[4,2,128,256]{2,3,1,0:T(8,128)(2,1)S(1)} %bitcast.157, bf16[2,8,128,2048]{3,2,1,0:T(8,128)(2,1)S(1)} %bitcast.149, s32[]{:T(128)S(6)} %select_n.83), kind=kOutput, calls=%fused_computation.17 | convolution fusion | flops 1073741824 | bytes 9961476 | tf_op jit(solution)/shard_map/xti,kxtw->kiw/dot_general | solution.py:43
  77.3 4.5 %fusion.6 = f32[4,256,2048,1]{2,1,3,0:T(8,128)} fusion(bf16[4,2,128,256]{2,3,1,0:T(8,128)(2,1)S(1)} %bitcast.163, bf16[2,8,128,2048]{3,2,1,0:T(8,128)(2,1)S(1)} %bitcast.150, s32[]{:T(128)S(6)} %select_n.85), kind=kOutput, calls=%fused_computation.15 | convolution fusion | flops 1073741824 | bytes 9961476 | tf_op jit(solution)/shard_map/xti,kxtw->kiw/dot_general | solution.py:43
  81.8 4.5 %fusion.3 = f32[4,256,2048,1]{2,1,3,0:T(8,128)} fusion(bf16[4,2,128,256]{2,3,1,0:T(8,128)(2,1)S(1)} %bitcast.165, bf16[2,8,128,2048]{3,2,1,0:T(8,128)(2,1)S(1)} %bitcast.151, s32[]{:T(128)S(6)} %select_n.89), kind=kOutput, calls=%fused_computation.12 | convolution fusion | flops 1073741824 | bytes 9961476 | tf_op jit(solution)/shard_map/xti,kxtw->kiw/dot_general | solution.py:43
  86.2 4.5 %fusion.1 = f32[4,256,2048,1]{2,1,3,0:T(8,128)} fusion(bf16[4,2,128,256]{2,3,1,0:T(8,128)(2,1)S(1)} %bitcast.166, bf16[2,8,128,2048]{3,2,1,0:T(8,128)(2,1)S(1)} %bitcast.152, s32[]{:T(128)S(6)} %select_n.91), kind=kOutput, calls=%fused_computation.10 | convolution fusion | flops 1073741824 | bytes 9961476 | tf_op jit(solution)/shard_map/xti,kxtw->kiw/dot_general | solution.py:43
  90.7 23.0 %fusion = f32[4,2048,256]{1,2,0:T(8,128)} fusion(f32[4,256,2048,1]{2,1,3,0:T(8,128)} %fusion.1, f32[4,256,2048,1]{2,1,3,0:T(8,128)} %fusion.3, f32[4,256,2048,1]{2,1,3,0:T(8,128)} %fusion.6, f32[4,256,2048,1]{2,1,3,0:T(8,128)} %fusion.8, f32[4,256,2048,1]{2,1,3,0:T(8,128)} %fusion.10, f32[4,256,2048,1]{2,1,3,0:T(8,128)} %fusion.12, ...), kind=kOutput, calls=%fused_computation.1 | convolution fusion | flops 1088421888 | bytes 68681728 | tf_op jit(solution)/shard_map/xti,kxtw->kiw/dot_general | solution.py:43
  113.7 11.8 %reshape.80 = f32[4,2,2,512,256]{3,2,1,4,0:T(2,128)} reshape(f32[4,2048,256]{1,2,0:T(8,128)} %fusion) | data formatting | bytes 16777216 | tf_op jit(solution)/shard_map/reshape | solution.py:57
  125.4 12.1 %constant_dynamic-slice_fusion.1 = (f32[4,2,1,512,256]{3,2,1,4,0:T(1,128)}, f32[4,2,1,512,256]{3,2,1,4,0:T(1,128)}) fusion(f32[4,2,2,512,256]{3,2,1,4,0:T(2,128)} %reshape.80, s32[]{:T(128)S(6)} %select_n.92, s32[]{:T(128)S(6)} %select_n.93), kind=kLoop, calls=%fused_computation.44 | loop fusion | bytes 16777224 | tf_op jit(solution)/shard_map/jit(dynamic_index_in_dim)/dynamic_slice | solution.py:58
  137.6 10.9 %copy.38 = f32[4,2,1,512,256]{4,3,1,0,2:T(8,128)} copy(f32[4,2,1,512,256]{3,2,1,4,0:T(1,128)} %get-tuple-element.3) | data formatting | bytes 8388608 | tf_op jit(solution)/shard_map/jit(dynamic_index_in_dim)/dynamic_slice | solution.py:59
  148.5 1.4 collective-permute-start.8
  149.9 10.9 %copy.37 = f32[4,2,1,512,256]{4,3,1,0,2:T(8,128)} copy(f32[4,2,1,512,256]{3,2,1,4,0:T(1,128)} %get-tuple-element.2) | data formatting | bytes 8388608 | tf_op jit(solution)/shard_map/jit(dynamic_index_in_dim)/dynamic_slice | solution.py:58
  160.8 6.0 %bitcast_add_fusion.7 = f32[4,2,512,256]{3,2,1,0:T(8,128)} fusion(f32[4,2,512,256]{3,2,1,0:T(8,128)} %collective-permute-done.8, f32[4,2,1,512,256]{4,3,1,0,2:T(8,128)} %copy.37), kind=kLoop, calls=%fused_computation.8 | loop fusion | flops 1048576 | bytes 12582912 | tf_op jit(solution)/shard_map/add | solution.py:60
  166.8 4.7 %all-to-all-start.1 = ((f32[8,512,256]{2,1,0:T(8,128)}), f32[8,512,256]{2,1,0:T(8,128)}, u32[]{:S(2)}, u32[]{:S(2)}) async-start(f32[8,512,256]{2,1,0:T(8,128)} %bitcast.142), calls=%async_computation.1 | async-start | bytes 8388608 | tf_op jit(solution)/shard_map/all_to_all | solution.py:61
  171.7 50.8 %all-to-all-done.1 = f32[8,512,256]{2,1,0:T(8,128)} async-done(((f32[8,512,256]{2,1,0:T(8,128)}), f32[8,512,256]{2,1,0:T(8,128)}, u32[]{:S(2)}, u32[]{:S(2)}) %all-to-all-start.1) | async-done | bytes 4194336 | tf_op jit(solution)/shard_map/all_to_all | solution.py:61
  222.5 2.5 reduce_sum.27
  225.2 9.7 %all_to_all.26 = f32[8,32,256]{2,1,0:T(8,128)S(1)} all-to-all(f32[8,32,256]{2,1,0:T(8,128)S(1)} %fusion.24), channel_id=1, replica_groups=mesh['y'=4,'xlo'=2,'z'=8,'xhi'=2,'core'=2] {'xlo','xhi','core'}, dimensions={0} | all-to-all | bytes 524288 | tf_op jit(solution)/shard_map/all_to_all | solution.py:66
  235.0 15.6 %all_to_all.27 = f32[8,32,256]{2,1,0:T(8,128)S(1)} all-to-all(f32[8,32,256]{2,1,0:T(8,128)S(1)} %broadcast_in_dim.22), channel_id=1, replica_groups=mesh['y'=4,'xlo'=2,'z'=8,'xhi'=2,'core'=2] {'z'}, dimensions={0} | all-to-all | bytes 524288 | tf_op jit(solution)/shard_map/all_to_all | solution.py:67
  251.3 5.9 %all-to-all-start.4 = ((f32[8,32,256]{2,1,0:T(8,128)}), f32[8,32,256]{2,1,0:T(8,128)S(1)}, u32[]{:S(2)}, u32[]{:S(2)}) async-start(f32[8,32,256]{2,1,0:T(8,128)} %broadcast_in_dim.23), calls=%async_computation.4 | async-start | bytes 524288 | tf_op jit(solution)/shard_map/all_to_all | solution.py:68
  258.0 5.7 %all-to-all-done.4 = f32[8,32,256]{2,1,0:T(8,128)S(1)} async-done(((f32[8,32,256]{2,1,0:T(8,128)}), f32[8,32,256]{2,1,0:T(8,128)S(1)}, u32[]{:S(2)}, u32[]{:S(2)}) %all-to-all-start.4) | async-done | bytes 262176 | tf_op jit(solution)/shard_map/all_to_all | solution.py:68
  (37 shorter events, 4.6 us)
Async XLA Ops:
  17.8 3.4 %collective-permute-start = (bf16[8,128,256]{1,2,0:T(8,128)(2,1)S(1)}, bf16[8,128,256]{1,2,0:T(8,128)(2,1)S(1)}, u32[]{:S(2)}, u32[]{:S(2)}) collective-permute-start(bf16[8,128,256]{1,2,0:T(8,128)(2,1)S(1)} %all_to_all.25), channel_id=1, source_target_pairs={{0,1},{1,0},{2,3},{3,2},{4,5},{5,4},{6,7},{7,6},{8,9},{9,8},{10,11... | collective-permute-start | bytes 1572872 | tf_op jit(solution)/shard_map/ppermute | solution.py:37
  21.3 17.4 %collective-permute-start.1 = (bf16[2,8,128,256]{2,3,1,0:T(8,128)(2,1)S(1)}, bf16[2,8,128,256]{2,3,1,0:T(8,128)(2,1)S(1)}, u32[]{:S(2)}, u32[]{:S(2)}) collective-permute-start(bf16[2,8,128,256]{2,3,1,0:T(8,128)(2,1)S(1)} %pad_maximum_fusion), channel_id=1, source_target_pairs={{0,4},{1,29},{4,8},{5,1},{8,12},{9,5},{12,16},{13,9},{16,20},{17,1... | collective-permute-start | bytes 3145736 | tf_op jit(solution)/shard_map/ppermute | solution.py:51
  38.7 14.9 %collective-permute-start.3 = (bf16[2,8,128,256]{2,3,1,0:T(8,128)(2,1)S(1)}, bf16[2,8,128,256]{2,3,1,0:T(8,128)(2,1)S(1)}, u32[]{:S(2)}, u32[]{:S(2)}) collective-permute-start(bf16[2,8,128,256]{2,3,1,0:T(8,128)(2,1)S(1)} %collective-permute-done.1), channel_id=1, source_target_pairs={{0,4},{1,29},{4,8},{5,1},{8,12},{9,5},{12,16},{13,9},{16,20},{17,1... | collective-permute-start | bytes 3145736 | tf_op jit(solution)/shard_map/ppermute | solution.py:51
  41.9 20.6 %collective-permute-start.2 = (bf16[8,128,256]{1,2,0:T(8,128)(2,1)S(1)}, bf16[8,128,256]{1,2,0:T(8,128)(2,1)S(1)}, u32[]{:S(2)}, u32[]{:S(2)}) collective-permute-start(bf16[8,128,256]{1,2,0:T(8,128)(2,1)S(1)} %get-tuple-element.8), channel_id=1, source_target_pairs={{0,1},{1,0},{2,3},{3,2},{4,5},{5,4},{6,7},{7,6},{8,9},{9,8},{10,11... | collective-permute-start | bytes 1572872 | tf_op jit(solution)/shard_map/ppermute | solution.py:52
  42.0 20.5 %slice-start = ((s8[8388608]{0:T(1024)(128)(4,1)}), s8[4194304]{0:T(1024)(128)(4,1)S(1)}, s32[]{:S(2)}) async-start(s8[8388608]{0:T(1024)(128)(4,1)} %bitcast.146), calls=%async_computation.5 | async-start | bytes 8388608
  53.6 14.9 %collective-permute-start.5 = (bf16[2,8,128,256]{2,3,1,0:T(8,128)(2,1)S(1)}, bf16[2,8,128,256]{2,3,1,0:T(8,128)(2,1)S(1)}, u32[]{:S(2)}, u32[]{:S(2)}) collective-permute-start(bf16[2,8,128,256]{2,3,1,0:T(8,128)(2,1)S(1)} %collective-permute-done.3), channel_id=1, source_target_pairs={{0,4},{1,29},{4,8},{5,1},{8,12},{9,5},{12,16},{13,9},{16,20},{17,1... | collective-permute-start | bytes 3145736 | tf_op jit(solution)/shard_map/ppermute | solution.py:51
  56.7 5.9 %slice-start.1 = ((s8[8388608]{0:T(1024)(128)(4,1)}), s8[4194304]{0:T(1024)(128)(4,1)S(1)}, s32[]{:S(2)}) async-start(s8[8388608]{0:T(1024)(128)(4,1)} %bitcast.146), calls=%async_computation.6 | async-start | bytes 8388608
  67.1 10.2 %collective-permute-start.4 = (bf16[8,128,256]{1,2,0:T(8,128)(2,1)S(1)}, bf16[8,128,256]{1,2,0:T(8,128)(2,1)S(1)}, u32[]{:S(2)}, u32[]{:S(2)}) collective-permute-start(bf16[8,128,256]{1,2,0:T(8,128)(2,1)S(1)} %get-tuple-element.10), channel_id=1, source_target_pairs={{0,1},{1,0},{2,3},{3,2},{4,5},{5,4},{6,7},{7,6},{8,9},{9,8},{10,11... | collective-permute-start | bytes 1572872 | tf_op jit(solution)/shard_map/ppermute | solution.py:52
  68.7 13.1 %collective-permute-start.6 = (bf16[8,128,256]{1,2,0:T(8,128)(2,1)S(1)}, bf16[8,128,256]{1,2,0:T(8,128)(2,1)S(1)}, u32[]{:S(2)}, u32[]{:S(2)}) collective-permute-start(bf16[8,128,256]{1,2,0:T(8,128)(2,1)S(1)} %get-tuple-element.6), channel_id=1, source_target_pairs={{0,1},{1,0},{2,3},{3,2},{4,5},{5,4},{6,7},{7,6},{8,9},{9,8},{10,11... | collective-permute-start | bytes 1572872 | tf_op jit(solution)/shard_map/ppermute | solution.py:52
  77.2 9.0 %collective-permute-start.7 = (bf16[8,128,256]{1,2,0:T(8,128)(2,1)S(1)}, bf16[8,128,256]{1,2,0:T(8,128)(2,1)S(1)}, u32[]{:S(2)}, u32[]{:S(2)}) collective-permute-start(bf16[8,128,256]{1,2,0:T(8,128)(2,1)S(1)} %get-tuple-element.5), channel_id=1, source_target_pairs={{0,4},{1,29},{4,8},{5,1},{8,12},{9,5},{12,16},{13,9},{16,20},{17,1... | collective-permute-start | bytes 1572872 | tf_op jit(solution)/shard_map/ppermute | solution.py:54
  148.5 12.3 %collective-permute-start.8 = (f32[4,2,512,256]{3,2,1,0:T(8,128)}, f32[4,2,512,256]{3,2,1,0:T(8,128)}, u32[]{:S(2)}, u32[]{:S(2)}) collective-permute-start(f32[4,2,512,256]{3,2,1,0:T(8,128)} %bitcast.155), channel_id=1, source_target_pairs={{0,1},{1,0},{2,3},{3,2},{4,5},{5,4},{6,7},{7,6},{8,9},{9,8},{10,11... | collective-permute-start | bytes 12582920 | tf_op jit(solution)/shard_map/ppermute | solution.py:60
  160.8 10.7 %copy-start = (bf16[1,512,256]{2,1,0:T(8,128)(2,1)S(1)}, bf16[1,512,256]{2,1,0:T(8,128)(2,1)}, u32[]{:S(2)}) copy-start(bf16[1,512,256]{2,1,0:T(8,128)(2,1)} %param.5) | copy-start | bytes 786436
  166.8 96.9 %copy-start.1 = (f32[1,256,256]{2,1,0:T(8,128)S(1)}, f32[1,256,256]{2,1,0:T(8,128)}, u32[]{:S(2)}) copy-start(f32[1,256,256]{2,1,0:T(8,128)} %param.7) | copy-start | bytes 786436
  166.8 55.7 %all-to-all-start.1 = ((f32[8,512,256]{2,1,0:T(8,128)}), f32[8,512,256]{2,1,0:T(8,128)}, u32[]{:S(2)}, u32[]{:S(2)}) async-start(f32[8,512,256]{2,1,0:T(8,128)} %bitcast.142), calls=%async_computation.1 | async-start | bytes 8388608 | tf_op jit(solution)/shard_map/all_to_all | solution.py:61
  251.3 12.4 %all-to-all-start.4 = ((f32[8,32,256]{2,1,0:T(8,128)}), f32[8,32,256]{2,1,0:T(8,128)S(1)}, u32[]{:S(2)}, u32[]{:S(2)}) async-start(f32[8,32,256]{2,1,0:T(8,128)} %broadcast_in_dim.23), calls=%async_computation.4 | async-start | bytes 524288 | tf_op jit(solution)/shard_map/all_to_all | solution.py:68

commit v2 on v1

v2 whole, which is shorter than its diff:
```python
import functools

import jax
import jax.numpy as jnp
from jax import lax
from jax.experimental import pallas as pl
from jax.experimental.pallas import tpu as pltpu
from jax.sharding import Mesh, PartitionSpec as P

AXES = ("y", "xlo", "z", "xhi", "core")
ROW = ("xlo", "z")
COL = ("xhi", "core")
ALONG_X = ("xlo", "xhi", "core")
F32 = jnp.float32
F16 = jnp.float16
BF16 = jnp.bfloat16
SWAP = [(0, 1), (1, 0)]
VMEM = 48 * 2**20


def products(cols, rows):
    turned = [c[...].reshape(-1, c.shape[-1]).T for c in cols]
    kids = sum(r.shape[0] for r in rows[0])
    out = []
    for k in range(kids):
        total = None
        for t, group in zip(turned, rows):
            part, at = group[0], k
            if at >= part.shape[0]:
                at -= part.shape[0]
                part = group[1]
            d = jnp.dot(t, part[at], preferred_element_type=F32)
            total = d if total is None else total + d
        out.append(total)
    return out


def add_kernel(num, more, where_ref, *refs):
    cols, rows = refs[:num], [[r] for r in refs[num : 2 * num]]
    out_ref = refs[-1]
    for k, value in enumerate(products(cols, rows)):
        out_ref[k] = refs[2 * num][k] + value if more else value


def add_blocks(blocks, where, rows, partial=None):
    num, tile = len(rows), 512
    kids, _, width = rows[0].shape
    _, _, quarter, height = blocks.shape
    cost = 2 * num * 2 * quarter * height * kids * width
    moved = num * (blocks.nbytes // 8 + rows[0].nbytes) + kids * height * width * 4 * (1 if partial is None else 2)
    own = pl.BlockSpec((kids, tile, width), lambda i, w: (0, i, 0))
    return pl.pallas_call(
        functools.partial(add_kernel, num, partial is not None),
        out_shape=jax.ShapeDtypeStruct((kids, height, width), F32),
        grid_spec=pltpu.PrefetchScalarGridSpec(
            num_scalar_prefetch=1,
            grid=(height // tile,),
            in_specs=[
                pl.BlockSpec((2, 1, quarter, tile), lambda i, w, b=b: (0, w[b], 0, i)) for b in range(num)
            ]
            + [pl.BlockSpec(r.shape, lambda i, w: (0, 0, 0)) for r in rows]
            + ([] if partial is None else [own]),
            out_specs=own,
        ),
        input_output_aliases={} if partial is None else {1 + 2 * num: 0},
        compiler_params=pltpu.CompilerParams(vmem_limit_bytes=VMEM),
        cost_estimate=pl.CostEstimate(flops=cost, bytes_accessed=moved, transcendentals=0),
        name="add_blocks",
    )(where, *([blocks] * num), *rows, *([] if partial is None else [partial]))


def half_kernel(where_ref, col_ref, low_ref, high_ref, partial_ref, out_ref, top_ref):
    @pl.when((pl.program_id(0) == 0) & (pl.program_id(1) == 0))
    def _():
        top_ref[...] = jnp.zeros_like(top_ref)

    top = top_ref[...]
    for k, value in enumerate(products([col_ref], [[low_ref, high_ref]])):
        value = partial_ref[k] + value
        out_ref[k, 0] = value
        top = jnp.maximum(top, jnp.max(jnp.abs(value).reshape(-1, *top.shape), axis=0))
    top_ref[...] = top


def finish_half(blocks, where, low, high, partial):
    tile = 256
    _, _, quarter, height = blocks.shape
    kids, _, width = partial.shape
    per = height // 4 // tile
    return pl.pallas_call(
        half_kernel,
        out_shape=(
            jax.ShapeDtypeStruct((kids, 2, height // 4, width), F32),
            jax.ShapeDtypeStruct((8, width), F32),
        ),
        grid_spec=pltpu.PrefetchScalarGridSpec(
            num_scalar_prefetch=1,
            grid=(2, per),
            in_specs=[
                pl.BlockSpec((2, 1, quarter, tile), lambda h, i, w: (0, w[0], 0, (h * 2 + w[1]) * per + i)),
                pl.BlockSpec(low.shape, lambda h, i, w: (0, 0, 0)),
                pl.BlockSpec(high.shape, lambda h, i, w: (0, 0, 0)),
                pl.BlockSpec((kids, tile, width), lambda h, i, w: (0, (h * 2 + w[1]) * per + i, 0)),
            ],
            out_specs=(
                pl.BlockSpec((kids, 1, tile, width), lambda h, i, w: (0, h, i, 0)),
                pl.BlockSpec((8, width), lambda h, i, w: (0, 0)),
            ),
        ),
        compiler_params=pltpu.CompilerParams(vmem_limit_bytes=VMEM),
        cost_estimate=pl.CostEstimate(
            flops=2 * 2 * quarter * (height // 2) * kids * width,
            bytes_accessed=blocks.nbytes // 16 + partial.nbytes,
            transcendentals=0,
        ),
        name="finish_half",
    )(where, blocks, low, high, partial)


def shards(ancestor_cols, factor, block_mask, diag_inverse):
    num_z = lax.axis_size("z")
    num_y = lax.axis_size("y")
    quarter = ancestor_cols.shape[2]
    height = ancestor_cols.shape[3]
    width = factor.shape[2]
    sub = factor.shape[1]
    z = lax.axis_index("z")
    core = lax.axis_index("core")
    group = (lax.axis_index("xlo") * num_z + z) * 4 + lax.axis_index("xhi") * 2 + core
    per = sub // width
    live = lax.dynamic_slice_in_dim(block_mask[0], group * per, per, 0)
    masked = (factor.reshape(per, width, width) * live[:, None, None].astype(BF16)).reshape(sub, width)
    blocks = ancestor_cols.reshape(2, num_z, quarter, height)

    pieces = jnp.broadcast_to(masked.reshape(num_y, 1, quarter, width), (num_y, 2, quarter, width))
    own = lax.all_to_all(pieces.reshape(num_y * 2, quarter, width), ("y", "xlo"), 0, 0)
    own = own.reshape(num_y, 2 * quarter, width)

    up = [(i, (i + 1) % num_z) for i in range(num_z)]
    down = [(i, (i - 1) % num_z) for i in range(num_z)]

    def at(*offsets):
        return jnp.stack([jnp.remainder(z + o, num_z) for o in offsets]).astype(jnp.int32)

    below, above = lax.ppermute(own, "z", up), lax.ppermute(own, "z", down)
    below2, above2 = lax.ppermute(below, "z", up), lax.ppermute(above, "z", down)
    partial = add_blocks(blocks, at(0, -1, 1), [own, below, above])
    below3, above3 = lax.ppermute(below2, "z", up), lax.ppermute(above2, "z", down)
    partial = add_blocks(blocks, at(-2, 2), [below2, above2], partial)
    half = num_y // 2
    low, high = lax.ppermute(below3[:half], "z", up), lax.ppermute(above3[half:], "z", down)
    partial = add_blocks(blocks, at(-3, 3), [below3, above3], partial)

    far = jnp.remainder(z + 4, num_z)
    give, give_top = finish_half(blocks, jnp.stack([far, 1 - core]).astype(jnp.int32), low, high, partial)
    got, got_top = lax.ppermute(give, "core", SWAP), lax.ppermute(give_top, "core", SWAP)
    keep, keep_top = finish_half(blocks, jnp.stack([far, core]).astype(jnp.int32), low, high, partial)

    bound = jnp.maximum(jnp.max(keep_top) + jnp.max(got_top), 2.0**-100)
    power = jnp.ceil(jnp.log2(bound)) + 1.0
    scaled = ((keep + got) * jnp.exp2(15.0 - power)).astype(F16).reshape(num_y * 2, sub, width)
    tail = jnp.broadcast_to(power.astype(F16), (num_y * 2, 16, width))
    parts = lax.all_to_all(jnp.concatenate([scaled, tail], 1), ("y", "xhi"), 0, 0)
    back = jnp.exp2(parts[:, sub, 0].astype(F32) - 15.0)
    total = jnp.sum(parts[:, :sub].astype(F32) * back[:, None, None], 0)
    inverse_cols = (-total).astype(BF16)

    product = jnp.einsum("jw,jv->wv", masked, inverse_cols, preferred_element_type=F32)
    split = product.reshape(8, width // 8, width)
    mine = jnp.sum(lax.all_to_all(split, ALONG_X, 0, 0), 0)
    over_z = jnp.sum(lax.all_to_all(jnp.broadcast_to(mine, (num_z,) + mine.shape), "z", 0, 0), 0)
    whole = lax.all_to_all(jnp.broadcast_to(over_z, (8,) + over_z.shape), ALONG_X, 0, 0)
    return inverse_cols[None], diag_inverse - whole.reshape(1, width, width)


def solution(mesh):
    fine = Mesh(mesh.devices.reshape(4, 2, 8, 2, 2), AXES)
    rows = ROW + COL
    in_specs = (P(None, COL, "y", ROW), P("y", rows, None), P("y", None), P("y", None, None))
    out_specs = (P("y", rows, None), P("y", None, None))
    return jax.shard_map(shards, mesh=fine, in_specs=in_specs, out_specs=out_specs, check_vma=False)
```

time: 266 us -> 178 us (0.67)
  matrix products: 57.3 us -> 0.23 us
  local copies, waits for them, and re-layouts: 47.5 us -> 5.15 us
  Pallas kernels: 0 us -> 37.1 us
  waiting for transfers between devices: 76.6 us -> 53.8 us
    dot_general x8 -> x0, matrix products: 57.1 us -> none  [term(): jnp.einsum('xti,kxtw->kiw', cols, rows.reshape(num_y, 2, quarter, width),...]
    pallas_call x0 -> x5, Pallas kernels: none -> 37.1 us  [the longest x3 26.6 us: add_blocks(): pl.pallas_call(functools.partial(add_kernel, num, partial is not None), o...]
    dynamic_slice x3 -> x0, local copies, waits for them, and re-layouts: 34 us -> none  [the longest x2 23 us: shards(): keep = lax.dynamic_index_in_dim(halves, core, 2, keepdims=False)]
    all_to_all x1, waiting for transfers between devices: 50.8 us -> 28.1 us  [shards(): lax.all_to_all(jnp.concatenate([scaled, tail], 1), ('y', 'xhi'), 0, 0)]
    reshape x1 -> x0, local copies, waits for them, and re-layouts: 11.8 us -> none  [shards(): halves = partial.reshape(num_y, 2, 2, sub, width)]
    add x1 -> x0, other arithmetic: 5.97 us -> none  [shards(): summed = keep + lax.ppermute(give, 'core', SWAP)]
    convert_element_type x1 -> x2, other arithmetic: 0.74 us -> 4.89 us  [the longest x1 4.15 us: shards(): ((keep + got) * jnp.exp2(15.0 - power)).astype(F16)]
    ppermute x9 -> x10, starting transfers between devices: 19.4 us -> 18.7 us  [the longest x2 5.58 us: shards(): below, above = (lax.ppermute(own, 'z', up), lax.ppermute(own, 'z', down))]
  transfers between devices with their start and end apart: 11 -> 12, of which waited for: 6 -> 5; matrix products, arithmetic and copies ran while one was open for 16% -> 1% of each run, Pallas kernels for 0% -> 18%
where the time goes in v2:
time: 178 us; the launch traced here: 177 us
  waiting for transfers between devices  53.8 us (30%)
  blocking collectives  40.3 us (23%)
  Pallas kernels  37.1 us (21%)
  starting transfers between devices  28.6 us (16%)
  other arithmetic  9.46 us (5%)
  local copies, waits for them, and re-layouts  5.15 us (3%)
  between operations  2.19 us (1%)
    all_to_all x1, waiting for transfers between devices, shards(): lax.all_to_all(jnp.concatenate([scaled, tail], 1), ('y', 'xhi'), 0, 0)  28.1 us
    pallas_call x3, Pallas kernels, add_blocks(): pl.pallas_call(functools.partial(add_kernel, num, partial is not None), o...  26.6 us
    all_to_all x1, blocking collectives, shards(): lax.all_to_all(pieces.reshape(num_y * 2, quarter, width), ('y', 'xlo'), 0...  15 us
    all_to_all x1, blocking collectives, shards(): lax.all_to_all(jnp.broadcast_to(mine, (num_z,) + mine.shape), 'z', 0, 0)  14.9 us
    pallas_call x2, Pallas kernels, finish_half(): pl.pallas_call(half_kernel, out_shape=(jax.ShapeDtypeStruct((kids, 2, hei...  10.5 us
    all_to_all x1, blocking collectives, shards(): mine = jnp.sum(lax.all_to_all(split, ALONG_X, 0, 0), 0)  10.5 us
    ppermute x2, waiting for transfers between devices, shards(): below, above = (lax.ppermute(own, 'z', up), lax.ppermute(own, 'z', down))  10.4 us
    ppermute x1, waiting for transfers between devices, shards(): lax.ppermute(below, 'z', up)  9.29 us
  transfers between devices with their start and end apart: 12, of which 5 were waited for; matrix products, arithmetic and copies ran while one was open for 1% of the time, Pallas kernels for 18%

profile of v2, /device:TPU:1, one launch (start us, length us, event | category | flops | bytes accessed | tf_op | source)
XLA Modules:
  0.0 176.8 jit_solution(11106965723918796295)
XLA Ops:
  0.6 0.7 convert_bitcast_fusion
  1.5 1.0 broadcast_multiply_fusion
  2.6 15.0 %all_to_all.25 = bf16[8,128,256]{2,1,0:T(8,128)(2,1)S(1)} all-to-all(bf16[8,128,256]{2,1,0:T(8,128)(2,1)S(1)} %bitcast.49), channel_id=1, replica_groups=mesh['y'=4,'xlo'=2,'z'=8,'xhi'=2,'core'=2] {'y','xlo'}, dimensions={0} | all-to-all | bytes 1048576 | tf_op jit(solution)/shard_map/all_to_all | solution.py:136
  17.6 1.6 collective-permute-start
  19.2 3.9 %collective-permute-start.4 = (bf16[4,256,256]{2,1,0:T(8,128)(2,1)S(1)}, bf16[4,256,256]{2,1,0:T(8,128)(2,1)S(1)}, u32[]{:S(2)}, u32[]{:S(2)}) collective-permute-start(bf16[4,256,256]{2,1,0:T(8,128)(2,1)S(1)} %bitcast.37), channel_id=1, source_target_pairs={{0,28},{4,0},{8,4},{12,8},{16,12},{20,16},{24,20},{28,24},{1,29},{... | collective-permute-start | bytes 1572872 | tf_op jit(solution)/shard_map/ppermute | solution.py:145
  23.2 10.4 %collective-permute-done.refs_4_ = bf16[4,256,256]{2,1,0:T(8,128)(2,1)S(1)} collective-permute-done((bf16[4,256,256]{2,1,0:T(8,128)(2,1)S(1)}, bf16[4,256,256]{2,1,0:T(8,128)(2,1)S(1)}, u32[]{:S(2)}, u32[]{:S(2)}) %collective-permute-start) | collective-permute-done | bytes 524320 | tf_op jit(solution)/shard_map/ppermute | solution.py:145
  33.5 2.7 %collective-permute-start.5 = (bf16[4,256,256]{2,1,0:T(8,128)(2,1)S(1)}, bf16[4,256,256]{2,1,0:T(8,128)(2,1)S(1)}, u32[]{:S(2)}, u32[]{:S(2)}) collective-permute-start(bf16[4,256,256]{2,1,0:T(8,128)(2,1)S(1)} %collective-permute-done.4.refs_5_), channel_id=1, source_target_pairs={{0,28},{4,0},{8,4},{12,8},{16,12},{20,16},{24,20},{28,24},{1,29},{... | collective-permute-start | bytes 1572872 | tf_op jit(solution)/shard_map/ppermute | solution.py:146
  36.4 9.3 %collective-permute-done.1.refs_2_ = bf16[4,256,256]{2,1,0:T(8,128)(2,1)S(1)} collective-permute-done((bf16[4,256,256]{2,1,0:T(8,128)(2,1)S(1)}, bf16[4,256,256]{2,1,0:T(8,128)(2,1)S(1)}, u32[]{:S(2)}, u32[]{:S(2)}) %collective-permute-start.1) | collective-permute-done | bytes 524320 | tf_op jit(solution)/shard_map/ppermute | solution.py:146
  45.7 2.7 %collective-permute-start.6 = (bf16[4,256,256]{2,1,0:T(8,128)(2,1)S(1)}, bf16[4,256,256]{2,1,0:T(8,128)(2,1)S(1)}, u32[]{:S(2)}, u32[]{:S(2)}) collective-permute-start(bf16[4,256,256]{2,1,0:T(8,128)(2,1)S(1)} %collective-permute-done.5.refs_3_), channel_id=1, source_target_pairs={{0,28},{4,0},{8,4},{12,8},{16,12},{20,16},{24,20},{28,24},{1,29},{... | collective-permute-start | bytes 1572872 | tf_op jit(solution)/shard_map/ppermute | solution.py:148
  48.5 8.0 %add_blocks.3.refs_4_ = f32[4,2048,256]{2,1,0:T(8,128)} custom-call(s32[3]{0:T(128)S(1)} %pad_add_fusion.3.where_ref, bf16[2,8,128,2048]{3,2,1,0:T(8,128)(2,1)} %bitcast.39, bf16[2,8,128,2048]{3,2,1,0:T(8,128)(2,1)} %bitcast.40, bf16[2,8,128,2048]{3,2,1,0:T(8,128)(2,1)} %bitcast.41, bf16[4,256,256]{2,1,0:T(8,128)(2,1)S(1)} %bitcast.38, ...), custom_call_target="tpu_custom_call" | custom-call | flops 3221225472 | bytes 13107200 | tf_op jit(solution)/shard_map/add_blocks/pallas_call | solution.py:52
  56.5 0.3 collective-permute-done.2.refs_2_
  57.0 2.7 %collective-permute-start.7 = (bf16[2,256,256]{2,1,0:T(8,128)(2,1)S(1)}, bf16[2,256,256]{2,1,0:T(8,128)(2,1)S(1)}, u32[]{:S(2)}, u32[]{:S(2)}) collective-permute-start(bf16[2,256,256]{2,1,0:T(8,128)(2,1)S(1)} %slice.17), channel_id=1, source_target_pairs={{0,28},{4,0},{8,4},{12,8},{16,12},{20,16},{24,20},{28,24},{1,29},{... | collective-permute-start | bytes 786440 | tf_op jit(solution)/shard_map/ppermute | solution.py:151
  59.7 9.3 %add_blocks.4.refs_4_ = f32[4,2048,256]{2,1,0:T(8,128)} custom-call(s32[2]{0:T(128)S(1)} %pad_add_fusion.2.where_ref, bf16[2,8,128,2048]{3,2,1,0:T(8,128)(2,1)} %bitcast.42, bf16[2,8,128,2048]{3,2,1,0:T(8,128)(2,1)} %bitcast.43, bf16[4,256,256]{2,1,0:T(8,128)(2,1)S(1)} %collective-permute-done.1.refs_2_, ...), custom_call_target="tpu_custom_call", output_to_operand_aliasing={{}: (5, {})} | custom-call | flops 2147483648 | bytes 19922944 | tf_op jit(solution)/shard_map/add_blocks/pallas_call | solution.py:52
  69.0 9.3 %add_blocks.5.partial_ref = f32[4,2048,256]{2,1,0:T(8,128)} custom-call(s32[2]{0:T(128)S(1)} %pad_add_fusion.1.where_ref, bf16[2,8,128,2048]{3,2,1,0:T(8,128)(2,1)} %bitcast.44, bf16[2,8,128,2048]{3,2,1,0:T(8,128)(2,1)} %bitcast.45, bf16[4,256,256]{2,1,0:T(8,128)(2,1)S(1)} %collective-permute-done.2.refs_2_, ...), custom_call_target="tpu_custom_call", output_to_operand_aliasing={{}: (5, {})} | custom-call | flops 2147483648 | bytes 19922944 | tf_op jit(solution)/shard_map/add_blocks/pallas_call | solution.py:52
  78.3 6.0 %finish_half.3 = (f32[4,2,512,256]{3,2,1,0:T(8,128)}, f32[8,256]{1,0:T(8,128)S(1)}) custom-call(s32[2]{0:T(128)S(1)} %get-tuple-element.11.where_ref, bf16[2,8,128,2048]{3,2,1,0:T(8,128)(2,1)} %bitcast.46, bf16[2,256,256]{2,1,0:T(8,128)(2,1)S(1)} %collective-permute-done.3.low_ref, bf16[2,256,256]{2,1,0:T(8,128)(2,1)S(1)} %collective-permute-done.7.high_ref, ...), custom_call_target="tpu_custom_call" | custom-call | flops 536870912 | bytes 8912896 | tf_op jit(solution)/shard_map/finish_half/pallas_call | solution.py:90
  84.3 4.9 %collective-permute-start.8 = (f32[4,2,512,256]{3,2,1,0:T(8,128)}, f32[4,2,512,256]{3,2,1,0:T(8,128)}, u32[]{:S(2)}, u32[]{:S(2)}) collective-permute-start(f32[4,2,512,256]{3,2,1,0:T(8,128)} %get-tuple-element.7), channel_id=1, source_target_pairs={{0,1},{1,0},{2,3},{3,2},{4,5},{5,4},{6,7},{7,6},{8,9},{9,8},{10,11... | collective-permute-start | bytes 12582920 | tf_op jit(solution)/shard_map/ppermute | solution.py:156
  89.2 4.5 %finish_half.2 = (f32[4,2,512,256]{3,2,1,0:T(8,128)S(1)}, f32[8,256]{1,0:T(8,128)S(1)}) custom-call(s32[2]{0:T(128)S(1)} %get-tuple-element.10.where_ref, bf16[2,8,128,2048]{3,2,1,0:T(8,128)(2,1)} %bitcast.47, bf16[2,256,256]{2,1,0:T(8,128)(2,1)S(1)} %collective-permute-done.3.low_ref, bf16[2,256,256]{2,1,0:T(8,128)(2,1)S(1)} %collective-permute-done.7.high_ref, ...), custom_call_target="tpu_custom_call" | custom-call | flops 536870912 | bytes 8912896 | tf_op jit(solution)/shard_map/finish_half/pallas_call | solution.py:90
  93.7 1.9 %copy-done = f32[4,2,512,256]{3,2,1,0:T(8,128)} copy-done((f32[4,2,512,256]{3,2,1,0:T(8,128)}, f32[4,2,512,256]{3,2,1,0:T(8,128)S(1)}, u32[]{:S(2)}) %copy-start) | copy-done | bytes 4194328
  95.6 0.6 reduce_max.18
  96.2 0.6 reduce_max.19
  98.2 4.1 %multiply_convert_fusion = f16[4,2,512,256]{3,2,1,0:T(8,128)(2,1)S(1)} fusion(f32[4,2,512,256]{3,2,1,0:T(8,128)} %copy-done, f32[4,2,512,256]{3,2,1,0:T(8,128)} %collective-permute-done.8, f32[]{:T(128)S(6)} %exp2.15), kind=kLoop, calls=%fused_computation.1 | loop fusion | flops 3145728 | bytes 10485764 | tf_op jit(solution)/shard_map/convert_element_type | solution.py:161
  102.4 1.9 %concatenate.3 = f16[8,528,256]{2,1,0:T(8,128)(2,1)} pad(f16[8,512,256]{2,1,0:T(8,128)(2,1)S(1)} %bitcast.48, f16[]{:T(256)S(6)} %convert_element_type.40), padding=0_0x0_16x0_0 | pad | bytes 4259842 | tf_op jit(solution)/shard_map/concatenate | solution.py:163
  104.3 4.0 %all-to-all-start.1 = ((f16[8,528,256]{2,1,0:T(8,128)(2,1)}), f16[8,528,256]{2,1,0:T(8,128)(2,1)S(1)}, u32[]{:S(2)}, u32[]{:S(2)}) async-start(f16[8,528,256]{2,1,0:T(8,128)(2,1)} %concatenate.3), calls=%async_computation.1 | async-start | bytes 4325376 | tf_op jit(solution)/shard_map/all_to_all | solution.py:163
  108.6 28.1 %all-to-all-done.1 = f16[8,528,256]{2,1,0:T(8,128)(2,1)S(1)} async-done(((f16[8,528,256]{2,1,0:T(8,128)(2,1)}), f16[8,528,256]{2,1,0:T(8,128)(2,1)S(1)}, u32[]{:S(2)}, u32[]{:S(2)}) %all-to-all-start.1) | async-done | bytes 2162720 | tf_op jit(solution)/shard_map/all_to_all | solution.py:163
  136.8 0.5 multiply_reduce_fusion
  137.6 10.5 %all_to_all.26 = f32[8,32,256]{2,1,0:T(8,128)S(1)} all-to-all(f32[8,32,256]{2,1,0:T(8,128)S(1)} %fusion), channel_id=1, replica_groups=mesh['y'=4,'xlo'=2,'z'=8,'xhi'=2,'core'=2] {'xlo','xhi','core'}, dimensions={0} | all-to-all | bytes 524288 | tf_op jit(solution)/shard_map/all_to_all | solution.py:170
  148.1 14.9 %all_to_all.27 = f32[8,32,256]{2,1,0:T(8,128)S(1)} all-to-all(f32[8,32,256]{2,1,0:T(8,128)S(1)} %broadcast_in_dim.7), channel_id=1, replica_groups=mesh['y'=4,'xlo'=2,'z'=8,'xhi'=2,'core'=2] {'z'}, dimensions={0} | all-to-all | bytes 524288 | tf_op jit(solution)/shard_map/all_to_all | solution.py:171
  163.0 0.7 broadcast_in_dim.8
  163.7 5.9 %all-to-all-start.4 = ((f32[8,32,256]{2,1,0:T(8,128)}), f32[8,32,256]{2,1,0:T(8,128)S(1)}, u32[]{:S(2)}, u32[]{:S(2)}) async-start(f32[8,32,256]{2,1,0:T(8,128)} %broadcast_in_dim.8), calls=%async_computation.4 | async-start | bytes 524288 | tf_op jit(solution)/shard_map/all_to_all | solution.py:172
  169.7 0.7 fusion.2
  170.4 5.7 %all-to-all-done.4 = f32[8,32,256]{2,1,0:T(8,128)S(1)} async-done(((f32[8,32,256]{2,1,0:T(8,128)}), f32[8,32,256]{2,1,0:T(8,128)S(1)}, u32[]{:S(2)}, u32[]{:S(2)}) %all-to-all-start.4) | async-done | bytes 262176 | tf_op jit(solution)/shard_map/all_to_all | solution.py:172
  176.1 0.7 bitcast_subtract_fusion
  (36 shorter events, 1.3 us)
Async XLA Ops:
  17.6 15.9 %collective-permute-start = (bf16[4,256,256]{2,1,0:T(8,128)(2,1)S(1)}, bf16[4,256,256]{2,1,0:T(8,128)(2,1)S(1)}, u32[]{:S(2)}, u32[]{:S(2)}) collective-permute-start(bf16[4,256,256]{2,1,0:T(8,128)(2,1)S(1)} %bitcast.36), channel_id=1, source_target_pairs={{0,4},{4,8},{8,12},{12,16},{16,20},{20,24},{24,28},{28,0},{1,5},{5... | collective-permute-start | bytes 1572872 | tf_op jit(solution)/shard_map/ppermute | solution.py:145
  19.2 14.3 %collective-permute-start.4 = (bf16[4,256,256]{2,1,0:T(8,128)(2,1)S(1)}, bf16[4,256,256]{2,1,0:T(8,128)(2,1)S(1)}, u32[]{:S(2)}, u32[]{:S(2)}) collective-permute-start(bf16[4,256,256]{2,1,0:T(8,128)(2,1)S(1)} %bitcast.37), channel_id=1, source_target_pairs={{0,28},{4,0},{8,4},{12,8},{16,12},{20,16},{24,20},{28,24},{1,29},{... | collective-permute-start | bytes 1572872 | tf_op jit(solution)/shard_map/ppermute | solution.py:145
  33.5 12.1 %collective-permute-start.1 = (bf16[4,256,256]{2,1,0:T(8,128)(2,1)S(1)}, bf16[4,256,256]{2,1,0:T(8,128)(2,1)S(1)}, u32[]{:S(2)}, u32[]{:S(2)}) collective-permute-start(bf16[4,256,256]{2,1,0:T(8,128)(2,1)S(1)} %collective-permute-done.refs_4_), channel_id=1, source_target_pairs={{0,4},{4,8},{8,12},{12,16},{16,20},{20,24},{24,28},{28,0},{1,5},{5... | collective-permute-start | bytes 1572872 | tf_op jit(solution)/shard_map/ppermute | solution.py:146
  33.5 12.1 %collective-permute-start.5 = (bf16[4,256,256]{2,1,0:T(8,128)(2,1)S(1)}, bf16[4,256,256]{2,1,0:T(8,128)(2,1)S(1)}, u32[]{:S(2)}, u32[]{:S(2)}) collective-permute-start(bf16[4,256,256]{2,1,0:T(8,128)(2,1)S(1)} %collective-permute-done.4.refs_5_), channel_id=1, source_target_pairs={{0,28},{4,0},{8,4},{12,8},{16,12},{20,16},{24,20},{28,24},{1,29},{... | collective-permute-start | bytes 1572872 | tf_op jit(solution)/shard_map/ppermute | solution.py:146
  45.7 11.2 %collective-permute-start.2 = (bf16[4,256,256]{2,1,0:T(8,128)(2,1)S(1)}, bf16[4,256,256]{2,1,0:T(8,128)(2,1)S(1)}, u32[]{:S(2)}, u32[]{:S(2)}) collective-permute-start(bf16[4,256,256]{2,1,0:T(8,128)(2,1)S(1)} %collective-permute-done.1.refs_2_), channel_id=1, source_target_pairs={{0,4},{4,8},{8,12},{12,16},{16,20},{20,24},{24,28},{28,0},{1,5},{5... | collective-permute-start | bytes 1572872 | tf_op jit(solution)/shard_map/ppermute | solution.py:148
  45.7 11.3 %collective-permute-start.6 = (bf16[4,256,256]{2,1,0:T(8,128)(2,1)S(1)}, bf16[4,256,256]{2,1,0:T(8,128)(2,1)S(1)}, u32[]{:S(2)}, u32[]{:S(2)}) collective-permute-start(bf16[4,256,256]{2,1,0:T(8,128)(2,1)S(1)} %collective-permute-done.5.refs_3_), channel_id=1, source_target_pairs={{0,28},{4,0},{8,4},{12,8},{16,12},{20,16},{24,20},{28,24},{1,29},{... | collective-permute-start | bytes 1572872 | tf_op jit(solution)/shard_map/ppermute | solution.py:148
  56.9 21.4 %collective-permute-start.3 = (bf16[2,256,256]{2,1,0:T(8,128)(2,1)S(1)}, bf16[2,256,256]{2,1,0:T(8,128)(2,1)S(1)}, u32[]{:S(2)}, u32[]{:S(2)}) collective-permute-start(bf16[2,256,256]{2,1,0:T(8,128)(2,1)S(1)} %slice.16), channel_id=1, source_target_pairs={{0,4},{4,8},{8,12},{12,16},{16,20},{20,24},{24,28},{28,0},{1,5},{5... | collective-permute-start | bytes 786440 | tf_op jit(solution)/shard_map/ppermute | solution.py:151
  57.0 21.3 %collective-permute-start.7 = (bf16[2,256,256]{2,1,0:T(8,128)(2,1)S(1)}, bf16[2,256,256]{2,1,0:T(8,128)(2,1)S(1)}, u32[]{:S(2)}, u32[]{:S(2)}) collective-permute-start(bf16[2,256,256]{2,1,0:T(8,128)(2,1)S(1)} %slice.17), channel_id=1, source_target_pairs={{0,28},{4,0},{8,4},{12,8},{16,12},{20,16},{24,20},{28,24},{1,29},{... | collective-permute-start | bytes 786440 | tf_op jit(solution)/shard_map/ppermute | solution.py:151
  84.3 14.0 %collective-permute-start.8 = (f32[4,2,512,256]{3,2,1,0:T(8,128)}, f32[4,2,512,256]{3,2,1,0:T(8,128)}, u32[]{:S(2)}, u32[]{:S(2)}) collective-permute-start(f32[4,2,512,256]{3,2,1,0:T(8,128)} %get-tuple-element.7), channel_id=1, source_target_pairs={{0,1},{1,0},{2,3},{3,2},{4,5},{5,4},{6,7},{7,6},{8,9},{9,8},{10,11... | collective-permute-start | bytes 12582920 | tf_op jit(solution)/shard_map/ppermute | solution.py:156
  89.2 7.1 %collective-permute-start.9 = (f32[8,256]{1,0:T(8,128)S(1)}, f32[8,256]{1,0:T(8,128)S(1)}, u32[]{:S(2)}, u32[]{:S(2)}) collective-permute-start(f32[8,256]{1,0:T(8,128)S(1)} %get-tuple-element.9), channel_id=1, source_target_pairs={{0,1},{1,0},{2,3},{3,2},{4,5},{5,4},{6,7},{7,6},{8,9},{9,8},{10,11... | collective-permute-start | bytes 24584 | tf_op jit(solution)/shard_map/ppermute | solution.py:156
  93.7 1.9 %copy-start = (f32[4,2,512,256]{3,2,1,0:T(8,128)}, f32[4,2,512,256]{3,2,1,0:T(8,128)S(1)}, u32[]{:S(2)}) copy-start(f32[4,2,512,256]{3,2,1,0:T(8,128)S(1)} %get-tuple-element.6) | copy-start | bytes 12582916
  102.4 5.9 %copy-start.1 = (bf16[1,512,256]{2,1,0:T(8,128)(2,1)S(1)}, bf16[1,512,256]{2,1,0:T(8,128)(2,1)}, u32[]{:S(2)}) copy-start(bf16[1,512,256]{2,1,0:T(8,128)(2,1)} %param.5) | copy-start | bytes 786436
  104.3 32.4 %all-to-all-start.1 = ((f16[8,528,256]{2,1,0:T(8,128)(2,1)}), f16[8,528,256]{2,1,0:T(8,128)(2,1)S(1)}, u32[]{:S(2)}, u32[]{:S(2)}) async-start(f16[8,528,256]{2,1,0:T(8,128)(2,1)} %concatenate.3), calls=%async_computation.1 | async-start | bytes 4325376 | tf_op jit(solution)/shard_map/all_to_all | solution.py:163
  108.3 67.8 %copy-start.2 = (f32[1,256,256]{2,1,0:T(8,128)S(1)}, f32[1,256,256]{2,1,0:T(8,128)}, u32[]{:S(2)}) copy-start(f32[1,256,256]{2,1,0:T(8,128)} %param.7) | copy-start | bytes 786436
  163.7 12.4 %all-to-all-start.4 = ((f32[8,32,256]{2,1,0:T(8,128)}), f32[8,32,256]{2,1,0:T(8,128)S(1)}, u32[]{:S(2)}, u32[]{:S(2)}) async-start(f32[8,32,256]{2,1,0:T(8,128)} %broadcast_in_dim.8), calls=%async_computation.4 | async-start | bytes 524288 | tf_op jit(solution)/shard_map/all_to_all | solution.py:172

commit v3 on v1

v3 whole, which is shorter than its diff:
```python
import functools

import jax
import jax.numpy as jnp
from jax import lax
from jax.experimental import pallas as pl
from jax.experimental.pallas import tpu as pltpu
from jax.sharding import Mesh, PartitionSpec as P

AXES = ("y", "xlo", "z", "xhi", "core")
ROW = ("xlo", "z")
COL = ("xhi", "core")
ALONG_X = ("xlo", "xhi", "core")
F32 = jnp.float32
F16 = jnp.float16
BF16 = jnp.bfloat16
SWAP = [(0, 1), (1, 0)]
TILE = 512


def turn_kernel(cols_ref, out_ref):
    out_ref[0] = cols_ref[...].reshape(-1, cols_ref.shape[-1]).T


def turn(blocks):
    pair, num, quarter, height = blocks.shape
    tile = 512
    return pl.pallas_call(
        turn_kernel,
        out_shape=jax.ShapeDtypeStruct((num, height, pair * quarter), BF16),
        grid=(num, height // tile),
        in_specs=[pl.BlockSpec((pair, 1, quarter, tile), lambda z, i: (0, z, 0, i))],
        out_specs=pl.BlockSpec((1, tile, pair * quarter), lambda z, i: (z, i, 0)),
        compiler_params=pltpu.CompilerParams(vmem_limit_bytes=16 * 2**20),
        cost_estimate=pl.CostEstimate(flops=0, bytes_accessed=2 * blocks.nbytes, transcendentals=0),
        name="turn",
    )(blocks)


def half_kernel(num, more, where_ref, turned_ref, *refs):
    rows, (out_ref, held, sems) = refs[:num], refs[-3:]
    kids, _, sub, _ = out_ref.shape
    per = sub // TILE

    def copy(c):
        begin = pl.multiple_of((2 * (c // per) + where_ref[num]) * sub + (c % per) * TILE, TILE)
        blocks = pl.ds(where_ref[0], 1) if num == 1 else slice(None)
        return pltpu.make_async_copy(turned_ref.at[blocks, pl.ds(begin, TILE)], held.at[c], sems.at[c])

    for c in range(2 * per):
        copy(c).start()

    @pl.loop(0, 2 * per)
    def _(c):
        copy(c).wait()
        here = pl.ds(pl.multiple_of((c % per) * TILE, TILE), TILE)
        cols = [held[c, 0 if num == 1 else where_ref[b]] for b in range(num)]
        cols = jnp.concatenate(cols, 1)
        for k in range(kids):
            value = jnp.dot(cols, jnp.concatenate([r[k] for r in rows], 0), preferred_element_type=F32)
            out_ref[k, c // per, here] = refs[num][k, c // per, here] + value if more else value


def half_product(turned, where, rows, partial=None):
    num = len(rows)
    count, height, depth = turned.shape
    kids, _, width = rows[0].shape
    sub = height // 4
    more = [] if partial is None else [partial]
    chunks = 2 * sub // TILE
    return pl.pallas_call(
        functools.partial(half_kernel, num, bool(more)),
        out_shape=jax.ShapeDtypeStruct((kids, 2, sub, width), F32),
        in_specs=[pl.BlockSpec(memory_space=pltpu.SMEM), pl.BlockSpec(memory_space=pl.ANY)]
        + [pl.BlockSpec(memory_space=pltpu.VMEM)] * (len(rows) + len(more)),
        out_specs=pl.BlockSpec(memory_space=pltpu.VMEM),
        scratch_shapes=[
            pltpu.VMEM((chunks, 1 if num == 1 else count, TILE, depth), BF16),
            pltpu.SemaphoreType.DMA((chunks,)),
        ],
        input_output_aliases={2 + len(rows): 0} if more else {},
        compiler_params=pltpu.CompilerParams(vmem_limit_bytes=20 * 2**20),
        cost_estimate=pl.CostEstimate(
            flops=num * depth * height * kids * width,
            bytes_accessed=num * depth * height + kids * height * width * 2 * (1 + len(more)),
            transcendentals=0,
        ),
        name="half_product",
    )(where, turned, *rows, *more)


def pair_kernel(keep_ref, got_ref, message_ref):
    sub, width = keep_ref.shape[2:]
    both = keep_ref[0, 0] + got_ref[0, 0]
    top = jnp.max(jnp.max(jnp.abs(both).reshape(-1, 8, width), axis=0), axis=(0, 1), keepdims=True)
    power = jnp.ceil(jnp.log2(jnp.maximum(top, 2.0**-100))) + 1.0
    message_ref[0, :sub] = both * jnp.exp2(15.0 - power)
    message_ref[0, sub:] = jnp.broadcast_to(power, (message_ref.shape[1] - sub, width))


def add_pair(keep, got):
    kids, halves, sub, width = keep.shape
    spec = pl.BlockSpec((1, 1, sub, width), lambda k, h: (k, h, 0, 0))
    return pl.pallas_call(
        pair_kernel,
        out_shape=jax.ShapeDtypeStruct((kids * halves, sub + 16, width), F32),
        grid=(kids, halves),
        in_specs=[spec, spec],
        out_specs=pl.BlockSpec((1, sub + 16, width), lambda k, h: (k * halves + h, 0, 0)),
        compiler_params=pltpu.CompilerParams(vmem_limit_bytes=16 * 2**20),
        cost_estimate=pl.CostEstimate(flops=keep.size * 4, bytes_accessed=3 * keep.nbytes, transcendentals=0),
        name="add_pair",
    )(keep, got)


def shards(ancestor_cols, factor, block_mask, diag_inverse):
    num_z = lax.axis_size("z")
    num_y = lax.axis_size("y")
    quarter = ancestor_cols.shape[2]
    height = ancestor_cols.shape[3]
    width = factor.shape[2]
    sub = factor.shape[1]
    z = lax.axis_index("z")
    core = lax.axis_index("core")
    group = (lax.axis_index("xlo") * num_z + z) * 4 + lax.axis_index("xhi") * 2 + core
    per = sub // width
    live = lax.dynamic_slice_in_dim(block_mask[0], group * per, per, 0)
    masked = (factor.reshape(per, width, width) * live[:, None, None].astype(BF16)).reshape(sub, width)
    blocks = ancestor_cols.reshape(2, num_z, quarter, height)

    order = [jnp.remainder(z + o, num_z) for o in (0, -1, 1, -2, 2, -3, 3, num_z // 2)]
    first, last, every = order[:7] + [1 - core], order[7:] + [1 - core], order + [core]
    first, last, every = (jnp.stack(w).astype(jnp.int32) for w in (first, last, every))

    pieces = jnp.broadcast_to(masked.reshape(num_y, 1, quarter, width), (num_y, 2, quarter, width))
    pieces, first, last, every = lax.optimization_barrier((pieces, first, last, every))
    own = lax.all_to_all(pieces.reshape(num_y * 2, quarter, width), ("y", "xlo"), 0, 0)
    own = own.reshape(num_y, 2 * quarter, width)

    up = [(i, (i + 1) % num_z) for i in range(num_z)]
    down = [(i, (i - 1) % num_z) for i in range(num_z)]
    below, above = lax.ppermute(own, "z", up), lax.ppermute(own, "z", down)
    below, above, turned = lax.optimization_barrier((below, above, turn(blocks)))
    below2, above2 = lax.ppermute(below, "z", up), lax.ppermute(above, "z", down)
    below3, above3 = lax.ppermute(below2, "z", up), lax.ppermute(above2, "z", down)
    far = lax.ppermute(below3, "z", up)

    near = [own, below, above, below2, above2, below3, above3]
    partial = half_product(turned, first, near)
    give = half_product(turned, last, [far], partial)
    got = lax.ppermute(give, "core", SWAP)
    keep = half_product(turned, every, near + [far])

    parts = lax.all_to_all(add_pair(keep, got).astype(F16), ("y", "xhi"), 0, 0)
    back = jnp.exp2(parts[:, sub, 0].astype(F32) - 15.0)
    total = jnp.sum(parts[:, :sub].astype(F32) * back[:, None, None], 0)
    inverse_cols = lax.optimization_barrier((-total).astype(BF16))

    product = jnp.einsum("jw,jv->wv", masked, inverse_cols, preferred_element_type=F32)
    split = product.reshape(8, width // 8, width)
    mine = jnp.sum(lax.all_to_all(split, ALONG_X, 0, 0), 0)
    over_z = jnp.sum(lax.all_to_all(jnp.broadcast_to(mine, (num_z,) + mine.shape), "z", 0, 0), 0)
    whole = lax.all_to_all(jnp.broadcast_to(over_z, (8,) + over_z.shape), ALONG_X, 0, 0)
    return inverse_cols[None], diag_inverse - whole.reshape(1, width, width)


def solution(mesh):
    fine = Mesh(mesh.devices.reshape(4, 2, 8, 2, 2), AXES)
    rows = ROW + COL
    in_specs = (P(None, COL, "y", ROW), P("y", rows, None), P("y", None), P("y", None, None))
    out_specs = (P("y", rows, None), P("y", None, None))
    return jax.shard_map(shards, mesh=fine, in_specs=in_specs, out_specs=out_specs, check_vma=False)
```

time: 266 us -> 156 us (0.59)
  matrix products: 57.3 us -> 0.23 us
  local copies, waits for them, and re-layouts: 47.5 us -> 4.02 us
  waiting for transfers between devices: 76.6 us -> 55 us
  Pallas kernels: 0 us -> 19 us
  blocking collectives: 40.2 us -> 51.4 us
  starting transfers between devices: 30.1 us -> 20.2 us
  other arithmetic: 11.9 us -> 4.98 us
    dot_general x8 -> x0, matrix products: 57.1 us -> none  [term(): jnp.einsum('xti,kxtw->kiw', cols, rows.reshape(num_y, 2, quarter, width),...]
    dynamic_slice x3 -> x0, local copies, waits for them, and re-layouts: 34 us -> none  [the longest x2 23 us: shards(): keep = lax.dynamic_index_in_dim(halves, core, 2, keepdims=False)]
    all_to_all x2 -> x1, waiting for transfers between devices: 56.4 us -> 28.3 us  [shards(): parts = lax.all_to_all(add_pair(keep, got).astype(F16), ('y', 'xhi'), 0, 0)]
    pallas_call x0 -> x5, Pallas kernels: none -> 19 us  [the longest x3 12.2 us: half_product(): pl.pallas_call(functools.partial(half_kernel, num, bool(more)), out_shape...]
    reshape x1 -> x0, local copies, waits for them, and re-layouts: 11.8 us -> none  [shards(): halves = partial.reshape(num_y, 2, 2, sub, width)]
    all_to_all x0 -> x1, blocking collectives: none -> 11.4 us  [shards(): lax.all_to_all(jnp.broadcast_to(over_z, (8,) + over_z.shape), ALONG_X, 0, 0)]
    all_to_all x2 -> x1, starting transfers between devices: 10.6 us -> 3.98 us  [shards(): parts = lax.all_to_all(add_pair(keep, got).astype(F16), ('y', 'xhi'), 0, 0)]
    ppermute x9 -> x8, waiting for transfers between devices: 20.2 us -> 26.7 us  [the longest x1 9.44 us: shards(): lax.ppermute(below, 'z', up)]
  transfers between devices with their start and end apart: 11 -> 9, of which waited for: 6 -> 6; matrix products, arithmetic and copies ran while one was open for 16% -> 0% of each run, Pallas kernels for 0% -> 10%
where the time goes in v3:
time: 156 us
  waiting for transfers between devices  55 us (35%)
  blocking collectives  51.4 us (33%)
  starting transfers between devices  20.2 us (13%)
  Pallas kernels  19 us (12%)
  other arithmetic  4.98 us (3%)
  local copies, waits for them, and re-layouts  4.02 us (3%)
    all_to_all x1, waiting for transfers between devices, shards(): parts = lax.all_to_all(add_pair(keep, got).astype(F16), ('y', 'xhi'), 0, 0)  28.3 us
    all_to_all x1, blocking collectives, shards(): lax.all_to_all(pieces.reshape(num_y * 2, quarter, width), ('y', 'xlo'), 0...  15 us
    all_to_all x1, blocking collectives, shards(): lax.all_to_all(jnp.broadcast_to(mine, (num_z,) + mine.shape), 'z', 0, 0)  14.7 us
    pallas_call x3, Pallas kernels, half_product(): pl.pallas_call(functools.partial(half_kernel, num, bool(more)), out_shape...  12.2 us
    all_to_all x1, blocking collectives, shards(): lax.all_to_all(jnp.broadcast_to(over_z, (8,) + over_z.shape), ALONG_X, 0, 0)  11.4 us
    all_to_all x1, blocking collectives, shards(): mine = jnp.sum(lax.all_to_all(split, ALONG_X, 0, 0), 0)  10.4 us
    ppermute x1, waiting for transfers between devices, shards(): lax.ppermute(below, 'z', up)  9.44 us
    ppermute x1, waiting for transfers between devices, shards(): lax.ppermute(below2, 'z', up)  8.52 us
  transfers between devices with their start and end apart: 9, of which 6 were waited for; matrix products, arithmetic and copies ran while one was open for 0% of the time, Pallas kernels for 10%

profile of v3, /device:TPU:1, one launch (start us, length us, event | category | flops | bytes accessed | tf_op | source)
XLA Modules:
  0.0 155.8 jit_solution(536984813339565279)
XLA Ops:
  0.9 0.1 stack.60.where_ref
  1.0 0.7 convert_bitcast_fusion
  1.8 0.1 mul.52
  1.9 1.0 broadcast_multiply_fusion
  3.0 15.0 %all_to_all.25 = bf16[8,128,256]{2,1,0:T(8,128)(2,1)S(1)} all-to-all(bf16[8,128,256]{2,1,0:T(8,128)(2,1)S(1)} %bitcast.37), channel_id=1, replica_groups=mesh['y'=4,'xlo'=2,'z'=8,'xhi'=2,'core'=2] {'y','xlo'}, dimensions={0} | all-to-all | bytes 1048576 | tf_op jit(solution)/shard_map/all_to_all | solution.py:137
  17.9 1.6 %collective-permute-start = (bf16[4,256,256]{2,1,0:T(8,128)(2,1)S(1)}, bf16[4,256,256]{2,1,0:T(8,128)(2,1)S(1)}, u32[]{:S(2)}, u32[]{:S(2)}) collective-permute-start(bf16[4,256,256]{2,1,0:T(8,128)(2,1)S(1)} %bitcast.33), channel_id=1, source_target_pairs={{0,4},{4,8},{8,12},{12,16},{16,20},{20,24},{24,28},{28,0},{1,5},{5... | collective-permute-start | bytes 1572872 | tf_op jit(solution)/shard_map/ppermute | solution.py:142
  19.6 3.9 %collective-permute-start.1 = (bf16[4,256,256]{2,1,0:T(8,128)(2,1)S(1)}, bf16[4,256,256]{2,1,0:T(8,128)(2,1)S(1)}, u32[]{:S(2)}, u32[]{:S(2)}) collective-permute-start(bf16[4,256,256]{2,1,0:T(8,128)(2,1)S(1)} %bitcast.34), channel_id=1, source_target_pairs={{0,28},{4,0},{8,4},{12,8},{16,12},{20,16},{24,20},{28,24},{1,29},{... | collective-permute-start | bytes 1572872 | tf_op jit(solution)/shard_map/ppermute | solution.py:142
  23.5 3.4 %copy-done = bf16[16,1,128,2048]{3,2,1,0:T(8,128)(2,1)S(1)} copy-done((bf16[16,1,128,2048]{3,2,1,0:T(8,128)(2,1)S(1)}, bf16[16,1,128,2048]{3,2,1,0:T(8,128)(2,1)}, u32[]{:S(2)}) %copy-start) | copy-done | bytes 8388632
  26.9 4.9 %turn.1.turned_ref = bf16[8,2048,256]{2,1,0:T(8,128)(2,1)S(1)} custom-call(bf16[2,8,128,2048]{3,2,1,0:T(8,128)(2,1)S(1)} %bitcast.32), custom_call_target="tpu_custom_call" | custom-call | bytes 16777216 | tf_op jit(solution)/shard_map/turn/pallas_call | solution.py:28
  31.8 2.1 %collective-permute-done.refs_1_ = bf16[4,256,256]{2,1,0:T(8,128)(2,1)S(1)} collective-permute-done((bf16[4,256,256]{2,1,0:T(8,128)(2,1)S(1)}, bf16[4,256,256]{2,1,0:T(8,128)(2,1)S(1)}, u32[]{:S(2)}, u32[]{:S(2)}) %collective-permute-start) | collective-permute-done | bytes 524320 | tf_op jit(solution)/shard_map/ppermute | solution.py:142
  33.9 2.7 %collective-permute-start.3 = (bf16[4,256,256]{2,1,0:T(8,128)(2,1)S(1)}, bf16[4,256,256]{2,1,0:T(8,128)(2,1)S(1)}, u32[]{:S(2)}, u32[]{:S(2)}) collective-permute-start(bf16[4,256,256]{2,1,0:T(8,128)(2,1)S(1)} %collective-permute-done.1.refs_2_), channel_id=1, source_target_pairs={{0,28},{4,0},{8,4},{12,8},{16,12},{20,16},{24,20},{28,24},{1,29},{... | collective-permute-start | bytes 1572872 | tf_op jit(solution)/shard_map/ppermute | solution.py:144
  36.6 9.4 %collective-permute-done.2.refs_3_ = bf16[4,256,256]{2,1,0:T(8,128)(2,1)S(1)} collective-permute-done((bf16[4,256,256]{2,1,0:T(8,128)(2,1)S(1)}, bf16[4,256,256]{2,1,0:T(8,128)(2,1)S(1)}, u32[]{:S(2)}, u32[]{:S(2)}) %collective-permute-start.2) | collective-permute-done | bytes 524320 | tf_op jit(solution)/shard_map/ppermute | solution.py:144
  46.0 2.7 %collective-permute-start.5 = (bf16[4,256,256]{2,1,0:T(8,128)(2,1)S(1)}, bf16[4,256,256]{2,1,0:T(8,128)(2,1)S(1)}, u32[]{:S(2)}, u32[]{:S(2)}) collective-permute-start(bf16[4,256,256]{2,1,0:T(8,128)(2,1)S(1)} %collective-permute-done.3.refs_4_), channel_id=1, source_target_pairs={{0,28},{4,0},{8,4},{12,8},{16,12},{20,16},{24,20},{28,24},{1,29},{... | collective-permute-start | bytes 1572872 | tf_op jit(solution)/shard_map/ppermute | solution.py:145
  48.7 8.5 %collective-permute-done.4.refs_5_ = bf16[4,256,256]{2,1,0:T(8,128)(2,1)S(1)} collective-permute-done((bf16[4,256,256]{2,1,0:T(8,128)(2,1)S(1)}, bf16[4,256,256]{2,1,0:T(8,128)(2,1)S(1)}, u32[]{:S(2)}, u32[]{:S(2)}) %collective-permute-start.4) | collective-permute-done | bytes 524320 | tf_op jit(solution)/shard_map/ppermute | solution.py:145
  57.2 5.0 %half_product.4.refs_1_ = f32[4,2,512,256]{3,2,1,0:T(8,128)S(1)} custom-call(s32[8]{0:T(128)S(1)} %stack.56.where_ref, bf16[8,2048,256]{2,1,0:T(8,128)(2,1)S(1)} %turn.1.turned_ref, bf16[4,256,256]{2,1,0:T(8,128)(2,1)S(1)} %bitcast.35, bf16[4,256,256]{2,1,0:T(8,128)(2,1)S(1)} %collective-permute-done.refs_1_, ...), custom_call_target="tpu_custom_call" | custom-call | flops 3758096384 | bytes 7864320 | tf_op jit(solution)/shard_map/half_product/pallas_call | solution.py:71
  62.2 5.4 %collective-permute-done.6.refs_7_.refs_0_ = bf16[4,256,256]{2,1,0:T(8,128)(2,1)S(1)} collective-permute-done((bf16[4,256,256]{2,1,0:T(8,128)(2,1)S(1)}, bf16[4,256,256]{2,1,0:T(8,128)(2,1)S(1)}, u32[]{:S(2)}, u32[]{:S(2)}) %collective-permute-start.6) | collective-permute-done | bytes 524320 | tf_op jit(solution)/shard_map/ppermute | solution.py:146
  67.5 1.7 %half_product.5 = f32[4,2,512,256]{3,2,1,0:T(8,128)S(1)} custom-call(s32[2]{0:T(128)S(1)} %pad_add_fusion.where_ref, bf16[8,2048,256]{2,1,0:T(8,128)(2,1)S(1)} %turn.1.turned_ref, bf16[4,256,256]{2,1,0:T(8,128)(2,1)S(1)} %collective-permute-done.6.refs_7_.refs_0_, f32[4,2,512,256]{3,2,1,0:T(8,128)S(1)} %half_product.4.refs_1_), custom_call_target="tpu_custom_call", output_to_operand_aliasing={{}: (3, {})} | custom-call | flops 536870912 | bytes 8912896 | tf_op jit(solution)/shard_map/half_product/pallas_call | solution.py:71
  69.3 5.3 %collective-permute-start.7 = (f32[4,2,512,256]{3,2,1,0:T(8,128)S(1)}, f32[4,2,512,256]{3,2,1,0:T(8,128)S(1)}, u32[]{:S(2)}, u32[]{:S(2)}) collective-permute-start(f32[4,2,512,256]{3,2,1,0:T(8,128)S(1)} %half_product.5), channel_id=1, source_target_pairs={{0,1},{1,0},{2,3},{3,2},{4,5},{5,4},{6,7},{7,6},{8,9},{9,8},{10,11... | collective-permute-start | bytes 12582920 | tf_op jit(solution)/shard_map/ppermute | solution.py:151
  74.6 5.5 %half_product.3.keep_ref = f32[4,2,512,256]{3,2,1,0:T(8,128)S(1)} custom-call(s32[9]{0:T(128)S(1)} %stack.60.where_ref, bf16[8,2048,256]{2,1,0:T(8,128)(2,1)S(1)} %turn.1.turned_ref, bf16[4,256,256]{2,1,0:T(8,128)(2,1)S(1)} %bitcast.36, bf16[4,256,256]{2,1,0:T(8,128)(2,1)S(1)} %collective-permute-done.refs_1_, ...), custom_call_target="tpu_custom_call" | custom-call | flops 4294967296 | bytes 8388608 | tf_op jit(solution)/shard_map/half_product/pallas_call | solution.py:71
  80.1 1.3 collective-permute-done.7.got_ref
  81.4 1.9 %add_pair.1 = f32[8,528,256]{2,1,0:T(8,128)S(1)} custom-call(f32[4,2,512,256]{3,2,1,0:T(8,128)S(1)} %half_product.3.keep_ref, f32[4,2,512,256]{3,2,1,0:T(8,128)S(1)} %collective-permute-done.7.got_ref), custom_call_target="tpu_custom_call" | custom-call | flops 4194304 | bytes 12582912 | tf_op jit(solution)/shard_map/add_pair/pallas_call | solution.py:104
  83.3 1.6 %convert_element_type.26 = f16[8,528,256]{2,1,0:T(8,128)(2,1)} convert(f32[8,528,256]{2,1,0:T(8,128)S(1)} %add_pair.1) | non-fusion elementwise | flops 1081344 | bytes 6488064 | tf_op jit(solution)/shard_map/convert_element_type | solution.py:154
  85.0 4.0 %all-to-all-start.1 = ((f16[8,528,256]{2,1,0:T(8,128)(2,1)}), f16[8,528,256]{2,1,0:T(8,128)(2,1)S(1)}, u32[]{:S(2)}, u32[]{:S(2)}) async-start(f16[8,528,256]{2,1,0:T(8,128)(2,1)} %convert_element_type.26), calls=%async_computation.1 | async-start | bytes 4325376 | tf_op jit(solution)/shard_map/all_to_all | solution.py:154
  89.0 0.1 copy.10
  89.2 28.3 %all-to-all-done.1 = f16[8,528,256]{2,1,0:T(8,128)(2,1)S(1)} async-done(((f16[8,528,256]{2,1,0:T(8,128)(2,1)}), f16[8,528,256]{2,1,0:T(8,128)(2,1)S(1)}, u32[]{:S(2)}, u32[]{:S(2)}) %all-to-all-start.1) | async-done | bytes 2162720 | tf_op jit(solution)/shard_map/all_to_all | solution.py:154
  117.5 0.2 fusion.5
  117.7 0.5 multiply_reduce_fusion
  118.3 0.2 fusion
  118.5 10.4 %all_to_all.26 = f32[8,32,256]{2,1,0:T(8,128)S(1)} all-to-all(f32[8,32,256]{2,1,0:T(8,128)S(1)} %fusion), channel_id=1, replica_groups=mesh['y'=4,'xlo'=2,'z'=8,'xhi'=2,'core'=2] {'xlo','xhi','core'}, dimensions={0} | all-to-all | bytes 524288 | tf_op jit(solution)/shard_map/all_to_all | solution.py:161
  128.9 14.7 %all_to_all.27 = f32[8,32,256]{2,1,0:T(8,128)S(1)} all-to-all(f32[8,32,256]{2,1,0:T(8,128)S(1)} %broadcast_in_dim.18), channel_id=1, replica_groups=mesh['y'=4,'xlo'=2,'z'=8,'xhi'=2,'core'=2] {'z'}, dimensions={0} | all-to-all | bytes 524288 | tf_op jit(solution)/shard_map/all_to_all | solution.py:162
  143.7 11.4 %all_to_all.28 = f32[8,32,256]{2,1,0:T(8,128)S(1)} all-to-all(f32[8,32,256]{2,1,0:T(8,128)S(1)} %broadcast_in_dim.19), channel_id=1, replica_groups=mesh['y'=4,'xlo'=2,'z'=8,'xhi'=2,'core'=2] {'xlo','xhi','core'}, dimensions={0} | all-to-all | bytes 524288 | tf_op jit(solution)/shard_map/all_to_all | solution.py:163
  155.1 0.7 bitcast_subtract_fusion
  (25 shorter events, 0.5 us)
Async XLA Ops:
  17.9 15.9 %collective-permute-start = (bf16[4,256,256]{2,1,0:T(8,128)(2,1)S(1)}, bf16[4,256,256]{2,1,0:T(8,128)(2,1)S(1)}, u32[]{:S(2)}, u32[]{:S(2)}) collective-permute-start(bf16[4,256,256]{2,1,0:T(8,128)(2,1)S(1)} %bitcast.33), channel_id=1, source_target_pairs={{0,4},{4,8},{8,12},{12,16},{16,20},{20,24},{24,28},{28,0},{1,5},{5... | collective-permute-start | bytes 1572872 | tf_op jit(solution)/shard_map/ppermute | solution.py:142
  19.6 14.3 %collective-permute-start.1 = (bf16[4,256,256]{2,1,0:T(8,128)(2,1)S(1)}, bf16[4,256,256]{2,1,0:T(8,128)(2,1)S(1)}, u32[]{:S(2)}, u32[]{:S(2)}) collective-permute-start(bf16[4,256,256]{2,1,0:T(8,128)(2,1)S(1)} %bitcast.34), channel_id=1, source_target_pairs={{0,28},{4,0},{8,4},{12,8},{16,12},{20,16},{24,20},{28,24},{1,29},{... | collective-permute-start | bytes 1572872 | tf_op jit(solution)/shard_map/ppermute | solution.py:142
  23.5 3.4 %copy-start = (bf16[16,1,128,2048]{3,2,1,0:T(8,128)(2,1)S(1)}, bf16[16,1,128,2048]{3,2,1,0:T(8,128)(2,1)}, u32[]{:S(2)}) copy-start(bf16[16,1,128,2048]{3,2,1,0:T(8,128)(2,1)} %param.4) | copy-start | bytes 25165828
  33.9 12.1 %collective-permute-start.2 = (bf16[4,256,256]{2,1,0:T(8,128)(2,1)S(1)}, bf16[4,256,256]{2,1,0:T(8,128)(2,1)S(1)}, u32[]{:S(2)}, u32[]{:S(2)}) collective-permute-start(bf16[4,256,256]{2,1,0:T(8,128)(2,1)S(1)} %collective-permute-done.refs_1_), channel_id=1, source_target_pairs={{0,4},{4,8},{8,12},{12,16},{16,20},{20,24},{24,28},{28,0},{1,5},{5... | collective-permute-start | bytes 1572872 | tf_op jit(solution)/shard_map/ppermute | solution.py:144
  33.9 12.1 %collective-permute-start.3 = (bf16[4,256,256]{2,1,0:T(8,128)(2,1)S(1)}, bf16[4,256,256]{2,1,0:T(8,128)(2,1)S(1)}, u32[]{:S(2)}, u32[]{:S(2)}) collective-permute-start(bf16[4,256,256]{2,1,0:T(8,128)(2,1)S(1)} %collective-permute-done.1.refs_2_), channel_id=1, source_target_pairs={{0,28},{4,0},{8,4},{12,8},{16,12},{20,16},{24,20},{28,24},{1,29},{... | collective-permute-start | bytes 1572872 | tf_op jit(solution)/shard_map/ppermute | solution.py:144
  46.0 11.2 %collective-permute-start.4 = (bf16[4,256,256]{2,1,0:T(8,128)(2,1)S(1)}, bf16[4,256,256]{2,1,0:T(8,128)(2,1)S(1)}, u32[]{:S(2)}, u32[]{:S(2)}) collective-permute-start(bf16[4,256,256]{2,1,0:T(8,128)(2,1)S(1)} %collective-permute-done.2.refs_3_), channel_id=1, source_target_pairs={{0,4},{4,8},{8,12},{12,16},{16,20},{20,24},{24,28},{28,0},{1,5},{5... | collective-permute-start | bytes 1572872 | tf_op jit(solution)/shard_map/ppermute | solution.py:145
  46.0 11.2 %collective-permute-start.5 = (bf16[4,256,256]{2,1,0:T(8,128)(2,1)S(1)}, bf16[4,256,256]{2,1,0:T(8,128)(2,1)S(1)}, u32[]{:S(2)}, u32[]{:S(2)}) collective-permute-start(bf16[4,256,256]{2,1,0:T(8,128)(2,1)S(1)} %collective-permute-done.3.refs_4_), channel_id=1, source_target_pairs={{0,28},{4,0},{8,4},{12,8},{16,12},{20,16},{24,20},{28,24},{1,29},{... | collective-permute-start | bytes 1572872 | tf_op jit(solution)/shard_map/ppermute | solution.py:145
  57.2 10.3 %collective-permute-start.6 = (bf16[4,256,256]{2,1,0:T(8,128)(2,1)S(1)}, bf16[4,256,256]{2,1,0:T(8,128)(2,1)S(1)}, u32[]{:S(2)}, u32[]{:S(2)}) collective-permute-start(bf16[4,256,256]{2,1,0:T(8,128)(2,1)S(1)} %collective-permute-done.4.refs_5_), channel_id=1, source_target_pairs={{0,4},{4,8},{8,12},{12,16},{16,20},{20,24},{24,28},{28,0},{1,5},{5... | collective-permute-start | bytes 1572872 | tf_op jit(solution)/shard_map/ppermute | solution.py:146
  69.3 12.1 %collective-permute-start.7 = (f32[4,2,512,256]{3,2,1,0:T(8,128)S(1)}, f32[4,2,512,256]{3,2,1,0:T(8,128)S(1)}, u32[]{:S(2)}, u32[]{:S(2)}) collective-permute-start(f32[4,2,512,256]{3,2,1,0:T(8,128)S(1)} %half_product.5), channel_id=1, source_target_pairs={{0,1},{1,0},{2,3},{3,2},{4,5},{5,4},{6,7},{7,6},{8,9},{9,8},{10,11... | collective-permute-start | bytes 12582920 | tf_op jit(solution)/shard_map/ppermute | solution.py:151
  83.3 5.6 %copy-start.2 = (bf16[1,512,256]{2,1,0:T(8,128)(2,1)S(1)}, bf16[1,512,256]{2,1,0:T(8,128)(2,1)}, u32[]{:S(2)}) copy-start(bf16[1,512,256]{2,1,0:T(8,128)(2,1)} %param.5) | copy-start | bytes 786436
  85.0 32.6 %all-to-all-start.1 = ((f16[8,528,256]{2,1,0:T(8,128)(2,1)}), f16[8,528,256]{2,1,0:T(8,128)(2,1)S(1)}, u32[]{:S(2)}, u32[]{:S(2)}) async-start(f16[8,528,256]{2,1,0:T(8,128)(2,1)} %convert_element_type.26), calls=%async_computation.1 | async-start | bytes 4325376 | tf_op jit(solution)/shard_map/all_to_all | solution.py:154
  89.0 66.1 %copy-start.3 = (f32[1,256,256]{2,1,0:T(8,128)S(1)}, f32[1,256,256]{2,1,0:T(8,128)}, u32[]{:S(2)}) copy-start(f32[1,256,256]{2,1,0:T(8,128)} %param.7) | copy-start | bytes 786436
  118.2 37.6 %copy-start.1 = (bf16[512,256]{1,0:T(8,128)(2,1)}, bf16[512,256]{1,0:T(8,128)(2,1)S(1)}, u32[]{:S(2)}) copy-start(bf16[512,256]{1,0:T(8,128)(2,1)S(1)} %negate_convert_fusion) | copy-start | bytes 786436

commit v4 on v3

v4 whole, which is shorter than its diff:
```python
import functools

import jax
import jax.numpy as jnp
from jax import lax
from jax.experimental import pallas as pl
from jax.experimental.pallas import tpu as pltpu
from jax.sharding import Mesh, PartitionSpec as P

AXES = ("y", "xlo", "z", "xhi", "core")
ROW = ("xlo", "z")
COL = ("xhi", "core")
ALONG_X = ("xlo", "xhi", "core")
F32 = jnp.float32
F16 = jnp.float16
BF16 = jnp.bfloat16
SWAP = [(0, 1), (1, 0)]
def mask_kernel(place_ref, mask_ref, factor_ref, pieces_ref, masked_ref):
    pair, quarter = pieces_ref.shape[1:3]
    width = factor_ref.shape[2]
    for k in range(pieces_ref.shape[0]):
        block = place_ref[0] + k * quarter // width
        part = factor_ref[0, k * quarter : (k + 1) * quarter]
        part = jnp.where(mask_ref[0, block] != 0, part, jnp.zeros_like(part))
        masked_ref[k * quarter : (k + 1) * quarter] = part
        for x in range(pair):
            pieces_ref[k, x] = part


def mask(place, block_mask, factor, quarter):
    _, sub, width = factor.shape
    return pl.pallas_call(
        mask_kernel,
        out_shape=(
            jax.ShapeDtypeStruct((sub // quarter, 2, quarter, width), BF16),
            jax.ShapeDtypeStruct((sub, width), BF16),
        ),
        in_specs=[pl.BlockSpec(memory_space=pltpu.SMEM)] * 2 + [pl.BlockSpec(memory_space=pltpu.VMEM)],
        out_specs=tuple([pl.BlockSpec(memory_space=pltpu.VMEM)] * 2),
        cost_estimate=pl.CostEstimate(flops=factor.size, bytes_accessed=4 * factor.nbytes, transcendentals=0),
        name="mask",
    )(place, block_mask, factor)


def turn_kernel(cols_ref, out_ref):
    out_ref[0] = cols_ref[...].reshape(-1, cols_ref.shape[-1]).T


def turn(blocks):
    pair, num, quarter, height = blocks.shape
    tile = 512
    return pl.pallas_call(
        turn_kernel,
        out_shape=jax.ShapeDtypeStruct((num, height, pair * quarter), BF16),
        grid=(num, height // tile),
        in_specs=[pl.BlockSpec((pair, 1, quarter, tile), lambda z, i: (0, z, 0, i))],
        out_specs=pl.BlockSpec((1, tile, pair * quarter), lambda z, i: (z, i, 0)),
        compiler_params=pltpu.CompilerParams(vmem_limit_bytes=16 * 2**20),
        cost_estimate=pl.CostEstimate(flops=0, bytes_accessed=2 * blocks.nbytes, transcendentals=0),
        name="turn",
    )(blocks)


def rows_of(where_ref, half, sub):
    return pl.ds(pl.multiple_of((2 * half + where_ref[where_ref.shape[0] - 1]) * sub, sub), sub)


def pick_kernel(where_ref, turned_ref, out_ref):
    for b in range(out_ref.shape[0]):
        for h in range(2):
            out_ref[b, h] = turned_ref[where_ref[b], rows_of(where_ref, h, out_ref.shape[2])]


def pick(turned, where):
    _, height, depth = turned.shape
    num = where.shape[0] - 1
    return pl.pallas_call(
        pick_kernel,
        out_shape=jax.ShapeDtypeStruct((num, 2, height // 4, depth), BF16),
        in_specs=[pl.BlockSpec(memory_space=pltpu.SMEM), pl.BlockSpec(memory_space=pltpu.VMEM)],
        out_specs=pl.BlockSpec(memory_space=pltpu.VMEM),
        compiler_params=pltpu.CompilerParams(vmem_limit_bytes=16 * 2**20),
        cost_estimate=pl.CostEstimate(flops=0, bytes_accessed=2 * num * height * depth, transcendentals=0),
        name="pick",
    )(where, turned)


def half_kernel(num, spare, more, where_ref, turned_ref, *refs):
    rows, out_ref = refs[: num + len(spare)], refs[-1]
    parts_ref = refs[num + len(spare)] if spare else None
    kids, _, sub, _ = out_ref.shape
    for h in range(2):
        here = rows_of(where_ref, h, sub)
        cols = [turned_ref[where_ref[b], here] for b in range(num)] + [parts_ref[p, h] for p in spare]
        cols = jnp.concatenate(cols, 1)
        for k in range(kids):
            value = jnp.dot(cols, jnp.concatenate([r[k] for r in rows], 0), preferred_element_type=F32)
            out_ref[k, h] = refs[-2][k, h] + value if more else value


def half_product(turned, where, rows, partial=None, parts=None, spare=(), others=(), weight=1):
    num = len(rows)
    _, height, depth = turned.shape
    kids, _, width = rows[0].shape
    more = [] if partial is None else [partial]
    extra = [parts] if spare else []
    arrays = [turned, *rows, *others, *extra, *more]
    return pl.pallas_call(
        functools.partial(half_kernel, num, spare, bool(more)),
        out_shape=jax.ShapeDtypeStruct((kids, 2, height // 4, width), F32),
        in_specs=[pl.BlockSpec(memory_space=pltpu.SMEM)] + [pl.BlockSpec(memory_space=pltpu.VMEM)] * len(arrays),
        out_specs=pl.BlockSpec(memory_space=pltpu.VMEM),
        input_output_aliases={len(arrays): 0} if more else {},
        compiler_params=pltpu.CompilerParams(vmem_limit_bytes=16 * 2**20),
        cost_estimate=pl.CostEstimate(
            flops=weight * (num + len(spare)) * depth * height * kids * width,
            bytes_accessed=weight * num * depth * height,
            transcendentals=0,
        ),
        name="half_product",
    )(where, *arrays)


def pair_kernel(keep_ref, got_ref, parts_ref, rows_ref, message_ref):
    kids, halves, sub, width = keep_ref.shape
    last = parts_ref.shape[0] - 1
    for h in range(halves):
        for k in range(kids):
            both = jnp.dot(parts_ref[last, h], rows_ref[k], preferred_element_type=F32)
            both = both + (keep_ref[k, h] + got_ref[k, h])
            top = jnp.max(jnp.max(jnp.abs(both).reshape(-1, 8, width), axis=0), axis=(0, 1), keepdims=True)
            power = jnp.ceil(jnp.log2(jnp.maximum(top, 2.0**-100))) + 1.0
            message_ref[h * kids + k, :sub] = both * jnp.exp2(15.0 - power)
            message_ref[h * kids + k, sub:] = jnp.broadcast_to(power, (message_ref.shape[1] - sub, width))


def add_pair(keep, got, parts, rows):
    kids, halves, sub, width = keep.shape
    return pl.pallas_call(
        pair_kernel,
        out_shape=jax.ShapeDtypeStruct((kids * halves, sub + 16, width), F32),
        in_specs=[pl.BlockSpec(memory_space=pltpu.VMEM)] * 4,
        out_specs=pl.BlockSpec(memory_space=pltpu.VMEM),
        compiler_params=pltpu.CompilerParams(vmem_limit_bytes=16 * 2**20),
        cost_estimate=pl.CostEstimate(
            flops=2 * keep.size * parts.shape[3], bytes_accessed=3 * keep.nbytes, transcendentals=0
        ),
        name="add_pair",
    )(keep, got, parts, rows)


def shards(ancestor_cols, factor, block_mask, diag_inverse):
    num_z = lax.axis_size("z")
    num_y = lax.axis_size("y")
    quarter = ancestor_cols.shape[2]
    height = ancestor_cols.shape[3]
    width = factor.shape[2]
    sub = factor.shape[1]
    z = lax.axis_index("z")
    core = lax.axis_index("core")
    group = (lax.axis_index("xlo") * num_z + z) * 4 + lax.axis_index("xhi") * 2 + core
    blocks = ancestor_cols.reshape(2, num_z, quarter, height)

    order = [jnp.remainder(z + o, num_z) for o in (0, -1, 1, -2, 2, -3, 3, num_z // 2)]
    mine, theirs = [core], [1 - core]
    lists = [[group * (sub // width)], order[:7] + theirs, order[7:] + theirs, order + mine]
    places = jnp.stack(sum(lists, [])).astype(jnp.int32)
    ends = [sum(len(a) for a in lists[:n]) for n in range(len(lists) + 1)]
    place, first, given, every = (places[a:b] for a, b in zip(ends, ends[1:]))

    pieces, masked = mask(place, block_mask, factor, quarter)
    pieces, first, given, every = lax.optimization_barrier((pieces, first, given, every))
    own = lax.all_to_all(pieces.reshape(num_y * 2, quarter, width), ("y", "xlo"), 0, 0)
    own = own.reshape(num_y, 2 * quarter, width)

    up = [(i, (i + 1) % num_z) for i in range(num_z)]
    down = [(i, (i - 1) % num_z) for i in range(num_z)]
    below, above = lax.ppermute(own, "z", up), lax.ppermute(own, "z", down)
    below, turned = lax.optimization_barrier((below, turn(blocks)))
    below2, above2 = lax.ppermute(below, "z", up), lax.ppermute(above, "z", down)
    parts = lax.ppermute(pick(turned, given), "core", SWAP)
    below3, above3 = lax.ppermute(below2, "z", up), lax.ppermute(above2, "z", down)
    below3, parts = lax.optimization_barrier((below3, parts))
    far = lax.ppermute(below3, "z", up)

    near = [own, below, above, below2, above2, below3, above3]
    give = half_product(turned, first, near, weight=1)
    got = lax.ppermute(give, "core", SWAP)
    far_other = lax.ppermute(far, "core", SWAP)
    keep = half_product(turned, every, near + [far], weight=20)

    parts = lax.all_to_all(add_pair(keep, got, parts, far_other).astype(F16), ("xhi", "y"), 0, 0)
    back = jnp.exp2(parts[:, sub, 0].astype(F32) - 15.0)
    total = jnp.sum(parts[:, :sub].astype(F32) * back[:, None, None], 0)
    inverse_cols = lax.optimization_barrier((-total).astype(BF16))

    product = jnp.einsum("jw,jv->wv", masked, inverse_cols, preferred_element_type=F32)
    split = product.reshape(8, width // 8, width)
    mine = jnp.sum(lax.all_to_all(split, ALONG_X, 0, 0), 0)
    over_z = jnp.sum(lax.all_to_all(jnp.broadcast_to(mine, (num_z,) + mine.shape), "z", 0, 0), 0)
    whole = lax.all_to_all(jnp.broadcast_to(over_z, (8,) + over_z.shape), ALONG_X, 0, 0)
    return inverse_cols[None], diag_inverse - whole.reshape(1, width, width)


def solution(mesh):
    fine = Mesh(mesh.devices.reshape(4, 2, 8, 2, 2), AXES)
    rows = ROW + COL
    in_specs = (P(None, COL, "y", ROW), P("y", rows, None), P("y", None), P("y", None, None))
    out_specs = (P("y", rows, None), P("y", None, None))
    return jax.shard_map(shards, mesh=fine, in_specs=in_specs, out_specs=out_specs, check_vma=False)
```

time: 156 us -> 151 us (0.968)
  waiting for transfers between devices: 55 us -> 17.8 us
  blocking collectives: 51.4 us -> 84.2 us
  starting transfers between devices: 20.2 us -> 23.8 us
  other arithmetic: 4.98 us -> 1.82 us
    all_to_all x0 -> x1, blocking collectives: none -> 32.7 us  [shards(): lax.all_to_all(add_pair(keep, got, parts, far_other).astype(F16), ('xhi',...]
    all_to_all x1 -> x0, waiting for transfers between devices: 28.3 us -> none  [shards(): parts = lax.all_to_all(add_pair(keep, got).astype(F16), ('y', 'xhi'), 0, 0)]
    ppermute x0 -> x2, starting transfers between devices: none -> 8.39 us  [the longest x1 5.24 us: shards(): far_other = lax.ppermute(far, 'core', SWAP)]
    all_to_all x1 -> x0, starting transfers between devices: 3.98 us -> none  [shards(): parts = lax.all_to_all(add_pair(keep, got).astype(F16), ('y', 'xhi'), 0, 0)]
    ppermute x1, waiting for transfers between devices: 5.36 us -> 1.41 us  [shards(): far = lax.ppermute(below3, 'z', up)]
    ppermute x1, waiting for transfers between devices: 9.44 us -> 5.7 us  [shards(): lax.ppermute(below, 'z', up)]
    convert_element_type x2 -> x1, other arithmetic: 2.38 us -> 0.28 us  [shards(): add_pair(keep, got, parts, far_other).astype(F16)]
    unnamed x11 -> x8, local copies, waits for them, and re-layouts: 3.62 us -> 3.4 us
  transfers between devices with their start and end apart: 9 -> 10, of which waited for: 6 -> 4; matrix products, arithmetic and copies ran while one was open for 0% -> 0% of each run, Pallas kernels for 10% -> 10%
where the time goes in v4:
time: 151 us
  blocking collectives  84.2 us (56%)
  starting transfers between devices  23.8 us (16%)
  Pallas kernels  18.4 us (12%)
  waiting for transfers between devices  17.8 us (12%)
  local copies, waits for them, and re-layouts  3.6 us (2%)
  other arithmetic  1.82 us (1%)
    all_to_all x1, blocking collectives, shards(): lax.all_to_all(add_pair(keep, got, parts, far_other).astype(F16), ('xhi',...  32.7 us
    all_to_all x1, blocking collectives, shards(): lax.all_to_all(pieces.reshape(num_y * 2, quarter, width), ('y', 'xlo'), 0...  15.2 us
    all_to_all x1, blocking collectives, shards(): lax.all_to_all(jnp.broadcast_to(mine, (num_z,) + mine.shape), 'z', 0, 0)  14.7 us
    all_to_all x1, blocking collectives, shards(): lax.all_to_all(jnp.broadcast_to(over_z, (8,) + over_z.shape), ALONG_X, 0, 0)  11.4 us
    all_to_all x1, blocking collectives, shards(): mine = jnp.sum(lax.all_to_all(split, ALONG_X, 0, 0), 0)  10.2 us
    pallas_call x2, Pallas kernels, half_product(): pl.pallas_call(functools.partial(half_kernel, num, spare, bool(more)), ou...  9.52 us
    ppermute x1, waiting for transfers between devices, shards(): lax.ppermute(below2, 'z', up)  8.51 us
    ppermute x1, waiting for transfers between devices, shards(): lax.ppermute(below, 'z', up)  5.7 us
  transfers between devices with their start and end apart: 10, of which 4 were waited for; matrix products, arithmetic and copies ran while one was open for 0% of the time, Pallas kernels for 10%

profile of v4, /device:TPU:1, one launch (start us, length us, event | category | flops | bytes accessed | tf_op | source)
XLA Modules:
  0.0 150.7 jit_solution(13128553415428544425)
XLA Ops:
  0.7 0.1 pad_add_fusion.where_ref
  0.8 0.1 stack.59.where_ref
  0.9 0.1 stack.63.where_ref
  1.0 1.9 %mask.1 = (bf16[4,2,128,256]{3,2,1,0:T(8,128)(2,1)}, bf16[512,256]{1,0:T(8,128)(2,1)}) custom-call(s32[1]{0:T(128)} %bitcast.place_ref, s32[1,128]{1,0:T(1,128)} %mask_ref.1, bf16[1,512,256]{2,1,0:T(8,128)(2,1)} %factor_ref.1), custom_call_target="tpu_custom_call" | custom-call | flops 131072 | bytes 1048576 | tf_op jit(solution)/shard_map/mask/pallas_call | solution.py:32
  2.9 15.2 %all_to_all.25 = bf16[8,128,256]{2,1,0:T(8,128)(2,1)S(1)} all-to-all(bf16[8,128,256]{2,1,0:T(8,128)(2,1)} %bitcast.29), channel_id=1, replica_groups=mesh['y'=4,'xlo'=2,'z'=8,'xhi'=2,'core'=2] {'y','xlo'}, dimensions={0} | all-to-all | bytes 1048576 | tf_op jit(solution)/shard_map/all_to_all | solution.py:173
  18.0 1.6 %collective-permute-start = (bf16[4,256,256]{2,1,0:T(8,128)(2,1)S(1)}, bf16[4,256,256]{2,1,0:T(8,128)(2,1)S(1)}, u32[]{:S(2)}, u32[]{:S(2)}) collective-permute-start(bf16[4,256,256]{2,1,0:T(8,128)(2,1)S(1)} %bitcast.22), channel_id=1, source_target_pairs={{0,4},{4,8},{8,12},{12,16},{16,20},{20,24},{24,28},{28,0},{1,5},{5... | collective-permute-start | bytes 1572872 | tf_op jit(solution)/shard_map/ppermute | solution.py:178
  19.7 3.9 %collective-permute-start.1 = (bf16[4,256,256]{2,1,0:T(8,128)(2,1)S(1)}, bf16[4,256,256]{2,1,0:T(8,128)(2,1)S(1)}, u32[]{:S(2)}, u32[]{:S(2)}) collective-permute-start(bf16[4,256,256]{2,1,0:T(8,128)(2,1)S(1)} %bitcast.23), channel_id=1, source_target_pairs={{0,28},{4,0},{8,4},{12,8},{16,12},{20,16},{24,20},{28,24},{1,29},{... | collective-permute-start | bytes 1572872 | tf_op jit(solution)/shard_map/ppermute | solution.py:178
  23.6 3.4 %copy-done = bf16[16,1,128,2048]{3,2,1,0:T(8,128)(2,1)S(1)} copy-done((bf16[16,1,128,2048]{3,2,1,0:T(8,128)(2,1)S(1)}, bf16[16,1,128,2048]{3,2,1,0:T(8,128)(2,1)}, u32[]{:S(2)}) %copy-start) | copy-done | bytes 8388632
  27.0 4.9 %turn.1.turned_ref = bf16[8,2048,256]{2,1,0:T(8,128)(2,1)S(1)} custom-call(bf16[2,8,128,2048]{3,2,1,0:T(8,128)(2,1)S(1)} %bitcast.21), custom_call_target="tpu_custom_call" | custom-call | bytes 16777216 | tf_op jit(solution)/shard_map/turn/pallas_call | solution.py:52
  31.9 2.1 %collective-permute-done.refs_1_ = bf16[4,256,256]{2,1,0:T(8,128)(2,1)S(1)} collective-permute-done((bf16[4,256,256]{2,1,0:T(8,128)(2,1)S(1)}, bf16[4,256,256]{2,1,0:T(8,128)(2,1)S(1)}, u32[]{:S(2)}, u32[]{:S(2)}) %collective-permute-start) | collective-permute-done | bytes 524320 | tf_op jit(solution)/shard_map/ppermute | solution.py:178
  34.0 2.7 %collective-permute-start.3 = (bf16[4,256,256]{2,1,0:T(8,128)(2,1)S(1)}, bf16[4,256,256]{2,1,0:T(8,128)(2,1)S(1)}, u32[]{:S(2)}, u32[]{:S(2)}) collective-permute-start(bf16[4,256,256]{2,1,0:T(8,128)(2,1)S(1)} %collective-permute-done.1.refs_2_), channel_id=1, source_target_pairs={{0,28},{4,0},{8,4},{12,8},{16,12},{20,16},{24,20},{28,24},{1,29},{... | collective-permute-start | bytes 1572872 | tf_op jit(solution)/shard_map/ppermute | solution.py:180
  36.7 0.6 pick.1
  37.3 3.2 %collective-permute-start.5 = (bf16[1,2,512,256]{3,2,1,0:T(8,128)(2,1)S(1)}, bf16[1,2,512,256]{3,2,1,0:T(8,128)(2,1)S(1)}, u32[]{:S(2)}, u32[]{:S(2)}) collective-permute-start(bf16[1,2,512,256]{3,2,1,0:T(8,128)(2,1)S(1)} %pick.1), channel_id=1, source_target_pairs={{0,1},{1,0},{2,3},{3,2},{4,5},{5,4},{6,7},{7,6},{8,9},{9,8},{10,11... | collective-permute-start | bytes 1572872 | tf_op jit(solution)/shard_map/ppermute | solution.py:181
  40.4 5.7 %collective-permute-done.2.refs_3_ = bf16[4,256,256]{2,1,0:T(8,128)(2,1)S(1)} collective-permute-done((bf16[4,256,256]{2,1,0:T(8,128)(2,1)S(1)}, bf16[4,256,256]{2,1,0:T(8,128)(2,1)S(1)}, u32[]{:S(2)}, u32[]{:S(2)}) %collective-permute-start.2) | collective-permute-done | bytes 524320 | tf_op jit(solution)/shard_map/ppermute | solution.py:180
  46.1 2.7 %collective-permute-start.6 = (bf16[4,256,256]{2,1,0:T(8,128)(2,1)S(1)}, bf16[4,256,256]{2,1,0:T(8,128)(2,1)S(1)}, u32[]{:S(2)}, u32[]{:S(2)}) collective-permute-start(bf16[4,256,256]{2,1,0:T(8,128)(2,1)S(1)} %collective-permute-done.3.refs_4_), channel_id=1, source_target_pairs={{0,28},{4,0},{8,4},{12,8},{16,12},{20,16},{24,20},{28,24},{1,29},{... | collective-permute-start | bytes 1572872 | tf_op jit(solution)/shard_map/ppermute | solution.py:182
  48.8 8.5 %collective-permute-done.4.refs_5_ = bf16[4,256,256]{2,1,0:T(8,128)(2,1)S(1)} collective-permute-done((bf16[4,256,256]{2,1,0:T(8,128)(2,1)S(1)}, bf16[4,256,256]{2,1,0:T(8,128)(2,1)S(1)}, u32[]{:S(2)}, u32[]{:S(2)}) %collective-permute-start.4) | collective-permute-done | bytes 524320 | tf_op jit(solution)/shard_map/ppermute | solution.py:182
  57.3 4.5 %half_product.3 = f32[4,2,512,256]{3,2,1,0:T(8,128)S(1)} custom-call(s32[8]{0:T(128)S(1)} %stack.59.where_ref, bf16[8,2048,256]{2,1,0:T(8,128)(2,1)S(1)} %turn.1.turned_ref, bf16[4,256,256]{2,1,0:T(8,128)(2,1)S(1)} %bitcast.24, bf16[4,256,256]{2,1,0:T(8,128)(2,1)S(1)} %collective-permute-done.refs_1_, ...), custom_call_target="tpu_custom_call" | custom-call | flops 3758096384 | bytes 3670016 | tf_op jit(solution)/shard_map/half_product/pallas_call | solution.py:108
  61.8 4.4 %collective-permute-start.8 = (f32[4,2,512,256]{3,2,1,0:T(8,128)S(1)}, f32[4,2,512,256]{3,2,1,0:T(8,128)S(1)}, u32[]{:S(2)}, u32[]{:S(2)}) collective-permute-start(f32[4,2,512,256]{3,2,1,0:T(8,128)S(1)} %half_product.3), channel_id=1, source_target_pairs={{0,1},{1,0},{2,3},{3,2},{4,5},{5,4},{6,7},{7,6},{8,9},{9,8},{10,11... | collective-permute-start | bytes 12582920 | tf_op jit(solution)/shard_map/ppermute | solution.py:188
  66.2 1.4 collective-permute-done.7.refs_7_
  67.7 5.2 %collective-permute-start.9 = (bf16[4,256,256]{2,1,0:T(8,128)(2,1)S(1)}, bf16[4,256,256]{2,1,0:T(8,128)(2,1)S(1)}, u32[]{:S(2)}, u32[]{:S(2)}) collective-permute-start(bf16[4,256,256]{2,1,0:T(8,128)(2,1)S(1)} %collective-permute-done.7.refs_7_), channel_id=1, source_target_pairs={{0,1},{1,0},{2,3},{3,2},{4,5},{5,4},{6,7},{7,6},{8,9},{9,8},{10,11... | collective-permute-start | bytes 1572872 | tf_op jit(solution)/shard_map/ppermute | solution.py:189
  72.9 5.0 %half_product.2.keep_ref = f32[4,2,512,256]{3,2,1,0:T(8,128)S(1)} custom-call(s32[9]{0:T(128)S(1)} %stack.63.where_ref, bf16[8,2048,256]{2,1,0:T(8,128)(2,1)S(1)} %turn.1.turned_ref, bf16[4,256,256]{2,1,0:T(8,128)(2,1)S(1)} %bitcast.25, bf16[4,256,256]{2,1,0:T(8,128)(2,1)S(1)} %collective-permute-done.refs_1_, ...), custom_call_target="tpu_custom_call" | custom-call | flops 85899345920 | bytes 83886080 | tf_op jit(solution)/shard_map/half_product/pallas_call | solution.py:108
  78.0 1.5 %add_pair.1 = f32[8,528,256]{2,1,0:T(8,128)S(1)} custom-call(f32[4,2,512,256]{3,2,1,0:T(8,128)S(1)} %half_product.2.keep_ref, f32[4,2,512,256]{3,2,1,0:T(8,128)S(1)} %collective-permute-done.8.got_ref, bf16[1,2,512,256]{3,2,1,0:T(8,128)(2,1)S(1)} %collective-permute-done.5.parts_ref, bf16[4,256,256]{2,1,0:T(8,128)(2,1)S(1)} %collective-permute-done.9.rows_ref), custom_call_target="tpu_custom_call" | custom-call | flops 536870912 | bytes 12582912 | tf_op jit(solution)/shard_map/add_pair/pallas_call | solution.py:139
  79.5 0.3 convert_element_type.13
  79.8 32.7 %all_to_all.26 = f16[8,528,256]{2,1,0:T(8,128)(2,1)S(1)} all-to-all(f16[8,528,256]{2,1,0:T(8,128)(2,1)S(1)} %convert_element_type.13), channel_id=1, replica_groups=mesh['y'=4,'xlo'=2,'z'=8,'xhi'=2,'core'=2] {'xhi','y'}, dimensions={0} | all-to-all | bytes 4325376 | tf_op jit(solution)/shard_map/all_to_all | solution.py:192
  112.5 0.2 fusion.3
  112.7 0.5 multiply_reduce_fusion
  113.2 0.0 copy-start.1
  113.2 0.3 fusion.4
  113.5 10.2 %all_to_all.27 = f32[8,32,256]{2,1,0:T(8,128)S(1)} all-to-all(f32[8,32,256]{2,1,0:T(8,128)S(1)} %bitcast.27), channel_id=1, replica_groups=mesh['y'=4,'xlo'=2,'z'=8,'xhi'=2,'core'=2] {'xlo','xhi','core'}, dimensions={0} | all-to-all | bytes 524288 | tf_op jit(solution)/shard_map/all_to_all | solution.py:199
  123.7 14.7 %all_to_all.28 = f32[8,32,256]{2,1,0:T(8,128)S(1)} all-to-all(f32[8,32,256]{2,1,0:T(8,128)S(1)} %broadcast_in_dim.11), channel_id=1, replica_groups=mesh['y'=4,'xlo'=2,'z'=8,'xhi'=2,'core'=2] {'z'}, dimensions={0} | all-to-all | bytes 524288 | tf_op jit(solution)/shard_map/all_to_all | solution.py:200
  138.5 11.4 %all_to_all.29 = f32[8,32,256]{2,1,0:T(8,128)S(1)} all-to-all(f32[8,32,256]{2,1,0:T(8,128)S(1)} %broadcast_in_dim.12), channel_id=1, replica_groups=mesh['y'=4,'xlo'=2,'z'=8,'xhi'=2,'core'=2] {'xlo','xhi','core'}, dimensions={0} | all-to-all | bytes 524288 | tf_op jit(solution)/shard_map/all_to_all | solution.py:201
  149.9 0.7 bitcast_subtract_fusion
  (20 shorter events, 0.2 us)
Async XLA Ops:
  18.0 15.9 %collective-permute-start = (bf16[4,256,256]{2,1,0:T(8,128)(2,1)S(1)}, bf16[4,256,256]{2,1,0:T(8,128)(2,1)S(1)}, u32[]{:S(2)}, u32[]{:S(2)}) collective-permute-start(bf16[4,256,256]{2,1,0:T(8,128)(2,1)S(1)} %bitcast.22), channel_id=1, source_target_pairs={{0,4},{4,8},{8,12},{12,16},{16,20},{20,24},{24,28},{28,0},{1,5},{5... | collective-permute-start | bytes 1572872 | tf_op jit(solution)/shard_map/ppermute | solution.py:178
  19.7 14.3 %collective-permute-start.1 = (bf16[4,256,256]{2,1,0:T(8,128)(2,1)S(1)}, bf16[4,256,256]{2,1,0:T(8,128)(2,1)S(1)}, u32[]{:S(2)}, u32[]{:S(2)}) collective-permute-start(bf16[4,256,256]{2,1,0:T(8,128)(2,1)S(1)} %bitcast.23), channel_id=1, source_target_pairs={{0,28},{4,0},{8,4},{12,8},{16,12},{20,16},{24,20},{28,24},{1,29},{... | collective-permute-start | bytes 1572872 | tf_op jit(solution)/shard_map/ppermute | solution.py:178
  23.6 3.4 %copy-start = (bf16[16,1,128,2048]{3,2,1,0:T(8,128)(2,1)S(1)}, bf16[16,1,128,2048]{3,2,1,0:T(8,128)(2,1)}, u32[]{:S(2)}) copy-start(bf16[16,1,128,2048]{3,2,1,0:T(8,128)(2,1)} %param.4) | copy-start | bytes 25165828
  34.0 12.1 %collective-permute-start.2 = (bf16[4,256,256]{2,1,0:T(8,128)(2,1)S(1)}, bf16[4,256,256]{2,1,0:T(8,128)(2,1)S(1)}, u32[]{:S(2)}, u32[]{:S(2)}) collective-permute-start(bf16[4,256,256]{2,1,0:T(8,128)(2,1)S(1)} %collective-permute-done.refs_1_), channel_id=1, source_target_pairs={{0,4},{4,8},{8,12},{12,16},{16,20},{20,24},{24,28},{28,0},{1,5},{5... | collective-permute-start | bytes 1572872 | tf_op jit(solution)/shard_map/ppermute | solution.py:180
  34.0 12.1 %collective-permute-start.3 = (bf16[4,256,256]{2,1,0:T(8,128)(2,1)S(1)}, bf16[4,256,256]{2,1,0:T(8,128)(2,1)S(1)}, u32[]{:S(2)}, u32[]{:S(2)}) collective-permute-start(bf16[4,256,256]{2,1,0:T(8,128)(2,1)S(1)} %collective-permute-done.1.refs_2_), channel_id=1, source_target_pairs={{0,28},{4,0},{8,4},{12,8},{16,12},{20,16},{24,20},{28,24},{1,29},{... | collective-permute-start | bytes 1572872 | tf_op jit(solution)/shard_map/ppermute | solution.py:180
  37.3 11.5 %collective-permute-start.5 = (bf16[1,2,512,256]{3,2,1,0:T(8,128)(2,1)S(1)}, bf16[1,2,512,256]{3,2,1,0:T(8,128)(2,1)S(1)}, u32[]{:S(2)}, u32[]{:S(2)}) collective-permute-start(bf16[1,2,512,256]{3,2,1,0:T(8,128)(2,1)S(1)} %pick.1), channel_id=1, source_target_pairs={{0,1},{1,0},{2,3},{3,2},{4,5},{5,4},{6,7},{7,6},{8,9},{9,8},{10,11... | collective-permute-start | bytes 1572872 | tf_op jit(solution)/shard_map/ppermute | solution.py:181
  46.1 11.2 %collective-permute-start.4 = (bf16[4,256,256]{2,1,0:T(8,128)(2,1)S(1)}, bf16[4,256,256]{2,1,0:T(8,128)(2,1)S(1)}, u32[]{:S(2)}, u32[]{:S(2)}) collective-permute-start(bf16[4,256,256]{2,1,0:T(8,128)(2,1)S(1)} %collective-permute-done.2.refs_3_), channel_id=1, source_target_pairs={{0,4},{4,8},{8,12},{12,16},{16,20},{20,24},{24,28},{28,0},{1,5},{5... | collective-permute-start | bytes 1572872 | tf_op jit(solution)/shard_map/ppermute | solution.py:182
  46.1 11.2 %collective-permute-start.6 = (bf16[4,256,256]{2,1,0:T(8,128)(2,1)S(1)}, bf16[4,256,256]{2,1,0:T(8,128)(2,1)S(1)}, u32[]{:S(2)}, u32[]{:S(2)}) collective-permute-start(bf16[4,256,256]{2,1,0:T(8,128)(2,1)S(1)} %collective-permute-done.3.refs_4_), channel_id=1, source_target_pairs={{0,28},{4,0},{8,4},{12,8},{16,12},{20,16},{24,20},{28,24},{1,29},{... | collective-permute-start | bytes 1572872 | tf_op jit(solution)/shard_map/ppermute | solution.py:182
  57.3 10.3 %collective-permute-start.7 = (bf16[4,256,256]{2,1,0:T(8,128)(2,1)S(1)}, bf16[4,256,256]{2,1,0:T(8,128)(2,1)S(1)}, u32[]{:S(2)}, u32[]{:S(2)}) collective-permute-start(bf16[4,256,256]{2,1,0:T(8,128)(2,1)S(1)} %collective-permute-done.4.refs_5_), channel_id=1, source_target_pairs={{0,4},{4,8},{8,12},{12,16},{16,20},{20,24},{24,28},{28,0},{1,5},{5... | collective-permute-start | bytes 1572872 | tf_op jit(solution)/shard_map/ppermute | solution.py:184
  61.8 16.1 %collective-permute-start.8 = (f32[4,2,512,256]{3,2,1,0:T(8,128)S(1)}, f32[4,2,512,256]{3,2,1,0:T(8,128)S(1)}, u32[]{:S(2)}, u32[]{:S(2)}) collective-permute-start(f32[4,2,512,256]{3,2,1,0:T(8,128)S(1)} %half_product.3), channel_id=1, source_target_pairs={{0,1},{1,0},{2,3},{3,2},{4,5},{5,4},{6,7},{7,6},{8,9},{9,8},{10,11... | collective-permute-start | bytes 12582920 | tf_op jit(solution)/shard_map/ppermute | solution.py:188
  67.7 10.3 %collective-permute-start.9 = (bf16[4,256,256]{2,1,0:T(8,128)(2,1)S(1)}, bf16[4,256,256]{2,1,0:T(8,128)(2,1)S(1)}, u32[]{:S(2)}, u32[]{:S(2)}) collective-permute-start(bf16[4,256,256]{2,1,0:T(8,128)(2,1)S(1)} %collective-permute-done.7.refs_7_), channel_id=1, source_target_pairs={{0,1},{1,0},{2,3},{3,2},{4,5},{5,4},{6,7},{7,6},{8,9},{9,8},{10,11... | collective-permute-start | bytes 1572872 | tf_op jit(solution)/shard_map/ppermute | solution.py:189
  79.8 33.5 %copy-start.3 = (bf16[512,256]{1,0:T(8,128)(2,1)S(1)}, bf16[512,256]{1,0:T(8,128)(2,1)}, u32[]{:S(2)}) copy-start(bf16[512,256]{1,0:T(8,128)(2,1)} %get-tuple-element.21) | copy-start | bytes 786436
  112.5 37.4 %copy-start.2 = (f32[1,256,256]{2,1,0:T(8,128)S(1)}, f32[1,256,256]{2,1,0:T(8,128)}, u32[]{:S(2)}) copy-start(f32[1,256,256]{2,1,0:T(8,128)} %param.7) | copy-start | bytes 786436
  113.2 37.5 %copy-start.1 = (bf16[512,256]{1,0:T(8,128)(2,1)}, bf16[512,256]{1,0:T(8,128)(2,1)S(1)}, u32[]{:S(2)}) copy-start(bf16[512,256]{1,0:T(8,128)(2,1)S(1)} %negate_convert_fusion) | copy-start | bytes 786436

commit v5 on v4

--- a/solution.py
+++ b/solution.py
@@ -162,14 +162,14 @@
     blocks = ancestor_cols.reshape(2, num_z, quarter, height)
 
     order = [jnp.remainder(z + o, num_z) for o in (0, -1, 1, -2, 2, -3, 3, num_z // 2)]
-    mine, theirs = [core], [1 - core]
-    lists = [[group * (sub // width)], order[:7] + theirs, order[7:] + theirs, order + mine]
+    five, late, last, mine, theirs = order[:5], order[5:7], order[7:], [core], [1 - core]
+    lists = [[group * (sub // width)], five + theirs, late + theirs, last + theirs, five + mine, late + last + mine]
     places = jnp.stack(sum(lists, [])).astype(jnp.int32)
     ends = [sum(len(a) for a in lists[:n]) for n in range(len(lists) + 1)]
-    place, first, given, every = (places[a:b] for a, b in zip(ends, ends[1:]))
+    place, give5, give7, given, keep5, keep8 = (places[a:b] for a, b in zip(ends, ends[1:]))
 
     pieces, masked = mask(place, block_mask, factor, quarter)
-    pieces, first, given, every = lax.optimization_barrier((pieces, first, given, every))
+    pieces, give5, give7, given, keep5, keep8 = lax.optimization_barrier((pieces, give5, give7, given, keep5, keep8))
     own = lax.all_to_all(pieces.reshape(num_y * 2, quarter, width), ("y", "xlo"), 0, 0)
     own = own.reshape(num_y, 2 * quarter, width)
 
@@ -180,14 +180,16 @@
     below2, above2 = lax.ppermute(below, "z", up), lax.ppermute(above, "z", down)
     parts = lax.ppermute(pick(turned, given), "core", SWAP)
     below3, above3 = lax.ppermute(below2, "z", up), lax.ppermute(above2, "z", down)
-    below3, parts = lax.optimization_barrier((below3, parts))
+    near = [own, below, above, below2, above2]
+    give = half_product(turned, give5, near, weight=10)
+    keep = half_product(turned, keep5, near, weight=10)
+    below3, parts, keep, give = lax.optimization_barrier((below3, parts, keep, give))
     far = lax.ppermute(below3, "z", up)
 
-    near = [own, below, above, below2, above2, below3, above3]
-    give = half_product(turned, first, near, weight=1)
+    give = half_product(turned, give7, [below3, above3], give)
     got = lax.ppermute(give, "core", SWAP)
     far_other = lax.ppermute(far, "core", SWAP)
-    keep = half_product(turned, every, near + [far], weight=20)
+    keep = half_product(turned, keep8, [below3, above3, far], keep, weight=60)
 
     parts = lax.all_to_all(add_pair(keep, got, parts, far_other).astype(F16), ("xhi", "y"), 0, 0)
     back = jnp.exp2(parts[:, sub, 0].astype(F32) - 15.0)

time: 151 us -> 149 us (0.987)
  waiting for transfers between devices: 17.8 us -> 13.4 us
  Pallas kernels: 18.4 us -> 20.1 us
    ppermute x1, waiting for transfers between devices: 8.51 us -> 1.66 us  [shards(): lax.ppermute(below2, 'z', up)]
    ppermute x1, waiting for transfers between devices: 1.41 us -> 3.96 us  [shards(): far = lax.ppermute(below3, 'z', up)]
    pallas_call x2 -> x4, Pallas kernels: 9.52 us -> 11.2 us  [half_product(): pl.pallas_call(functools.partial(half_kernel, num, spare, bool(more)), ou...]
  transfers between devices with their start and end apart: 10 -> 10, of which waited for: 4 -> 4; matrix products, arithmetic and copies ran while one was open for 0% -> 0% of each run, Pallas kernels for 10% -> 11%
where the time goes in v5:
time: 149 us; the launch traced here: 148 us
  blocking collectives  84.2 us (57%)
  starting transfers between devices  23.8 us (16%)
  Pallas kernels  20.1 us (13%)
  waiting for transfers between devices  13.4 us (9%)
  local copies, waits for them, and re-layouts  3.6 us (2%)
  other arithmetic  1.97 us (1%)
    all_to_all x1, blocking collectives, shards(): lax.all_to_all(add_pair(keep, got, parts, far_other).astype(F16), ('xhi',...  32.7 us
    all_to_all x1, blocking collectives, shards(): lax.all_to_all(pieces.reshape(num_y * 2, quarter, width), ('y', 'xlo'), 0...  15.2 us
    all_to_all x1, blocking collectives, shards(): lax.all_to_all(jnp.broadcast_to(mine, (num_z,) + mine.shape), 'z', 0, 0)  14.7 us
    all_to_all x1, blocking collectives, shards(): lax.all_to_all(jnp.broadcast_to(over_z, (8,) + over_z.shape), ALONG_X, 0, 0)  11.4 us
    pallas_call x4, Pallas kernels, half_product(): pl.pallas_call(functools.partial(half_kernel, num, spare, bool(more)), ou...  11.2 us
    all_to_all x1, blocking collectives, shards(): mine = jnp.sum(lax.all_to_all(split, ALONG_X, 0, 0), 0)  10.2 us
    ppermute x1, waiting for transfers between devices, shards(): lax.ppermute(below, 'z', up)  5.7 us
    ppermute x2, starting transfers between devices, shards(): below, above = (lax.ppermute(own, 'z', up), lax.ppermute(own, 'z', down))  5.58 us
  transfers between devices with their start and end apart: 10, of which 4 were waited for; matrix products, arithmetic and copies ran while one was open for 0% of the time, Pallas kernels for 11%

profile of v5, /device:TPU:1, one launch (start us, length us, event | category | flops | bytes accessed | tf_op | source)
XLA Modules:
  0.0 148.3 jit_solution(14771993545899322097)
XLA Ops:
  0.7 0.1 stack.64.where_ref
  0.8 0.1 stack.71.where_ref
  1.1 1.9 %mask.1 = (bf16[4,2,128,256]{3,2,1,0:T(8,128)(2,1)}, bf16[512,256]{1,0:T(8,128)(2,1)}) custom-call(s32[1]{0:T(128)} %bitcast.place_ref, s32[1,128]{1,0:T(1,128)} %mask_ref.1, bf16[1,512,256]{2,1,0:T(8,128)(2,1)} %factor_ref.1), custom_call_target="tpu_custom_call" | custom-call | flops 131072 | bytes 1048576 | tf_op jit(solution)/shard_map/mask/pallas_call | solution.py:32
  3.0 15.2 %all_to_all.25 = bf16[8,128,256]{2,1,0:T(8,128)(2,1)S(1)} all-to-all(bf16[8,128,256]{2,1,0:T(8,128)(2,1)} %bitcast.29), channel_id=1, replica_groups=mesh['y'=4,'xlo'=2,'z'=8,'xhi'=2,'core'=2] {'y','xlo'}, dimensions={0} | all-to-all | bytes 1048576 | tf_op jit(solution)/shard_map/all_to_all | solution.py:173
  18.2 1.6 %collective-permute-start = (bf16[4,256,256]{2,1,0:T(8,128)(2,1)S(1)}, bf16[4,256,256]{2,1,0:T(8,128)(2,1)S(1)}, u32[]{:S(2)}, u32[]{:S(2)}) collective-permute-start(bf16[4,256,256]{2,1,0:T(8,128)(2,1)S(1)} %bitcast.22), channel_id=1, source_target_pairs={{0,4},{4,8},{8,12},{12,16},{16,20},{20,24},{24,28},{28,0},{1,5},{5... | collective-permute-start | bytes 1572872 | tf_op jit(solution)/shard_map/ppermute | solution.py:178
  19.8 3.9 %collective-permute-start.4 = (bf16[4,256,256]{2,1,0:T(8,128)(2,1)S(1)}, bf16[4,256,256]{2,1,0:T(8,128)(2,1)S(1)}, u32[]{:S(2)}, u32[]{:S(2)}) collective-permute-start(bf16[4,256,256]{2,1,0:T(8,128)(2,1)S(1)} %bitcast.23), channel_id=1, source_target_pairs={{0,28},{4,0},{8,4},{12,8},{16,12},{20,16},{24,20},{28,24},{1,29},{... | collective-permute-start | bytes 1572872 | tf_op jit(solution)/shard_map/ppermute | solution.py:178
  23.8 3.4 %copy-done = bf16[16,1,128,2048]{3,2,1,0:T(8,128)(2,1)S(1)} copy-done((bf16[16,1,128,2048]{3,2,1,0:T(8,128)(2,1)S(1)}, bf16[16,1,128,2048]{3,2,1,0:T(8,128)(2,1)}, u32[]{:S(2)}) %copy-start) | copy-done | bytes 8388632
  27.2 4.9 %turn.1.turned_ref = bf16[8,2048,256]{2,1,0:T(8,128)(2,1)S(1)} custom-call(bf16[2,8,128,2048]{3,2,1,0:T(8,128)(2,1)S(1)} %bitcast.21), custom_call_target="tpu_custom_call" | custom-call | bytes 16777216 | tf_op jit(solution)/shard_map/turn/pallas_call | solution.py:52
  32.0 2.1 %collective-permute-done.refs_1_ = bf16[4,256,256]{2,1,0:T(8,128)(2,1)S(1)} collective-permute-done((bf16[4,256,256]{2,1,0:T(8,128)(2,1)S(1)}, bf16[4,256,256]{2,1,0:T(8,128)(2,1)S(1)}, u32[]{:S(2)}, u32[]{:S(2)}) %collective-permute-start) | collective-permute-done | bytes 524320 | tf_op jit(solution)/shard_map/ppermute | solution.py:178
  34.1 2.7 %collective-permute-start.5 = (bf16[4,256,256]{2,1,0:T(8,128)(2,1)S(1)}, bf16[4,256,256]{2,1,0:T(8,128)(2,1)S(1)}, u32[]{:S(2)}, u32[]{:S(2)}) collective-permute-start(bf16[4,256,256]{2,1,0:T(8,128)(2,1)S(1)} %collective-permute-done.4.refs_2_), channel_id=1, source_target_pairs={{0,28},{4,0},{8,4},{12,8},{16,12},{20,16},{24,20},{28,24},{1,29},{... | collective-permute-start | bytes 1572872 | tf_op jit(solution)/shard_map/ppermute | solution.py:180
  36.8 0.6 pick.1
  37.4 3.2 %collective-permute-start.3 = (bf16[1,2,512,256]{3,2,1,0:T(8,128)(2,1)S(1)}, bf16[1,2,512,256]{3,2,1,0:T(8,128)(2,1)S(1)}, u32[]{:S(2)}, u32[]{:S(2)}) collective-permute-start(bf16[1,2,512,256]{3,2,1,0:T(8,128)(2,1)S(1)} %pick.1), channel_id=1, source_target_pairs={{0,1},{1,0},{2,3},{3,2},{4,5},{5,4},{6,7},{7,6},{8,9},{9,8},{10,11... | collective-permute-start | bytes 1572872 | tf_op jit(solution)/shard_map/ppermute | solution.py:181
  40.6 5.7 %collective-permute-done.1.refs_3_ = bf16[4,256,256]{2,1,0:T(8,128)(2,1)S(1)} collective-permute-done((bf16[4,256,256]{2,1,0:T(8,128)(2,1)S(1)}, bf16[4,256,256]{2,1,0:T(8,128)(2,1)S(1)}, u32[]{:S(2)}, u32[]{:S(2)}) %collective-permute-start.1) | collective-permute-done | bytes 524320 | tf_op jit(solution)/shard_map/ppermute | solution.py:180
  46.3 2.7 %collective-permute-start.6 = (bf16[4,256,256]{2,1,0:T(8,128)(2,1)S(1)}, bf16[4,256,256]{2,1,0:T(8,128)(2,1)S(1)}, u32[]{:S(2)}, u32[]{:S(2)}) collective-permute-start(bf16[4,256,256]{2,1,0:T(8,128)(2,1)S(1)} %collective-permute-done.5.refs_4_), channel_id=1, source_target_pairs={{0,28},{4,0},{8,4},{12,8},{16,12},{20,16},{24,20},{28,24},{1,29},{... | collective-permute-start | bytes 1572872 | tf_op jit(solution)/shard_map/ppermute | solution.py:182
  48.9 3.4 %half_product.5.refs_2_ = f32[4,2,512,256]{3,2,1,0:T(8,128)S(1)} custom-call(s32[6]{0:T(128)S(1)} %stack.64.where_ref, bf16[8,2048,256]{2,1,0:T(8,128)(2,1)S(1)} %turn.1.turned_ref, bf16[4,256,256]{2,1,0:T(8,128)(2,1)S(1)} %bitcast.24, bf16[4,256,256]{2,1,0:T(8,128)(2,1)S(1)} %collective-permute-done.refs_1_, ...), custom_call_target="tpu_custom_call" | custom-call | flops 26843545600 | bytes 26214400 | tf_op jit(solution)/shard_map/half_product/pallas_call | solution.py:108
  52.4 3.4 %half_product.4.refs_3_ = f32[4,2,512,256]{3,2,1,0:T(8,128)S(1)} custom-call(s32[6]{0:T(128)S(1)} %stack.71.where_ref, bf16[8,2048,256]{2,1,0:T(8,128)(2,1)S(1)} %turn.1.turned_ref, bf16[4,256,256]{2,1,0:T(8,128)(2,1)S(1)} %bitcast.25, bf16[4,256,256]{2,1,0:T(8,128)(2,1)S(1)} %collective-permute-done.refs_1_, ...), custom_call_target="tpu_custom_call" | custom-call | flops 26843545600 | bytes 26214400 | tf_op jit(solution)/shard_map/half_product/pallas_call | solution.py:108
  55.8 1.7 %collective-permute-done.2.refs_0_ = bf16[4,256,256]{2,1,0:T(8,128)(2,1)S(1)} collective-permute-done((bf16[4,256,256]{2,1,0:T(8,128)(2,1)S(1)}, bf16[4,256,256]{2,1,0:T(8,128)(2,1)S(1)}, u32[]{:S(2)}, u32[]{:S(2)}) %collective-permute-start.2) | collective-permute-done | bytes 524320 | tf_op jit(solution)/shard_map/ppermute | solution.py:182
  57.5 1.9 %half_product.7 = f32[4,2,512,256]{3,2,1,0:T(8,128)S(1)} custom-call(s32[3]{0:T(128)S(1)} %pad_add_fusion.where_ref, bf16[8,2048,256]{2,1,0:T(8,128)(2,1)S(1)} %turn.1.turned_ref, bf16[4,256,256]{2,1,0:T(8,128)(2,1)S(1)} %collective-permute-done.2.refs_0_, bf16[4,256,256]{2,1,0:T(8,128)(2,1)S(1)} %collective-permute-done.6.refs_1_, ...), custom_call_target="tpu_custom_call", output_to_operand_aliasing={{}: (4, {})} | custom-call | flops 1073741824 | bytes 1048576 | tf_op jit(solution)/shard_map/half_product/pallas_call | solution.py:108
  59.4 4.4 %collective-permute-start.8 = (f32[4,2,512,256]{3,2,1,0:T(8,128)S(1)}, f32[4,2,512,256]{3,2,1,0:T(8,128)S(1)}, u32[]{:S(2)}, u32[]{:S(2)}) collective-permute-start(f32[4,2,512,256]{3,2,1,0:T(8,128)S(1)} %half_product.7), channel_id=1, source_target_pairs={{0,1},{1,0},{2,3},{3,2},{4,5},{5,4},{6,7},{7,6},{8,9},{9,8},{10,11... | collective-permute-start | bytes 12582920 | tf_op jit(solution)/shard_map/ppermute | solution.py:190
  63.8 4.0 %collective-permute-done.7.refs_2_ = bf16[4,256,256]{2,1,0:T(8,128)(2,1)S(1)} collective-permute-done((bf16[4,256,256]{2,1,0:T(8,128)(2,1)S(1)}, bf16[4,256,256]{2,1,0:T(8,128)(2,1)S(1)}, u32[]{:S(2)}, u32[]{:S(2)}) %collective-permute-start.7) | collective-permute-done | bytes 524320 | tf_op jit(solution)/shard_map/ppermute | solution.py:187
  67.8 5.2 %collective-permute-start.9 = (bf16[4,256,256]{2,1,0:T(8,128)(2,1)S(1)}, bf16[4,256,256]{2,1,0:T(8,128)(2,1)S(1)}, u32[]{:S(2)}, u32[]{:S(2)}) collective-permute-start(bf16[4,256,256]{2,1,0:T(8,128)(2,1)S(1)} %collective-permute-done.7.refs_2_), channel_id=1, source_target_pairs={{0,1},{1,0},{2,3},{3,2},{4,5},{5,4},{6,7},{7,6},{8,9},{9,8},{10,11... | collective-permute-start | bytes 1572872 | tf_op jit(solution)/shard_map/ppermute | solution.py:191
  73.0 2.5 %half_product.6.keep_ref = f32[4,2,512,256]{3,2,1,0:T(8,128)S(1)} custom-call(s32[4]{0:T(128)S(1)} %pad_add_fusion.2.where_ref, bf16[8,2048,256]{2,1,0:T(8,128)(2,1)S(1)} %turn.1.turned_ref, bf16[4,256,256]{2,1,0:T(8,128)(2,1)S(1)} %collective-permute-done.2.refs_0_, ...), custom_call_target="tpu_custom_call", output_to_operand_aliasing={{}: (5, {})} | custom-call | flops 96636764160 | bytes 94371840 | tf_op jit(solution)/shard_map/half_product/pallas_call | solution.py:108
  75.5 1.5 %add_pair.1 = f32[8,528,256]{2,1,0:T(8,128)S(1)} custom-call(f32[4,2,512,256]{3,2,1,0:T(8,128)S(1)} %half_product.6.keep_ref, f32[4,2,512,256]{3,2,1,0:T(8,128)S(1)} %collective-permute-done.8.got_ref, bf16[1,2,512,256]{3,2,1,0:T(8,128)(2,1)S(1)} %collective-permute-done.3.parts_ref, bf16[4,256,256]{2,1,0:T(8,128)(2,1)S(1)} %collective-permute-done.9.rows_ref), custom_call_target="tpu_custom_call" | custom-call | flops 536870912 | bytes 12582912 | tf_op jit(solution)/shard_map/add_pair/pallas_call | solution.py:139
  77.1 0.3 convert_element_type.13
  77.4 32.7 %all_to_all.26 = f16[8,528,256]{2,1,0:T(8,128)(2,1)S(1)} all-to-all(f16[8,528,256]{2,1,0:T(8,128)(2,1)S(1)} %convert_element_type.13), channel_id=1, replica_groups=mesh['y'=4,'xlo'=2,'z'=8,'xhi'=2,'core'=2] {'xhi','y'}, dimensions={0} | all-to-all | bytes 4325376 | tf_op jit(solution)/shard_map/all_to_all | solution.py:194
  110.1 0.2 fusion.3
  110.2 0.5 multiply_reduce_fusion
  110.8 0.3 fusion.4
  111.1 10.2 %all_to_all.27 = f32[8,32,256]{2,1,0:T(8,128)S(1)} all-to-all(f32[8,32,256]{2,1,0:T(8,128)S(1)} %bitcast.27), channel_id=1, replica_groups=mesh['y'=4,'xlo'=2,'z'=8,'xhi'=2,'core'=2] {'xlo','xhi','core'}, dimensions={0} | all-to-all | bytes 524288 | tf_op jit(solution)/shard_map/all_to_all | solution.py:201
  121.3 14.7 %all_to_all.28 = f32[8,32,256]{2,1,0:T(8,128)S(1)} all-to-all(f32[8,32,256]{2,1,0:T(8,128)S(1)} %broadcast_in_dim.11), channel_id=1, replica_groups=mesh['y'=4,'xlo'=2,'z'=8,'xhi'=2,'core'=2] {'z'}, dimensions={0} | all-to-all | bytes 524288 | tf_op jit(solution)/shard_map/all_to_all | solution.py:202
  136.1 11.4 %all_to_all.29 = f32[8,32,256]{2,1,0:T(8,128)S(1)} all-to-all(f32[8,32,256]{2,1,0:T(8,128)S(1)} %broadcast_in_dim.12), channel_id=1, replica_groups=mesh['y'=4,'xlo'=2,'z'=8,'xhi'=2,'core'=2] {'xlo','xhi','core'}, dimensions={0} | all-to-all | bytes 524288 | tf_op jit(solution)/shard_map/all_to_all | solution.py:203
  147.5 0.7 bitcast_subtract_fusion
  (24 shorter events, 0.4 us)
Async XLA Ops:
  18.2 15.9 %collective-permute-start = (bf16[4,256,256]{2,1,0:T(8,128)(2,1)S(1)}, bf16[4,256,256]{2,1,0:T(8,128)(2,1)S(1)}, u32[]{:S(2)}, u32[]{:S(2)}) collective-permute-start(bf16[4,256,256]{2,1,0:T(8,128)(2,1)S(1)} %bitcast.22), channel_id=1, source_target_pairs={{0,4},{4,8},{8,12},{12,16},{16,20},{20,24},{24,28},{28,0},{1,5},{5... | collective-permute-start | bytes 1572872 | tf_op jit(solution)/shard_map/ppermute | solution.py:178
  19.8 14.3 %collective-permute-start.4 = (bf16[4,256,256]{2,1,0:T(8,128)(2,1)S(1)}, bf16[4,256,256]{2,1,0:T(8,128)(2,1)S(1)}, u32[]{:S(2)}, u32[]{:S(2)}) collective-permute-start(bf16[4,256,256]{2,1,0:T(8,128)(2,1)S(1)} %bitcast.23), channel_id=1, source_target_pairs={{0,28},{4,0},{8,4},{12,8},{16,12},{20,16},{24,20},{28,24},{1,29},{... | collective-permute-start | bytes 1572872 | tf_op jit(solution)/shard_map/ppermute | solution.py:178
  23.8 3.4 %copy-start = (bf16[16,1,128,2048]{3,2,1,0:T(8,128)(2,1)S(1)}, bf16[16,1,128,2048]{3,2,1,0:T(8,128)(2,1)}, u32[]{:S(2)}) copy-start(bf16[16,1,128,2048]{3,2,1,0:T(8,128)(2,1)} %param.4) | copy-start | bytes 25165828
  34.1 12.1 %collective-permute-start.1 = (bf16[4,256,256]{2,1,0:T(8,128)(2,1)S(1)}, bf16[4,256,256]{2,1,0:T(8,128)(2,1)S(1)}, u32[]{:S(2)}, u32[]{:S(2)}) collective-permute-start(bf16[4,256,256]{2,1,0:T(8,128)(2,1)S(1)} %collective-permute-done.refs_1_), channel_id=1, source_target_pairs={{0,4},{4,8},{8,12},{12,16},{16,20},{20,24},{24,28},{28,0},{1,5},{5... | collective-permute-start | bytes 1572872 | tf_op jit(solution)/shard_map/ppermute | solution.py:180
  34.1 12.1 %collective-permute-start.5 = (bf16[4,256,256]{2,1,0:T(8,128)(2,1)S(1)}, bf16[4,256,256]{2,1,0:T(8,128)(2,1)S(1)}, u32[]{:S(2)}, u32[]{:S(2)}) collective-permute-start(bf16[4,256,256]{2,1,0:T(8,128)(2,1)S(1)} %collective-permute-done.4.refs_2_), channel_id=1, source_target_pairs={{0,28},{4,0},{8,4},{12,8},{16,12},{20,16},{24,20},{28,24},{1,29},{... | collective-permute-start | bytes 1572872 | tf_op jit(solution)/shard_map/ppermute | solution.py:180
  37.4 18.4 %collective-permute-start.3 = (bf16[1,2,512,256]{3,2,1,0:T(8,128)(2,1)S(1)}, bf16[1,2,512,256]{3,2,1,0:T(8,128)(2,1)S(1)}, u32[]{:S(2)}, u32[]{:S(2)}) collective-permute-start(bf16[1,2,512,256]{3,2,1,0:T(8,128)(2,1)S(1)} %pick.1), channel_id=1, source_target_pairs={{0,1},{1,0},{2,3},{3,2},{4,5},{5,4},{6,7},{7,6},{8,9},{9,8},{10,11... | collective-permute-start | bytes 1572872 | tf_op jit(solution)/shard_map/ppermute | solution.py:181
  46.3 11.2 %collective-permute-start.2 = (bf16[4,256,256]{2,1,0:T(8,128)(2,1)S(1)}, bf16[4,256,256]{2,1,0:T(8,128)(2,1)S(1)}, u32[]{:S(2)}, u32[]{:S(2)}) collective-permute-start(bf16[4,256,256]{2,1,0:T(8,128)(2,1)S(1)} %collective-permute-done.1.refs_3_), channel_id=1, source_target_pairs={{0,4},{4,8},{8,12},{12,16},{16,20},{20,24},{24,28},{28,0},{1,5},{5... | collective-permute-start | bytes 1572872 | tf_op jit(solution)/shard_map/ppermute | solution.py:182
  46.3 11.2 %collective-permute-start.6 = (bf16[4,256,256]{2,1,0:T(8,128)(2,1)S(1)}, bf16[4,256,256]{2,1,0:T(8,128)(2,1)S(1)}, u32[]{:S(2)}, u32[]{:S(2)}) collective-permute-start(bf16[4,256,256]{2,1,0:T(8,128)(2,1)S(1)} %collective-permute-done.5.refs_4_), channel_id=1, source_target_pairs={{0,28},{4,0},{8,4},{12,8},{16,12},{20,16},{24,20},{28,24},{1,29},{... | collective-permute-start | bytes 1572872 | tf_op jit(solution)/shard_map/ppermute | solution.py:182
  57.5 10.3 %collective-permute-start.7 = (bf16[4,256,256]{2,1,0:T(8,128)(2,1)S(1)}, bf16[4,256,256]{2,1,0:T(8,128)(2,1)S(1)}, u32[]{:S(2)}, u32[]{:S(2)}) collective-permute-start(bf16[4,256,256]{2,1,0:T(8,128)(2,1)S(1)} %collective-permute-done.2.refs_0_), channel_id=1, source_target_pairs={{0,4},{4,8},{8,12},{12,16},{16,20},{20,24},{24,28},{28,0},{1,5},{5... | collective-permute-start | bytes 1572872 | tf_op jit(solution)/shard_map/ppermute | solution.py:187
  59.4 16.1 %collective-permute-start.8 = (f32[4,2,512,256]{3,2,1,0:T(8,128)S(1)}, f32[4,2,512,256]{3,2,1,0:T(8,128)S(1)}, u32[]{:S(2)}, u32[]{:S(2)}) collective-permute-start(f32[4,2,512,256]{3,2,1,0:T(8,128)S(1)} %half_product.7), channel_id=1, source_target_pairs={{0,1},{1,0},{2,3},{3,2},{4,5},{5,4},{6,7},{7,6},{8,9},{9,8},{10,11... | collective-permute-start | bytes 12582920 | tf_op jit(solution)/shard_map/ppermute | solution.py:190
  67.8 7.7 %collective-permute-start.9 = (bf16[4,256,256]{2,1,0:T(8,128)(2,1)S(1)}, bf16[4,256,256]{2,1,0:T(8,128)(2,1)S(1)}, u32[]{:S(2)}, u32[]{:S(2)}) collective-permute-start(bf16[4,256,256]{2,1,0:T(8,128)(2,1)S(1)} %collective-permute-done.7.refs_2_), channel_id=1, source_target_pairs={{0,1},{1,0},{2,3},{3,2},{4,5},{5,4},{6,7},{7,6},{8,9},{9,8},{10,11... | collective-permute-start | bytes 1572872 | tf_op jit(solution)/shard_map/ppermute | solution.py:191
  77.4 33.5 %copy-start.3 = (bf16[512,256]{1,0:T(8,128)(2,1)S(1)}, bf16[512,256]{1,0:T(8,128)(2,1)}, u32[]{:S(2)}) copy-start(bf16[512,256]{1,0:T(8,128)(2,1)} %get-tuple-element.29) | copy-start | bytes 786436
  110.1 37.4 %copy-start.2 = (f32[1,256,256]{2,1,0:T(8,128)S(1)}, f32[1,256,256]{2,1,0:T(8,128)}, u32[]{:S(2)}) copy-start(f32[1,256,256]{2,1,0:T(8,128)} %param.7) | copy-start | bytes 786436
  110.8 37.5 %copy-start.1 = (bf16[512,256]{1,0:T(8,128)(2,1)}, bf16[512,256]{1,0:T(8,128)(2,1)S(1)}, u32[]{:S(2)}) copy-start(bf16[512,256]{1,0:T(8,128)(2,1)S(1)} %negate_convert_fusion) | copy-start | bytes 786436

commit v6 on v5

--- a/solution.py
+++ b/solution.py
@@ -85,35 +85,58 @@
     )(where, turned)
 
 
-def half_kernel(num, spare, more, where_ref, turned_ref, *refs):
-    rows, out_ref = refs[: num + len(spare)], refs[-1]
-    parts_ref = refs[num + len(spare)] if spare else None
+def part_kernel(first, rows_ref, out_ref):
+    out_ref[...] = rows_ref[first : first + out_ref.shape[0]]
+
+
+def part(rows, first):
+    return pl.pallas_call(
+        functools.partial(part_kernel, first),
+        out_shape=jax.ShapeDtypeStruct((rows.shape[0] // 2, *rows.shape[1:]), BF16),
+        in_specs=[pl.BlockSpec(memory_space=pltpu.VMEM)],
+        out_specs=pl.BlockSpec(memory_space=pltpu.VMEM),
+        compiler_params=pltpu.CompilerParams(vmem_limit_bytes=16 * 2**20),
+        cost_estimate=pl.CostEstimate(flops=0, bytes_accessed=0, transcendentals=0),
+        name="part",
+    )(rows)
+
+
+def child(rows, k):
+    for r in rows:
+        if k < r.shape[0]:
+            return r[k]
+        k -= r.shape[0]
+
+
+def half_kernel(num, split, more, where_ref, turned_ref, *refs):
+    rows, out_ref = [[r] for r in refs[:num]], refs[-1]
+    if split:
+        rows[-1].append(refs[num])
     kids, _, sub, _ = out_ref.shape
     for h in range(2):
         here = rows_of(where_ref, h, sub)
-        cols = [turned_ref[where_ref[b], here] for b in range(num)] + [parts_ref[p, h] for p in spare]
+        cols = [turned_ref[where_ref[b], here] for b in range(num)]
         cols = jnp.concatenate(cols, 1)
         for k in range(kids):
-            value = jnp.dot(cols, jnp.concatenate([r[k] for r in rows], 0), preferred_element_type=F32)
+            value = jnp.dot(cols, jnp.concatenate([child(r, k) for r in rows], 0), preferred_element_type=F32)
             out_ref[k, h] = refs[-2][k, h] + value if more else value
 
 
-def half_product(turned, where, rows, partial=None, parts=None, spare=(), others=(), weight=1):
-    num = len(rows)
+def half_product(turned, where, rows, partial=None, split=0, weight=1):
+    num = len(rows) - split
     _, height, depth = turned.shape
     kids, _, width = rows[0].shape
     more = [] if partial is None else [partial]
-    extra = [parts] if spare else []
-    arrays = [turned, *rows, *others, *extra, *more]
-    return pl.pallas_call(
-        functools.partial(half_kernel, num, spare, bool(more)),
+    arrays = [turned, *rows, *more]
+    return pl.pallas_call(
+        functools.partial(half_kernel, num, split, bool(more)),
         out_shape=jax.ShapeDtypeStruct((kids, 2, height // 4, width), F32),
         in_specs=[pl.BlockSpec(memory_space=pltpu.SMEM)] + [pl.BlockSpec(memory_space=pltpu.VMEM)] * len(arrays),
         out_specs=pl.BlockSpec(memory_space=pltpu.VMEM),
         input_output_aliases={len(arrays): 0} if more else {},
         compiler_params=pltpu.CompilerParams(vmem_limit_bytes=16 * 2**20),
         cost_estimate=pl.CostEstimate(
-            flops=weight * (num + len(spare)) * depth * height * kids * width,
+            flops=weight * num * depth * height * kids * width,
             bytes_accessed=weight * num * depth * height,
             transcendentals=0,
         ),
@@ -121,12 +144,12 @@
     )(where, *arrays)
 
 
-def pair_kernel(keep_ref, got_ref, parts_ref, rows_ref, message_ref):
+def pair_kernel(keep_ref, got_ref, parts_ref, low_ref, high_ref, message_ref):
     kids, halves, sub, width = keep_ref.shape
     last = parts_ref.shape[0] - 1
     for h in range(halves):
         for k in range(kids):
-            both = jnp.dot(parts_ref[last, h], rows_ref[k], preferred_element_type=F32)
+            both = jnp.dot(parts_ref[last, h], child([low_ref, high_ref], k), preferred_element_type=F32)
             both = both + (keep_ref[k, h] + got_ref[k, h])
             top = jnp.max(jnp.max(jnp.abs(both).reshape(-1, 8, width), axis=0), axis=(0, 1), keepdims=True)
             power = jnp.ceil(jnp.log2(jnp.maximum(top, 2.0**-100))) + 1.0
@@ -134,19 +157,19 @@
             message_ref[h * kids + k, sub:] = jnp.broadcast_to(power, (message_ref.shape[1] - sub, width))
 
 
-def add_pair(keep, got, parts, rows):
+def add_pair(keep, got, parts, low, high):
     kids, halves, sub, width = keep.shape
     return pl.pallas_call(
         pair_kernel,
         out_shape=jax.ShapeDtypeStruct((kids * halves, sub + 16, width), F32),
-        in_specs=[pl.BlockSpec(memory_space=pltpu.VMEM)] * 4,
+        in_specs=[pl.BlockSpec(memory_space=pltpu.VMEM)] * 5,
         out_specs=pl.BlockSpec(memory_space=pltpu.VMEM),
         compiler_params=pltpu.CompilerParams(vmem_limit_bytes=16 * 2**20),
         cost_estimate=pl.CostEstimate(
             flops=2 * keep.size * parts.shape[3], bytes_accessed=3 * keep.nbytes, transcendentals=0
         ),
         name="add_pair",
-    )(keep, got, parts, rows)
+    )(keep, got, parts, low, high)
 
 
 def shards(ancestor_cols, factor, block_mask, diag_inverse):
@@ -184,14 +207,14 @@
     give = half_product(turned, give5, near, weight=10)
     keep = half_product(turned, keep5, near, weight=10)
     below3, parts, keep, give = lax.optimization_barrier((below3, parts, keep, give))
-    far = lax.ppermute(below3, "z", up)
+    far = [lax.ppermute(part(below3, 0), "z", up), lax.ppermute(part(above3, num_y // 2), "z", down)]
 
     give = half_product(turned, give7, [below3, above3], give)
     got = lax.ppermute(give, "core", SWAP)
-    far_other = lax.ppermute(far, "core", SWAP)
-    keep = half_product(turned, keep8, [below3, above3, far], keep, weight=60)
-
-    parts = lax.all_to_all(add_pair(keep, got, parts, far_other).astype(F16), ("xhi", "y"), 0, 0)
+    other = [lax.ppermute(f, "core", SWAP) for f in far]
+    keep = half_product(turned, keep8, [below3, above3, *far], keep, split=1, weight=60)
+
+    parts = lax.all_to_all(add_pair(keep, got, parts, *other).astype(F16), ("xhi", "y"), 0, 0)
     back = jnp.exp2(parts[:, sub, 0].astype(F32) - 15.0)
     total = jnp.sum(parts[:, :sub].astype(F32) * back[:, None, None], 0)
     inverse_cols = lax.optimization_barrier((-total).astype(BF16))

time: 149 us -> 148 us (level)
    ppermute x2 -> x4, waiting for transfers between devices: 3.96 us -> 3.01 us  [the longest x2 3.01 us: shards(): other = [lax.ppermute(f, 'core', SWAP) for f in far]]
    ppermute x2 -> x4, starting transfers between devices: 5.24 us -> 4.85 us  [the longest x1 2.73 us: shards(): lax.ppermute(part(above3, num_y // 2), 'z', down)]
    pallas_call x4 -> x6, Pallas kernels: 11.2 us -> 11.3 us  [the longest x4 11.2 us: half_product(): pl.pallas_call(functools.partial(half_kernel, num, split, bool(more)), ou...]
  transfers between devices with their start and end apart: 10 -> 12, of which waited for: 4 -> 5; matrix products, arithmetic and copies ran while one was open for 0% -> 0% of each run, Pallas kernels for 11% -> 11%
where the time goes in v6:
time: 148 us
  blocking collectives  84.3 us (57%)
  starting transfers between devices  24.1 us (16%)
  Pallas kernels  20.1 us (14%)
  waiting for transfers between devices  12.5 us (8%)
  local copies, waits for them, and re-layouts  3.6 us (2%)
  other arithmetic  1.97 us (1%)
    all_to_all x1, blocking collectives, shards(): lax.all_to_all(add_pair(keep, got, parts, *other).astype(F16), ('xhi', 'y...  32.4 us
    all_to_all x1, blocking collectives, shards(): lax.all_to_all(pieces.reshape(num_y * 2, quarter, width), ('y', 'xlo'), 0...  15.2 us
    all_to_all x1, blocking collectives, shards(): lax.all_to_all(jnp.broadcast_to(mine, (num_z,) + mine.shape), 'z', 0, 0)  14.9 us
    all_to_all x1, blocking collectives, shards(): lax.all_to_all(jnp.broadcast_to(over_z, (8,) + over_z.shape), ALONG_X, 0, 0)  11.4 us
    pallas_call x4, Pallas kernels, half_product(): pl.pallas_call(functools.partial(half_kernel, num, split, bool(more)), ou...  11.2 us
    all_to_all x1, blocking collectives, shards(): mine = jnp.sum(lax.all_to_all(split, ALONG_X, 0, 0), 0)  10.5 us
    ppermute x1, waiting for transfers between devices, shards(): lax.ppermute(below, 'z', up)  5.7 us
    ppermute x2, starting transfers between devices, shards(): below, above = (lax.ppermute(own, 'z', up), lax.ppermute(own, 'z', down))  5.58 us
  transfers between devices with their start and end apart: 12, of which 5 were waited for; matrix products, arithmetic and copies ran while one was open for 0% of the time, Pallas kernels for 11%

profile of v6, /device:TPU:1, one launch (start us, length us, event | category | flops | bytes accessed | tf_op | source)
XLA Modules:
  0.0 147.9 jit_solution(7259387940319943488)
XLA Ops:
  1.1 1.9 %mask.1 = (bf16[4,2,128,256]{3,2,1,0:T(8,128)(2,1)}, bf16[512,256]{1,0:T(8,128)(2,1)}) custom-call(s32[1]{0:T(128)} %bitcast.place_ref, s32[1,128]{1,0:T(1,128)} %mask_ref.1, bf16[1,512,256]{2,1,0:T(8,128)(2,1)} %factor_ref.1), custom_call_target="tpu_custom_call" | custom-call | flops 131072 | bytes 1048576 | tf_op jit(solution)/shard_map/mask/pallas_call | solution.py:32
  3.0 15.2 %all_to_all.25 = bf16[8,128,256]{2,1,0:T(8,128)(2,1)S(1)} all-to-all(bf16[8,128,256]{2,1,0:T(8,128)(2,1)} %bitcast.29), channel_id=1, replica_groups=mesh['y'=4,'xlo'=2,'z'=8,'xhi'=2,'core'=2] {'y','xlo'}, dimensions={0} | all-to-all | bytes 1048576 | tf_op jit(solution)/shard_map/all_to_all | solution.py:196
  18.2 1.6 %collective-permute-start = (bf16[4,256,256]{2,1,0:T(8,128)(2,1)S(1)}, bf16[4,256,256]{2,1,0:T(8,128)(2,1)S(1)}, u32[]{:S(2)}, u32[]{:S(2)}) collective-permute-start(bf16[4,256,256]{2,1,0:T(8,128)(2,1)S(1)} %bitcast.22), channel_id=1, source_target_pairs={{0,4},{4,8},{8,12},{12,16},{16,20},{20,24},{24,28},{28,0},{1,5},{5... | collective-permute-start | bytes 1572872 | tf_op jit(solution)/shard_map/ppermute | solution.py:201
  19.8 3.9 %collective-permute-start.4 = (bf16[4,256,256]{2,1,0:T(8,128)(2,1)S(1)}, bf16[4,256,256]{2,1,0:T(8,128)(2,1)S(1)}, u32[]{:S(2)}, u32[]{:S(2)}) collective-permute-start(bf16[4,256,256]{2,1,0:T(8,128)(2,1)S(1)} %bitcast.23), channel_id=1, source_target_pairs={{0,28},{4,0},{8,4},{12,8},{16,12},{20,16},{24,20},{28,24},{1,29},{... | collective-permute-start | bytes 1572872 | tf_op jit(solution)/shard_map/ppermute | solution.py:201
  23.8 3.4 %copy-done = bf16[16,1,128,2048]{3,2,1,0:T(8,128)(2,1)S(1)} copy-done((bf16[16,1,128,2048]{3,2,1,0:T(8,128)(2,1)S(1)}, bf16[16,1,128,2048]{3,2,1,0:T(8,128)(2,1)}, u32[]{:S(2)}) %copy-start) | copy-done | bytes 8388632
  27.1 4.9 %turn.1.turned_ref = bf16[8,2048,256]{2,1,0:T(8,128)(2,1)S(1)} custom-call(bf16[2,8,128,2048]{3,2,1,0:T(8,128)(2,1)S(1)} %bitcast.21), custom_call_target="tpu_custom_call" | custom-call | bytes 16777216 | tf_op jit(solution)/shard_map/turn/pallas_call | solution.py:52
  32.0 2.1 %collective-permute-done.refs_1_ = bf16[4,256,256]{2,1,0:T(8,128)(2,1)S(1)} collective-permute-done((bf16[4,256,256]{2,1,0:T(8,128)(2,1)S(1)}, bf16[4,256,256]{2,1,0:T(8,128)(2,1)S(1)}, u32[]{:S(2)}, u32[]{:S(2)}) %collective-permute-start) | collective-permute-done | bytes 524320 | tf_op jit(solution)/shard_map/ppermute | solution.py:201
  34.1 2.7 %collective-permute-start.5 = (bf16[4,256,256]{2,1,0:T(8,128)(2,1)S(1)}, bf16[4,256,256]{2,1,0:T(8,128)(2,1)S(1)}, u32[]{:S(2)}, u32[]{:S(2)}) collective-permute-start(bf16[4,256,256]{2,1,0:T(8,128)(2,1)S(1)} %collective-permute-done.4.refs_2_), channel_id=1, source_target_pairs={{0,28},{4,0},{8,4},{12,8},{16,12},{20,16},{24,20},{28,24},{1,29},{... | collective-permute-start | bytes 1572872 | tf_op jit(solution)/shard_map/ppermute | solution.py:203
  36.8 0.6 pick.1
  37.4 3.2 %collective-permute-start.3 = (bf16[1,2,512,256]{3,2,1,0:T(8,128)(2,1)S(1)}, bf16[1,2,512,256]{3,2,1,0:T(8,128)(2,1)S(1)}, u32[]{:S(2)}, u32[]{:S(2)}) collective-permute-start(bf16[1,2,512,256]{3,2,1,0:T(8,128)(2,1)S(1)} %pick.1), channel_id=1, source_target_pairs={{0,1},{1,0},{2,3},{3,2},{4,5},{5,4},{6,7},{7,6},{8,9},{9,8},{10,11... | collective-permute-start | bytes 1572872 | tf_op jit(solution)/shard_map/ppermute | solution.py:204
  40.6 5.7 %collective-permute-done.1.refs_3_ = bf16[4,256,256]{2,1,0:T(8,128)(2,1)S(1)} collective-permute-done((bf16[4,256,256]{2,1,0:T(8,128)(2,1)S(1)}, bf16[4,256,256]{2,1,0:T(8,128)(2,1)S(1)}, u32[]{:S(2)}, u32[]{:S(2)}) %collective-permute-start.1) | collective-permute-done | bytes 524320 | tf_op jit(solution)/shard_map/ppermute | solution.py:203
  46.3 2.7 %collective-permute-start.6 = (bf16[4,256,256]{2,1,0:T(8,128)(2,1)S(1)}, bf16[4,256,256]{2,1,0:T(8,128)(2,1)S(1)}, u32[]{:S(2)}, u32[]{:S(2)}) collective-permute-start(bf16[4,256,256]{2,1,0:T(8,128)(2,1)S(1)} %collective-permute-done.5.refs_4_), channel_id=1, source_target_pairs={{0,28},{4,0},{8,4},{12,8},{16,12},{20,16},{24,20},{28,24},{1,29},{... | collective-permute-start | bytes 1572872 | tf_op jit(solution)/shard_map/ppermute | solution.py:205
  48.9 3.4 %half_product.5.refs_2_ = f32[4,2,512,256]{3,2,1,0:T(8,128)S(1)} custom-call(s32[6]{0:T(128)S(1)} %stack.64.where_ref, bf16[8,2048,256]{2,1,0:T(8,128)(2,1)S(1)} %turn.1.turned_ref, bf16[4,256,256]{2,1,0:T(8,128)(2,1)S(1)} %bitcast.24, bf16[4,256,256]{2,1,0:T(8,128)(2,1)S(1)} %collective-permute-done.refs_1_, ...), custom_call_target="tpu_custom_call" | custom-call | flops 26843545600 | bytes 26214400 | tf_op jit(solution)/shard_map/half_product/pallas_call | solution.py:131
  52.4 3.4 %half_product.4.refs_4_ = f32[4,2,512,256]{3,2,1,0:T(8,128)S(1)} custom-call(s32[6]{0:T(128)S(1)} %stack.71.where_ref, bf16[8,2048,256]{2,1,0:T(8,128)(2,1)S(1)} %turn.1.turned_ref, bf16[4,256,256]{2,1,0:T(8,128)(2,1)S(1)} %bitcast.25, bf16[4,256,256]{2,1,0:T(8,128)(2,1)S(1)} %collective-permute-done.refs_1_, ...), custom_call_target="tpu_custom_call" | custom-call | flops 26843545600 | bytes 26214400 | tf_op jit(solution)/shard_map/half_product/pallas_call | solution.py:131
  55.8 1.7 %collective-permute-done.2.rows_ref.refs_0_ = bf16[4,256,256]{2,1,0:T(8,128)(2,1)S(1)} collective-permute-done((bf16[4,256,256]{2,1,0:T(8,128)(2,1)S(1)}, bf16[4,256,256]{2,1,0:T(8,128)(2,1)S(1)}, u32[]{:S(2)}, u32[]{:S(2)}) %collective-permute-start.2) | collective-permute-done | bytes 524320 | tf_op jit(solution)/shard_map/ppermute | solution.py:205
  57.6 2.7 %collective-permute-start.8 = (bf16[2,256,256]{2,1,0:T(8,128)(2,1)S(1)}, bf16[2,256,256]{2,1,0:T(8,128)(2,1)S(1)}, u32[]{:S(2)}, u32[]{:S(2)}) collective-permute-start(bf16[2,256,256]{2,1,0:T(8,128)(2,1)S(1)} %part.3), channel_id=1, source_target_pairs={{0,28},{4,0},{8,4},{12,8},{16,12},{20,16},{24,20},{28,24},{1,29},{... | collective-permute-start | bytes 786440 | tf_op jit(solution)/shard_map/ppermute | solution.py:210
  60.3 1.9 %half_product.7 = f32[4,2,512,256]{3,2,1,0:T(8,128)S(1)} custom-call(s32[3]{0:T(128)S(1)} %pad_add_fusion.where_ref, bf16[8,2048,256]{2,1,0:T(8,128)(2,1)S(1)} %turn.1.turned_ref, bf16[4,256,256]{2,1,0:T(8,128)(2,1)S(1)} %collective-permute-done.2.rows_ref.refs_0_, ...), custom_call_target="tpu_custom_call", output_to_operand_aliasing={{}: (4, {})} | custom-call | flops 1073741824 | bytes 1048576 | tf_op jit(solution)/shard_map/half_product/pallas_call | solution.py:131
  62.3 5.2 %collective-permute-start.9 = (f32[4,2,512,256]{3,2,1,0:T(8,128)S(1)}, f32[4,2,512,256]{3,2,1,0:T(8,128)S(1)}, u32[]{:S(2)}, u32[]{:S(2)}) collective-permute-start(f32[4,2,512,256]{3,2,1,0:T(8,128)S(1)} %half_product.7), channel_id=1, source_target_pairs={{0,1},{1,0},{2,3},{3,2},{4,5},{5,4},{6,7},{7,6},{8,9},{9,8},{10,11... | collective-permute-start | bytes 12582920 | tf_op jit(solution)/shard_map/ppermute | solution.py:213
  67.5 2.0 %collective-permute-start.10 = (bf16[2,256,256]{2,1,0:T(8,128)(2,1)S(1)}, bf16[2,256,256]{2,1,0:T(8,128)(2,1)S(1)}, u32[]{:S(2)}, u32[]{:S(2)}) collective-permute-start(bf16[2,256,256]{2,1,0:T(8,128)(2,1)S(1)} %collective-permute-done.7.refs_2_), channel_id=1, source_target_pairs={{0,1},{1,0},{2,3},{3,2},{4,5},{5,4},{6,7},{7,6},{8,9},{9,8},{10,11... | collective-permute-start | bytes 786440 | tf_op jit(solution)/shard_map/ppermute | solution.py:214
  69.5 2.5 %half_product.6.keep_ref = f32[4,2,512,256]{3,2,1,0:T(8,128)S(1)} custom-call(s32[4]{0:T(128)S(1)} %pad_add_fusion.2.where_ref, bf16[8,2048,256]{2,1,0:T(8,128)(2,1)S(1)} %turn.1.turned_ref, bf16[4,256,256]{2,1,0:T(8,128)(2,1)S(1)} %collective-permute-done.2.rows_ref.refs_0_, ...), custom_call_target="tpu_custom_call", output_to_operand_aliasing={{}: (6, {})} | custom-call | flops 96636764160 | bytes 94371840 | tf_op jit(solution)/shard_map/half_product/pallas_call | solution.py:131
  72.0 2.6 %collective-permute-done.10.low_ref = bf16[2,256,256]{2,1,0:T(8,128)(2,1)S(1)} collective-permute-done((bf16[2,256,256]{2,1,0:T(8,128)(2,1)S(1)}, bf16[2,256,256]{2,1,0:T(8,128)(2,1)S(1)}, u32[]{:S(2)}, u32[]{:S(2)}) %collective-permute-start.10) | collective-permute-done | bytes 262176 | tf_op jit(solution)/shard_map/ppermute | solution.py:214
  74.6 0.4 collective-permute-done.11.high_ref
  75.0 1.5 %add_pair.1 = f32[8,528,256]{2,1,0:T(8,128)S(1)} custom-call(f32[4,2,512,256]{3,2,1,0:T(8,128)S(1)} %half_product.6.keep_ref, f32[4,2,512,256]{3,2,1,0:T(8,128)S(1)} %collective-permute-done.9.got_ref, bf16[1,2,512,256]{3,2,1,0:T(8,128)(2,1)S(1)} %collective-permute-done.3.parts_ref, bf16[2,256,256]{2,1,0:T(8,128)(2,1)S(1)} %collective-permute-done.10.low_ref, ...), custom_call_target="tpu_custom_call" | custom-call | flops 536870912 | bytes 12582912 | tf_op jit(solution)/shard_map/add_pair/pallas_call | solution.py:162
  76.5 0.3 convert_element_type.13
  76.8 32.4 %all_to_all.26 = f16[8,528,256]{2,1,0:T(8,128)(2,1)S(1)} all-to-all(f16[8,528,256]{2,1,0:T(8,128)(2,1)S(1)} %convert_element_type.13), channel_id=1, replica_groups=mesh['y'=4,'xlo'=2,'z'=8,'xhi'=2,'core'=2] {'xhi','y'}, dimensions={0} | all-to-all | bytes 4325376 | tf_op jit(solution)/shard_map/all_to_all | solution.py:217
  109.2 0.2 fusion.3
  109.4 0.5 multiply_reduce_fusion
  110.0 0.3 fusion.4
  110.2 10.5 %all_to_all.27 = f32[8,32,256]{2,1,0:T(8,128)S(1)} all-to-all(f32[8,32,256]{2,1,0:T(8,128)S(1)} %bitcast.27), channel_id=1, replica_groups=mesh['y'=4,'xlo'=2,'z'=8,'xhi'=2,'core'=2] {'xlo','xhi','core'}, dimensions={0} | all-to-all | bytes 524288 | tf_op jit(solution)/shard_map/all_to_all | solution.py:224
  120.8 14.9 %all_to_all.28 = f32[8,32,256]{2,1,0:T(8,128)S(1)} all-to-all(f32[8,32,256]{2,1,0:T(8,128)S(1)} %broadcast_in_dim.11), channel_id=1, replica_groups=mesh['y'=4,'xlo'=2,'z'=8,'xhi'=2,'core'=2] {'z'}, dimensions={0} | all-to-all | bytes 524288 | tf_op jit(solution)/shard_map/all_to_all | solution.py:225
  135.7 11.4 %all_to_all.29 = f32[8,32,256]{2,1,0:T(8,128)S(1)} all-to-all(f32[8,32,256]{2,1,0:T(8,128)S(1)} %broadcast_in_dim.12), channel_id=1, replica_groups=mesh['y'=4,'xlo'=2,'z'=8,'xhi'=2,'core'=2] {'xlo','xhi','core'}, dimensions={0} | all-to-all | bytes 524288 | tf_op jit(solution)/shard_map/all_to_all | solution.py:226
  147.1 0.7 bitcast_subtract_fusion
  (30 shorter events, 0.7 us)
Async XLA Ops:
  18.2 15.9 %collective-permute-start = (bf16[4,256,256]{2,1,0:T(8,128)(2,1)S(1)}, bf16[4,256,256]{2,1,0:T(8,128)(2,1)S(1)}, u32[]{:S(2)}, u32[]{:S(2)}) collective-permute-start(bf16[4,256,256]{2,1,0:T(8,128)(2,1)S(1)} %bitcast.22), channel_id=1, source_target_pairs={{0,4},{4,8},{8,12},{12,16},{16,20},{20,24},{24,28},{28,0},{1,5},{5... | collective-permute-start | bytes 1572872 | tf_op jit(solution)/shard_map/ppermute | solution.py:201
  19.8 14.3 %collective-permute-start.4 = (bf16[4,256,256]{2,1,0:T(8,128)(2,1)S(1)}, bf16[4,256,256]{2,1,0:T(8,128)(2,1)S(1)}, u32[]{:S(2)}, u32[]{:S(2)}) collective-permute-start(bf16[4,256,256]{2,1,0:T(8,128)(2,1)S(1)} %bitcast.23), channel_id=1, source_target_pairs={{0,28},{4,0},{8,4},{12,8},{16,12},{20,16},{24,20},{28,24},{1,29},{... | collective-permute-start | bytes 1572872 | tf_op jit(solution)/shard_map/ppermute | solution.py:201
  23.8 3.4 %copy-start = (bf16[16,1,128,2048]{3,2,1,0:T(8,128)(2,1)S(1)}, bf16[16,1,128,2048]{3,2,1,0:T(8,128)(2,1)}, u32[]{:S(2)}) copy-start(bf16[16,1,128,2048]{3,2,1,0:T(8,128)(2,1)} %param.4) | copy-start | bytes 25165828
  34.1 12.1 %collective-permute-start.1 = (bf16[4,256,256]{2,1,0:T(8,128)(2,1)S(1)}, bf16[4,256,256]{2,1,0:T(8,128)(2,1)S(1)}, u32[]{:S(2)}, u32[]{:S(2)}) collective-permute-start(bf16[4,256,256]{2,1,0:T(8,128)(2,1)S(1)} %collective-permute-done.refs_1_), channel_id=1, source_target_pairs={{0,4},{4,8},{8,12},{12,16},{16,20},{20,24},{24,28},{28,0},{1,5},{5... | collective-permute-start | bytes 1572872 | tf_op jit(solution)/shard_map/ppermute | solution.py:203
  34.1 12.1 %collective-permute-start.5 = (bf16[4,256,256]{2,1,0:T(8,128)(2,1)S(1)}, bf16[4,256,256]{2,1,0:T(8,128)(2,1)S(1)}, u32[]{:S(2)}, u32[]{:S(2)}) collective-permute-start(bf16[4,256,256]{2,1,0:T(8,128)(2,1)S(1)} %collective-permute-done.4.refs_2_), channel_id=1, source_target_pairs={{0,28},{4,0},{8,4},{12,8},{16,12},{20,16},{24,20},{28,24},{1,29},{... | collective-permute-start | bytes 1572872 | tf_op jit(solution)/shard_map/ppermute | solution.py:203
  37.4 18.4 %collective-permute-start.3 = (bf16[1,2,512,256]{3,2,1,0:T(8,128)(2,1)S(1)}, bf16[1,2,512,256]{3,2,1,0:T(8,128)(2,1)S(1)}, u32[]{:S(2)}, u32[]{:S(2)}) collective-permute-start(bf16[1,2,512,256]{3,2,1,0:T(8,128)(2,1)S(1)} %pick.1), channel_id=1, source_target_pairs={{0,1},{1,0},{2,3},{3,2},{4,5},{5,4},{6,7},{7,6},{8,9},{9,8},{10,11... | collective-permute-start | bytes 1572872 | tf_op jit(solution)/shard_map/ppermute | solution.py:204
  46.3 11.2 %collective-permute-start.2 = (bf16[4,256,256]{2,1,0:T(8,128)(2,1)S(1)}, bf16[4,256,256]{2,1,0:T(8,128)(2,1)S(1)}, u32[]{:S(2)}, u32[]{:S(2)}) collective-permute-start(bf16[4,256,256]{2,1,0:T(8,128)(2,1)S(1)} %collective-permute-done.1.refs_3_), channel_id=1, source_target_pairs={{0,4},{4,8},{8,12},{12,16},{16,20},{20,24},{24,28},{28,0},{1,5},{5... | collective-permute-start | bytes 1572872 | tf_op jit(solution)/shard_map/ppermute | solution.py:205
  46.3 11.3 %collective-permute-start.6 = (bf16[4,256,256]{2,1,0:T(8,128)(2,1)S(1)}, bf16[4,256,256]{2,1,0:T(8,128)(2,1)S(1)}, u32[]{:S(2)}, u32[]{:S(2)}) collective-permute-start(bf16[4,256,256]{2,1,0:T(8,128)(2,1)S(1)} %collective-permute-done.5.refs_4_), channel_id=1, source_target_pairs={{0,28},{4,0},{8,4},{12,8},{16,12},{20,16},{24,20},{28,24},{1,29},{... | collective-permute-start | bytes 1572872 | tf_op jit(solution)/shard_map/ppermute | solution.py:205
  57.5 10.0 %collective-permute-start.7 = (bf16[2,256,256]{2,1,0:T(8,128)(2,1)S(1)}, bf16[2,256,256]{2,1,0:T(8,128)(2,1)S(1)}, u32[]{:S(2)}, u32[]{:S(2)}) collective-permute-start(bf16[2,256,256]{2,1,0:T(8,128)(2,1)S(1)} %part.2), channel_id=1, source_target_pairs={{0,4},{4,8},{8,12},{12,16},{16,20},{20,24},{24,28},{28,0},{1,5},{5... | collective-permute-start | bytes 786440 | tf_op jit(solution)/shard_map/ppermute | solution.py:210
  57.6 11.9 %collective-permute-start.8 = (bf16[2,256,256]{2,1,0:T(8,128)(2,1)S(1)}, bf16[2,256,256]{2,1,0:T(8,128)(2,1)S(1)}, u32[]{:S(2)}, u32[]{:S(2)}) collective-permute-start(bf16[2,256,256]{2,1,0:T(8,128)(2,1)S(1)} %part.3), channel_id=1, source_target_pairs={{0,28},{4,0},{8,4},{12,8},{16,12},{20,16},{24,20},{28,24},{1,29},{... | collective-permute-start | bytes 786440 | tf_op jit(solution)/shard_map/ppermute | solution.py:210
  62.3 12.7 %collective-permute-start.9 = (f32[4,2,512,256]{3,2,1,0:T(8,128)S(1)}, f32[4,2,512,256]{3,2,1,0:T(8,128)S(1)}, u32[]{:S(2)}, u32[]{:S(2)}) collective-permute-start(f32[4,2,512,256]{3,2,1,0:T(8,128)S(1)} %half_product.7), channel_id=1, source_target_pairs={{0,1},{1,0},{2,3},{3,2},{4,5},{5,4},{6,7},{7,6},{8,9},{9,8},{10,11... | collective-permute-start | bytes 12582920 | tf_op jit(solution)/shard_map/ppermute | solution.py:213
  67.5 7.2 %collective-permute-start.10 = (bf16[2,256,256]{2,1,0:T(8,128)(2,1)S(1)}, bf16[2,256,256]{2,1,0:T(8,128)(2,1)S(1)}, u32[]{:S(2)}, u32[]{:S(2)}) collective-permute-start(bf16[2,256,256]{2,1,0:T(8,128)(2,1)S(1)} %collective-permute-done.7.refs_2_), channel_id=1, source_target_pairs={{0,1},{1,0},{2,3},{3,2},{4,5},{5,4},{6,7},{7,6},{8,9},{9,8},{10,11... | collective-permute-start | bytes 786440 | tf_op jit(solution)/shard_map/ppermute | solution.py:214
  69.5 5.5 %collective-permute-start.11 = (bf16[2,256,256]{2,1,0:T(8,128)(2,1)S(1)}, bf16[2,256,256]{2,1,0:T(8,128)(2,1)S(1)}, u32[]{:S(2)}, u32[]{:S(2)}) collective-permute-start(bf16[2,256,256]{2,1,0:T(8,128)(2,1)S(1)} %collective-permute-done.8.refs_3_), channel_id=1, source_target_pairs={{0,1},{1,0},{2,3},{3,2},{4,5},{5,4},{6,7},{7,6},{8,9},{9,8},{10,11... | collective-permute-start | bytes 786440 | tf_op jit(solution)/shard_map/ppermute | solution.py:214
  76.8 33.1 %copy-start.3 = (bf16[512,256]{1,0:T(8,128)(2,1)S(1)}, bf16[512,256]{1,0:T(8,128)(2,1)}, u32[]{:S(2)}) copy-start(bf16[512,256]{1,0:T(8,128)(2,1)} %get-tuple-element.29) | copy-start | bytes 786436
  109.2 37.9 %copy-start.2 = (f32[1,256,256]{2,1,0:T(8,128)S(1)}, f32[1,256,256]{2,1,0:T(8,128)}, u32[]{:S(2)}) copy-start(f32[1,256,256]{2,1,0:T(8,128)} %param.7) | copy-start | bytes 786436
  109.9 37.9 %copy-start.1 = (bf16[512,256]{1,0:T(8,128)(2,1)}, bf16[512,256]{1,0:T(8,128)(2,1)S(1)}, u32[]{:S(2)}) copy-start(bf16[512,256]{1,0:T(8,128)(2,1)S(1)} %negate_convert_fusion) | copy-start | bytes 786436

commit v7 on v5

--- a/solution.py
+++ b/solution.py
@@ -197,10 +197,16 @@
     inverse_cols = lax.optimization_barrier((-total).astype(BF16))
 
     product = jnp.einsum("jw,jv->wv", masked, inverse_cols, preferred_element_type=F32)
-    split = product.reshape(8, width // 8, width)
-    mine = jnp.sum(lax.all_to_all(split, ALONG_X, 0, 0), 0)
+    halves = product.reshape(2, width // 2, width)
+    mine = lax.dynamic_index_in_dim(halves, core, 0, keepdims=False)
+    give = lax.dynamic_index_in_dim(halves, 1 - core, 0, keepdims=False)
+    mine = mine + lax.ppermute(give, "core", SWAP)
+    mine = jnp.sum(lax.all_to_all(mine.reshape(4, width // 8, width), ("xlo", "xhi"), 0, 0), 0)
     over_z = jnp.sum(lax.all_to_all(jnp.broadcast_to(mine, (num_z,) + mine.shape), "z", 0, 0), 0)
-    whole = lax.all_to_all(jnp.broadcast_to(over_z, (8,) + over_z.shape), ALONG_X, 0, 0)
+    half = lax.all_to_all(jnp.broadcast_to(over_z, (4,) + over_z.shape), ("xlo", "xhi"), 0, 0)
+    half = half.reshape(width // 2, width)
+    rest = lax.ppermute(half, "core", SWAP)
+    whole = jnp.where(core == 0, jnp.concatenate([half, rest], 0), jnp.concatenate([rest, half], 0))
     return inverse_cols[None], diag_inverse - whole.reshape(1, width, width)
 
 

time: 149 us -> 149 us (level)
  blocking collectives: 84.2 us -> 44.2 us
  waiting for transfers between devices: 13.4 us -> 42.4 us
  starting transfers between devices: 23.8 us -> 33.8 us
    all_to_all x3 -> x2, blocking collectives: 54.3 us -> 15.3 us  [the longest x1 7.91 us: shards(): lax.all_to_all(mine.reshape(4, width // 8, width), ('xlo', 'xhi'), 0, 0)]
    all_to_all x0 -> x1, waiting for transfers between devices: none -> 26.9 us  [shards(): lax.all_to_all(add_pair(keep, got, parts, far_other).astype(F16), ('xhi',...]
    ppermute x0 -> x2, starting transfers between devices: none -> 5.93 us  [the longest x1 4.72 us: shards(): rest = lax.ppermute(half, 'core', SWAP)]
    all_to_all x0 -> x1, starting transfers between devices: none -> 4.11 us  [shards(): lax.all_to_all(add_pair(keep, got, parts, far_other).astype(F16), ('xhi',...]
    ppermute x0 -> x2, waiting for transfers between devices: none -> 1.97 us  [the longest x1 0.99 us: shards(): mine = mine + lax.ppermute(give, 'core', SWAP)]
  transfers between devices with their start and end apart: 10 -> 13, of which waited for: 4 -> 7; matrix products, arithmetic and copies ran while one was open for 0% -> 0% of each run, Pallas kernels for 11% -> 11%
where the time goes in v7:
time: 149 us
  blocking collectives  44.2 us (30%)
  waiting for transfers between devices  42.4 us (28%)
  starting transfers between devices  33.8 us (23%)
  Pallas kernels  20.1 us (13%)
  local copies, waits for them, and re-layouts  3.61 us (2%)
  other arithmetic  3.32 us (2%)
    all_to_all x1, waiting for transfers between devices, shards(): lax.all_to_all(add_pair(keep, got, parts, far_other).astype(F16), ('xhi',...  26.9 us
    all_to_all x1, blocking collectives, shards(): lax.all_to_all(pieces.reshape(num_y * 2, quarter, width), ('y', 'xlo'), 0...  15.2 us
    all_to_all x1, blocking collectives, shards(): lax.all_to_all(jnp.broadcast_to(mine, (num_z,) + mine.shape), 'z', 0, 0)  13.7 us
    pallas_call x4, Pallas kernels, half_product(): pl.pallas_call(functools.partial(half_kernel, num, spare, bool(more)), ou...  11.2 us
    all_to_all x1, blocking collectives, shards(): lax.all_to_all(mine.reshape(4, width // 8, width), ('xlo', 'xhi'), 0, 0)  7.91 us
    all_to_all x1, blocking collectives, shards(): lax.all_to_all(jnp.broadcast_to(over_z, (4,) + over_z.shape), ('xlo', 'xh...  7.44 us
    ppermute x1, waiting for transfers between devices, shards(): lax.ppermute(below, 'z', up)  5.7 us
    ppermute x2, starting transfers between devices, shards(): below, above = (lax.ppermute(own, 'z', up), lax.ppermute(own, 'z', down))  5.58 us
  transfers between devices with their start and end apart: 13, of which 7 were waited for; matrix products, arithmetic and copies ran while one was open for 0% of the time, Pallas kernels for 11%

profile of v7, /device:TPU:1, one launch (start us, length us, event | category | flops | bytes accessed | tf_op | source)
XLA Modules:
  0.0 148.6 jit_solution(4506257373853545960)
XLA Ops:
  1.1 1.9 %mask.1 = (bf16[4,2,128,256]{3,2,1,0:T(8,128)(2,1)}, bf16[512,256]{1,0:T(8,128)(2,1)}) custom-call(s32[1]{0:T(128)} %bitcast.place_ref, s32[1,128]{1,0:T(1,128)} %mask_ref.1, bf16[1,512,256]{2,1,0:T(8,128)(2,1)} %factor_ref.1), custom_call_target="tpu_custom_call" | custom-call | flops 131072 | bytes 1048576 | tf_op jit(solution)/shard_map/mask/pallas_call | solution.py:32
  3.0 15.2 %all_to_all.25 = bf16[8,128,256]{2,1,0:T(8,128)(2,1)S(1)} all-to-all(bf16[8,128,256]{2,1,0:T(8,128)(2,1)} %bitcast.34), channel_id=1, replica_groups=mesh['y'=4,'xlo'=2,'z'=8,'xhi'=2,'core'=2] {'y','xlo'}, dimensions={0} | all-to-all | bytes 1048576 | tf_op jit(solution)/shard_map/all_to_all | solution.py:173
  18.2 1.6 %collective-permute-start = (bf16[4,256,256]{2,1,0:T(8,128)(2,1)S(1)}, bf16[4,256,256]{2,1,0:T(8,128)(2,1)S(1)}, u32[]{:S(2)}, u32[]{:S(2)}) collective-permute-start(bf16[4,256,256]{2,1,0:T(8,128)(2,1)S(1)} %bitcast.27), channel_id=1, source_target_pairs={{0,4},{4,8},{8,12},{12,16},{16,20},{20,24},{24,28},{28,0},{1,5},{5... | collective-permute-start | bytes 1572872 | tf_op jit(solution)/shard_map/ppermute | solution.py:178
  19.8 3.9 %collective-permute-start.4 = (bf16[4,256,256]{2,1,0:T(8,128)(2,1)S(1)}, bf16[4,256,256]{2,1,0:T(8,128)(2,1)S(1)}, u32[]{:S(2)}, u32[]{:S(2)}) collective-permute-start(bf16[4,256,256]{2,1,0:T(8,128)(2,1)S(1)} %bitcast.28), channel_id=1, source_target_pairs={{0,28},{4,0},{8,4},{12,8},{16,12},{20,16},{24,20},{28,24},{1,29},{... | collective-permute-start | bytes 1572872 | tf_op jit(solution)/shard_map/ppermute | solution.py:178
  23.8 3.4 %copy-done = bf16[16,1,128,2048]{3,2,1,0:T(8,128)(2,1)S(1)} copy-done((bf16[16,1,128,2048]{3,2,1,0:T(8,128)(2,1)S(1)}, bf16[16,1,128,2048]{3,2,1,0:T(8,128)(2,1)}, u32[]{:S(2)}) %copy-start) | copy-done | bytes 8388632
  27.2 4.9 %turn.1.turned_ref = bf16[8,2048,256]{2,1,0:T(8,128)(2,1)S(1)} custom-call(bf16[2,8,128,2048]{3,2,1,0:T(8,128)(2,1)S(1)} %bitcast.26), custom_call_target="tpu_custom_call" | custom-call | bytes 16777216 | tf_op jit(solution)/shard_map/turn/pallas_call | solution.py:52
  32.0 2.1 %collective-permute-done.refs_1_ = bf16[4,256,256]{2,1,0:T(8,128)(2,1)S(1)} collective-permute-done((bf16[4,256,256]{2,1,0:T(8,128)(2,1)S(1)}, bf16[4,256,256]{2,1,0:T(8,128)(2,1)S(1)}, u32[]{:S(2)}, u32[]{:S(2)}) %collective-permute-start) | collective-permute-done | bytes 524320 | tf_op jit(solution)/shard_map/ppermute | solution.py:178
  34.1 2.7 %collective-permute-start.5 = (bf16[4,256,256]{2,1,0:T(8,128)(2,1)S(1)}, bf16[4,256,256]{2,1,0:T(8,128)(2,1)S(1)}, u32[]{:S(2)}, u32[]{:S(2)}) collective-permute-start(bf16[4,256,256]{2,1,0:T(8,128)(2,1)S(1)} %collective-permute-done.4.refs_2_), channel_id=1, source_target_pairs={{0,28},{4,0},{8,4},{12,8},{16,12},{20,16},{24,20},{28,24},{1,29},{... | collective-permute-start | bytes 1572872 | tf_op jit(solution)/shard_map/ppermute | solution.py:180
  36.8 0.6 pick.1
  37.4 3.2 %collective-permute-start.3 = (bf16[1,2,512,256]{3,2,1,0:T(8,128)(2,1)S(1)}, bf16[1,2,512,256]{3,2,1,0:T(8,128)(2,1)S(1)}, u32[]{:S(2)}, u32[]{:S(2)}) collective-permute-start(bf16[1,2,512,256]{3,2,1,0:T(8,128)(2,1)S(1)} %pick.1), channel_id=1, source_target_pairs={{0,1},{1,0},{2,3},{3,2},{4,5},{5,4},{6,7},{7,6},{8,9},{9,8},{10,11... | collective-permute-start | bytes 1572872 | tf_op jit(solution)/shard_map/ppermute | solution.py:181
  40.6 5.7 %collective-permute-done.1.refs_3_ = bf16[4,256,256]{2,1,0:T(8,128)(2,1)S(1)} collective-permute-done((bf16[4,256,256]{2,1,0:T(8,128)(2,1)S(1)}, bf16[4,256,256]{2,1,0:T(8,128)(2,1)S(1)}, u32[]{:S(2)}, u32[]{:S(2)}) %collective-permute-start.1) | collective-permute-done | bytes 524320 | tf_op jit(solution)/shard_map/ppermute | solution.py:180
  46.3 2.7 %collective-permute-start.6 = (bf16[4,256,256]{2,1,0:T(8,128)(2,1)S(1)}, bf16[4,256,256]{2,1,0:T(8,128)(2,1)S(1)}, u32[]{:S(2)}, u32[]{:S(2)}) collective-permute-start(bf16[4,256,256]{2,1,0:T(8,128)(2,1)S(1)} %collective-permute-done.5.refs_4_), channel_id=1, source_target_pairs={{0,28},{4,0},{8,4},{12,8},{16,12},{20,16},{24,20},{28,24},{1,29},{... | collective-permute-start | bytes 1572872 | tf_op jit(solution)/shard_map/ppermute | solution.py:182
  48.9 3.4 %half_product.5.refs_2_ = f32[4,2,512,256]{3,2,1,0:T(8,128)S(1)} custom-call(s32[6]{0:T(128)S(1)} %stack.64.where_ref, bf16[8,2048,256]{2,1,0:T(8,128)(2,1)S(1)} %turn.1.turned_ref, bf16[4,256,256]{2,1,0:T(8,128)(2,1)S(1)} %bitcast.29, bf16[4,256,256]{2,1,0:T(8,128)(2,1)S(1)} %collective-permute-done.refs_1_, ...), custom_call_target="tpu_custom_call" | custom-call | flops 26843545600 | bytes 26214400 | tf_op jit(solution)/shard_map/half_product/pallas_call | solution.py:108
  52.4 3.4 %half_product.4.refs_3_ = f32[4,2,512,256]{3,2,1,0:T(8,128)S(1)} custom-call(s32[6]{0:T(128)S(1)} %stack.71.where_ref, bf16[8,2048,256]{2,1,0:T(8,128)(2,1)S(1)} %turn.1.turned_ref, bf16[4,256,256]{2,1,0:T(8,128)(2,1)S(1)} %bitcast.30, bf16[4,256,256]{2,1,0:T(8,128)(2,1)S(1)} %collective-permute-done.refs_1_, ...), custom_call_target="tpu_custom_call" | custom-call | flops 26843545600 | bytes 26214400 | tf_op jit(solution)/shard_map/half_product/pallas_call | solution.py:108
  55.8 1.7 %collective-permute-done.2.refs_0_ = bf16[4,256,256]{2,1,0:T(8,128)(2,1)S(1)} collective-permute-done((bf16[4,256,256]{2,1,0:T(8,128)(2,1)S(1)}, bf16[4,256,256]{2,1,0:T(8,128)(2,1)S(1)}, u32[]{:S(2)}, u32[]{:S(2)}) %collective-permute-start.2) | collective-permute-done | bytes 524320 | tf_op jit(solution)/shard_map/ppermute | solution.py:182
  57.5 1.9 %half_product.7 = f32[4,2,512,256]{3,2,1,0:T(8,128)S(1)} custom-call(s32[3]{0:T(128)S(1)} %pad_add_fusion.where_ref, bf16[8,2048,256]{2,1,0:T(8,128)(2,1)S(1)} %turn.1.turned_ref, bf16[4,256,256]{2,1,0:T(8,128)(2,1)S(1)} %collective-permute-done.2.refs_0_, bf16[4,256,256]{2,1,0:T(8,128)(2,1)S(1)} %collective-permute-done.6.refs_1_, ...), custom_call_target="tpu_custom_call", output_to_operand_aliasing={{}: (4, {})} | custom-call | flops 1073741824 | bytes 1048576 | tf_op jit(solution)/shard_map/half_product/pallas_call | solution.py:108
  59.4 4.4 %collective-permute-start.8 = (f32[4,2,512,256]{3,2,1,0:T(8,128)S(1)}, f32[4,2,512,256]{3,2,1,0:T(8,128)S(1)}, u32[]{:S(2)}, u32[]{:S(2)}) collective-permute-start(f32[4,2,512,256]{3,2,1,0:T(8,128)S(1)} %half_product.7), channel_id=1, source_target_pairs={{0,1},{1,0},{2,3},{3,2},{4,5},{5,4},{6,7},{7,6},{8,9},{9,8},{10,11... | collective-permute-start | bytes 12582920 | tf_op jit(solution)/shard_map/ppermute | solution.py:190
  63.8 4.0 %collective-permute-done.7.refs_2_ = bf16[4,256,256]{2,1,0:T(8,128)(2,1)S(1)} collective-permute-done((bf16[4,256,256]{2,1,0:T(8,128)(2,1)S(1)}, bf16[4,256,256]{2,1,0:T(8,128)(2,1)S(1)}, u32[]{:S(2)}, u32[]{:S(2)}) %collective-permute-start.7) | collective-permute-done | bytes 524320 | tf_op jit(solution)/shard_map/ppermute | solution.py:187
  67.8 5.2 %collective-permute-start.9 = (bf16[4,256,256]{2,1,0:T(8,128)(2,1)S(1)}, bf16[4,256,256]{2,1,0:T(8,128)(2,1)S(1)}, u32[]{:S(2)}, u32[]{:S(2)}) collective-permute-start(bf16[4,256,256]{2,1,0:T(8,128)(2,1)S(1)} %collective-permute-done.7.refs_2_), channel_id=1, source_target_pairs={{0,1},{1,0},{2,3},{3,2},{4,5},{5,4},{6,7},{7,6},{8,9},{9,8},{10,11... | collective-permute-start | bytes 1572872 | tf_op jit(solution)/shard_map/ppermute | solution.py:191
  73.0 2.5 %half_product.6.keep_ref = f32[4,2,512,256]{3,2,1,0:T(8,128)S(1)} custom-call(s32[4]{0:T(128)S(1)} %pad_add_fusion.2.where_ref, bf16[8,2048,256]{2,1,0:T(8,128)(2,1)S(1)} %turn.1.turned_ref, bf16[4,256,256]{2,1,0:T(8,128)(2,1)S(1)} %collective-permute-done.2.refs_0_, ...), custom_call_target="tpu_custom_call", output_to_operand_aliasing={{}: (5, {})} | custom-call | flops 96636764160 | bytes 94371840 | tf_op jit(solution)/shard_map/half_product/pallas_call | solution.py:108
  75.5 1.5 %add_pair.1 = f32[8,528,256]{2,1,0:T(8,128)S(1)} custom-call(f32[4,2,512,256]{3,2,1,0:T(8,128)S(1)} %half_product.6.keep_ref, f32[4,2,512,256]{3,2,1,0:T(8,128)S(1)} %collective-permute-done.8.got_ref, bf16[1,2,512,256]{3,2,1,0:T(8,128)(2,1)S(1)} %collective-permute-done.3.parts_ref, bf16[4,256,256]{2,1,0:T(8,128)(2,1)S(1)} %collective-permute-done.9.rows_ref), custom_call_target="tpu_custom_call" | custom-call | flops 536870912 | bytes 12582912 | tf_op jit(solution)/shard_map/add_pair/pallas_call | solution.py:139
  77.1 1.6 %convert_element_type.13 = f16[8,528,256]{2,1,0:T(8,128)(2,1)} convert(f32[8,528,256]{2,1,0:T(8,128)S(1)} %add_pair.1) | non-fusion elementwise | flops 1081344 | bytes 6488064 | tf_op jit(solution)/shard_map/convert_element_type | solution.py:194
  78.7 4.1 %all-to-all-start.1 = ((f16[8,528,256]{2,1,0:T(8,128)(2,1)}), f16[8,528,256]{2,1,0:T(8,128)(2,1)S(1)}, u32[]{:S(2)}, u32[]{:S(2)}) async-start(f16[8,528,256]{2,1,0:T(8,128)(2,1)} %convert_element_type.13), calls=%async_computation.1 | async-start | bytes 4325376 | tf_op jit(solution)/shard_map/all_to_all | solution.py:194
  82.8 26.9 %all-to-all-done.1 = f16[8,528,256]{2,1,0:T(8,128)(2,1)S(1)} async-done(((f16[8,528,256]{2,1,0:T(8,128)(2,1)}), f16[8,528,256]{2,1,0:T(8,128)(2,1)S(1)}, u32[]{:S(2)}, u32[]{:S(2)}) %all-to-all-start.1) | async-done | bytes 2162720 | tf_op jit(solution)/shard_map/all_to_all | solution.py:194
  110.8 1.2 collective-permute-start.10
  112.0 1.0 collective-permute-done.10
  113.0 7.9 %all_to_all.26 = f32[4,32,256]{2,1,0:T(8,128)S(1)} all-to-all(f32[4,32,256]{2,1,0:T(8,128)S(1)} %bitcast.35), channel_id=1, replica_groups=mesh['y'=4,'xlo'=2,'z'=8,'xhi'=2,'core'=2] {'xlo','xhi'}, dimensions={0} | all-to-all | bytes 262144 | tf_op jit(solution)/shard_map/all_to_all | solution.py:204
  121.0 13.7 %all_to_all.27 = f32[8,32,256]{2,1,0:T(8,128)S(1)} all-to-all(f32[8,32,256]{2,1,0:T(8,128)S(1)} %broadcast_in_dim.11), channel_id=1, replica_groups=mesh['y'=4,'xlo'=2,'z'=8,'xhi'=2,'core'=2] {'z'}, dimensions={0} | all-to-all | bytes 524288 | tf_op jit(solution)/shard_map/all_to_all | solution.py:205
  134.7 7.4 %all_to_all.28 = f32[4,32,256]{2,1,0:T(8,128)S(1)} all-to-all(f32[4,32,256]{2,1,0:T(8,128)S(1)} %broadcast_in_dim.12), channel_id=1, replica_groups=mesh['y'=4,'xlo'=2,'z'=8,'xhi'=2,'core'=2] {'xlo','xhi'}, dimensions={0} | all-to-all | bytes 262144 | tf_op jit(solution)/shard_map/all_to_all | solution.py:206
  142.1 4.7 %collective-permute-start.11 = (f32[128,256]{1,0:T(8,128)S(1)}, f32[128,256]{1,0:T(8,128)S(1)}, u32[]{:S(2)}, u32[]{:S(2)}) collective-permute-start(f32[128,256]{1,0:T(8,128)S(1)} %bitcast.36), channel_id=1, source_target_pairs={{0,1},{1,0},{2,3},{3,2},{4,5},{5,4},{6,7},{7,6},{8,9},{9,8},{10,11... | collective-permute-start | bytes 393224 | tf_op jit(solution)/shard_map/ppermute | solution.py:208
  146.9 1.0 collective-permute-done.11
  147.8 0.7 fusion
  (31 shorter events, 1.5 us)
Async XLA Ops:
  18.2 15.9 %collective-permute-start = (bf16[4,256,256]{2,1,0:T(8,128)(2,1)S(1)}, bf16[4,256,256]{2,1,0:T(8,128)(2,1)S(1)}, u32[]{:S(2)}, u32[]{:S(2)}) collective-permute-start(bf16[4,256,256]{2,1,0:T(8,128)(2,1)S(1)} %bitcast.27), channel_id=1, source_target_pairs={{0,4},{4,8},{8,12},{12,16},{16,20},{20,24},{24,28},{28,0},{1,5},{5... | collective-permute-start | bytes 1572872 | tf_op jit(solution)/shard_map/ppermute | solution.py:178
  19.8 14.3 %collective-permute-start.4 = (bf16[4,256,256]{2,1,0:T(8,128)(2,1)S(1)}, bf16[4,256,256]{2,1,0:T(8,128)(2,1)S(1)}, u32[]{:S(2)}, u32[]{:S(2)}) collective-permute-start(bf16[4,256,256]{2,1,0:T(8,128)(2,1)S(1)} %bitcast.28), channel_id=1, source_target_pairs={{0,28},{4,0},{8,4},{12,8},{16,12},{20,16},{24,20},{28,24},{1,29},{... | collective-permute-start | bytes 1572872 | tf_op jit(solution)/shard_map/ppermute | solution.py:178
  23.8 3.4 %copy-start = (bf16[16,1,128,2048]{3,2,1,0:T(8,128)(2,1)S(1)}, bf16[16,1,128,2048]{3,2,1,0:T(8,128)(2,1)}, u32[]{:S(2)}) copy-start(bf16[16,1,128,2048]{3,2,1,0:T(8,128)(2,1)} %param.4) | copy-start | bytes 25165828
  34.1 12.1 %collective-permute-start.1 = (bf16[4,256,256]{2,1,0:T(8,128)(2,1)S(1)}, bf16[4,256,256]{2,1,0:T(8,128)(2,1)S(1)}, u32[]{:S(2)}, u32[]{:S(2)}) collective-permute-start(bf16[4,256,256]{2,1,0:T(8,128)(2,1)S(1)} %collective-permute-done.refs_1_), channel_id=1, source_target_pairs={{0,4},{4,8},{8,12},{12,16},{16,20},{20,24},{24,28},{28,0},{1,5},{5... | collective-permute-start | bytes 1572872 | tf_op jit(solution)/shard_map/ppermute | solution.py:180
  34.1 12.1 %collective-permute-start.5 = (bf16[4,256,256]{2,1,0:T(8,128)(2,1)S(1)}, bf16[4,256,256]{2,1,0:T(8,128)(2,1)S(1)}, u32[]{:S(2)}, u32[]{:S(2)}) collective-permute-start(bf16[4,256,256]{2,1,0:T(8,128)(2,1)S(1)} %collective-permute-done.4.refs_2_), channel_id=1, source_target_pairs={{0,28},{4,0},{8,4},{12,8},{16,12},{20,16},{24,20},{28,24},{1,29},{... | collective-permute-start | bytes 1572872 | tf_op jit(solution)/shard_map/ppermute | solution.py:180
  37.4 18.4 %collective-permute-start.3 = (bf16[1,2,512,256]{3,2,1,0:T(8,128)(2,1)S(1)}, bf16[1,2,512,256]{3,2,1,0:T(8,128)(2,1)S(1)}, u32[]{:S(2)}, u32[]{:S(2)}) collective-permute-start(bf16[1,2,512,256]{3,2,1,0:T(8,128)(2,1)S(1)} %pick.1), channel_id=1, source_target_pairs={{0,1},{1,0},{2,3},{3,2},{4,5},{5,4},{6,7},{7,6},{8,9},{9,8},{10,11... | collective-permute-start | bytes 1572872 | tf_op jit(solution)/shard_map/ppermute | solution.py:181
  46.3 11.2 %collective-permute-start.2 = (bf16[4,256,256]{2,1,0:T(8,128)(2,1)S(1)}, bf16[4,256,256]{2,1,0:T(8,128)(2,1)S(1)}, u32[]{:S(2)}, u32[]{:S(2)}) collective-permute-start(bf16[4,256,256]{2,1,0:T(8,128)(2,1)S(1)} %collective-permute-done.1.refs_3_), channel_id=1, source_target_pairs={{0,4},{4,8},{8,12},{12,16},{16,20},{20,24},{24,28},{28,0},{1,5},{5... | collective-permute-start | bytes 1572872 | tf_op jit(solution)/shard_map/ppermute | solution.py:182
  46.3 11.2 %collective-permute-start.6 = (bf16[4,256,256]{2,1,0:T(8,128)(2,1)S(1)}, bf16[4,256,256]{2,1,0:T(8,128)(2,1)S(1)}, u32[]{:S(2)}, u32[]{:S(2)}) collective-permute-start(bf16[4,256,256]{2,1,0:T(8,128)(2,1)S(1)} %collective-permute-done.5.refs_4_), channel_id=1, source_target_pairs={{0,28},{4,0},{8,4},{12,8},{16,12},{20,16},{24,20},{28,24},{1,29},{... | collective-permute-start | bytes 1572872 | tf_op jit(solution)/shard_map/ppermute | solution.py:182
  57.5 10.3 %collective-permute-start.7 = (bf16[4,256,256]{2,1,0:T(8,128)(2,1)S(1)}, bf16[4,256,256]{2,1,0:T(8,128)(2,1)S(1)}, u32[]{:S(2)}, u32[]{:S(2)}) collective-permute-start(bf16[4,256,256]{2,1,0:T(8,128)(2,1)S(1)} %collective-permute-done.2.refs_0_), channel_id=1, source_target_pairs={{0,4},{4,8},{8,12},{12,16},{16,20},{20,24},{24,28},{28,0},{1,5},{5... | collective-permute-start | bytes 1572872 | tf_op jit(solution)/shard_map/ppermute | solution.py:187
  59.4 16.1 %collective-permute-start.8 = (f32[4,2,512,256]{3,2,1,0:T(8,128)S(1)}, f32[4,2,512,256]{3,2,1,0:T(8,128)S(1)}, u32[]{:S(2)}, u32[]{:S(2)}) collective-permute-start(f32[4,2,512,256]{3,2,1,0:T(8,128)S(1)} %half_product.7), channel_id=1, source_target_pairs={{0,1},{1,0},{2,3},{3,2},{4,5},{5,4},{6,7},{7,6},{8,9},{9,8},{10,11... | collective-permute-start | bytes 12582920 | tf_op jit(solution)/shard_map/ppermute | solution.py:190
  67.8 7.7 %collective-permute-start.9 = (bf16[4,256,256]{2,1,0:T(8,128)(2,1)S(1)}, bf16[4,256,256]{2,1,0:T(8,128)(2,1)S(1)}, u32[]{:S(2)}, u32[]{:S(2)}) collective-permute-start(bf16[4,256,256]{2,1,0:T(8,128)(2,1)S(1)} %collective-permute-done.7.refs_2_), channel_id=1, source_target_pairs={{0,1},{1,0},{2,3},{3,2},{4,5},{5,4},{6,7},{7,6},{8,9},{9,8},{10,11... | collective-permute-start | bytes 1572872 | tf_op jit(solution)/shard_map/ppermute | solution.py:191
  78.7 31.8 %copy-start.2 = (bf16[512,256]{1,0:T(8,128)(2,1)S(1)}, bf16[512,256]{1,0:T(8,128)(2,1)}, u32[]{:S(2)}) copy-start(bf16[512,256]{1,0:T(8,128)(2,1)} %get-tuple-element.29) | copy-start | bytes 786436
  78.7 31.0 %all-to-all-start.1 = ((f16[8,528,256]{2,1,0:T(8,128)(2,1)}), f16[8,528,256]{2,1,0:T(8,128)(2,1)S(1)}, u32[]{:S(2)}, u32[]{:S(2)}) async-start(f16[8,528,256]{2,1,0:T(8,128)(2,1)} %convert_element_type.13), calls=%async_computation.1 | async-start | bytes 4325376 | tf_op jit(solution)/shard_map/all_to_all | solution.py:194
  82.8 65.0 %copy-start.3 = (f32[1,256,256]{2,1,0:T(8,128)S(1)}, f32[1,256,256]{2,1,0:T(8,128)}, u32[]{:S(2)}) copy-start(f32[1,256,256]{2,1,0:T(8,128)} %param.7) | copy-start | bytes 786436
  110.5 38.1 %copy-start.1 = (bf16[512,256]{1,0:T(8,128)(2,1)}, bf16[512,256]{1,0:T(8,128)(2,1)S(1)}, u32[]{:S(2)}) copy-start(bf16[512,256]{1,0:T(8,128)(2,1)S(1)} %negate_convert_fusion) | copy-start | bytes 786436
  110.8 2.2 %collective-permute-start.10 = (f32[128,256]{1,0:T(8,128)S(1)}, f32[128,256]{1,0:T(8,128)S(1)}, u32[]{:S(2)}, u32[]{:S(2)}) collective-permute-start(f32[128,256]{1,0:T(8,128)S(1)} %dynamic-slice_bitcast_fusion), channel_id=1, source_target_pairs={{0,1},{1,0},{2,3},{3,2},{4,5},{5,4},{6,7},{7,6},{8,9},{9,8},{10,11... | collective-permute-start | bytes 393224 | tf_op jit(solution)/shard_map/ppermute | solution.py:203
  142.1 5.7 %collective-permute-start.11 = (f32[128,256]{1,0:T(8,128)S(1)}, f32[128,256]{1,0:T(8,128)S(1)}, u32[]{:S(2)}, u32[]{:S(2)}) collective-permute-start(f32[128,256]{1,0:T(8,128)S(1)} %bitcast.36), channel_id=1, source_target_pairs={{0,1},{1,0},{2,3},{3,2},{4,5},{5,4},{6,7},{7,6},{8,9},{9,8},{10,11... | collective-permute-start | bytes 393224 | tf_op jit(solution)/shard_map/ppermute | solution.py:208
